TPU v7x, 256 devices: a whole 4x4x8 slice. The times are simulated.
256 devices in a mesh: group: 16 (over x, z_hi), member: 16 (over y, z_lo, core).
Axes of the slice: x: 4, y: 4, z: 8 (z_hi: 4, z_lo: 2; z = z_hi * 2 + z_lo), core: 2. Of those that a mesh axis runs over, the one named last changes fastest.
Arguments:
- prompt_k: bfloat16 [16, 1024, 1024], P('group', 'member'), may hold values from -6 to 6
- prompt_v: bfloat16 [16, 1024, 1024], P('group', 'member'), may hold values from -18 to 18
- resp_q: bfloat16 [16, 16, 128, 4096], P('group', 'member'), may hold values from -45 to 45
- resp_k: bfloat16 [16, 16, 128, 1024], P('group', 'member'), may hold values from -6 to 6
- resp_v: bfloat16 [16, 16, 128, 1024], P('group', 'member'), may hold values from -18 to 18
- out_grad: bfloat16 [16, 16, 128, 4096], P('group', 'member'), may hold values from -6 to 6
- lengths: int32 [16, 16], P('group', 'member'), may hold values from 16 to 128, as said below
- rewards: float32 [16, 16], P('group', 'member'), may hold values from -6 to 6
Outputs:
- attended: bfloat16 [16, 16, 128, 4096], P('group', 'member')
- grad_q: bfloat16 [16, 16, 128, 4096], P('group', 'member')
- grad_resp_k: bfloat16 [16, 16, 128, 1024], P('group', 'member')
- grad_resp_v: bfloat16 [16, 16, 128, 1024], P('group', 'member')
- grad_prompt_k: bfloat16 [16, 1024, 1024], P('group', 'member')
- grad_prompt_v: bfloat16 [16, 1024, 1024], P('group', 'member')
Inputs may be any that keep to these rules, and one draw needn't show every extreme that they name: In each group the lengths never fall from one member to the next, and the last member's response has exactly 128 live tokens.
All inputs are finite; a program needn't handle non-finite values.
Results may differ from a plain program's by a relative error of at most 0.0082.
Values may be sent and summed in bfloat16 or wider, within the bound.
No kernel may reach another device: no remote copies, remote signals or barrier semaphores. Data moves between devices by JAX's collectives and lax.ppermute only.
A program may use at most 128 MiB of HBM per device.

v0:
```python
import jax
import jax.numpy as jnp
from jax import lax
from jax.sharding import PartitionSpec as P

KVH = 8
HD = 128


def to_heads(rows_in, kv_heads, head_size):
    row_count = rows_in.shape[0]
    per_head = rows_in.shape[1] // (kv_heads * head_size)
    shaped = rows_in.reshape(row_count, kv_heads, per_head, head_size)
    return shaped.transpose(1, 2, 0, 3).reshape(kv_heads, per_head * row_count, head_size)


def from_heads(blocks, row_count):
    kv_heads, rows_all, head_size = blocks.shape
    per_head = rows_all // row_count
    shaped = blocks.reshape(kv_heads, per_head, row_count, head_size)
    return shaped.transpose(2, 0, 1, 3).reshape(row_count, kv_heads * per_head * head_size)


def head_terms(queries, cotangent, all_keys, all_values, allowed, score_scale):
    scores = jnp.dot(queries, all_keys.T, preferred_element_type=jnp.float32) * score_scale
    scores = jnp.where(allowed, scores, -jnp.inf)
    row_max = jnp.max(scores, axis=1, keepdims=True)
    raised = jnp.exp(scores - row_max)
    row_sum = jnp.sum(raised, axis=1, keepdims=True)
    probability = raised / row_sum
    probs_low = probability.astype(jnp.bfloat16)
    output = jnp.dot(probs_low, all_values, preferred_element_type=jnp.float32)
    dprobs = jnp.dot(cotangent, all_values.T, preferred_element_type=jnp.float32)
    row_delta = jnp.sum(cotangent.astype(jnp.float32) * output, axis=1, keepdims=True)
    dscores = (probability * (dprobs - row_delta)).astype(jnp.bfloat16)
    grad_query = jnp.dot(dscores, all_keys, preferred_element_type=jnp.float32) * score_scale
    grad_keys = jnp.dot(dscores.T, queries, preferred_element_type=jnp.float32) * score_scale
    grad_values = jnp.dot(probs_low.T, cotangent, preferred_element_type=jnp.float32)
    return (output, grad_query, grad_keys, grad_values, row_max, row_sum, row_delta)


def body(prompt_k, prompt_v, resp_q, resp_k, resp_v, out_grad, lengths, rewards):
    members = lax.axis_size("member")
    groups = lax.axis_size("group")
    slots = resp_q.shape[2]
    score_scale = float(HD) ** (-0.5)
    length = lengths[0, 0]
    reward = rewards[0, 0]
    own_tokens = length.astype(jnp.float32)
    reward_total = lax.psum(reward, "member")
    token_total = lax.psum(own_tokens, ("group", "member"))
    advantage = reward - reward_total / members
    factor = jnp.float32(slots * groups * members) / token_total
    position = jnp.arange(slots)
    live_rows = position < length
    weight = jnp.where(live_rows, advantage * factor, 0.0)
    cotangent = (out_grad[0, 0].astype(jnp.float32) * weight[:, None]).astype(jnp.bfloat16)
    whole_k, whole_v = (
        lax.all_gather(prompt_k, "member", axis=1, tiled=True),
        lax.all_gather(prompt_v, "member", axis=1, tiled=True),
    )
    prompt_len = whole_k.shape[1]
    all_keys = jnp.concatenate([whole_k[0], resp_k[0, 0]], axis=0)
    all_values = jnp.concatenate([whole_v[0], resp_v[0, 0]], axis=0)
    per_head = resp_q.shape[3] // (KVH * HD)
    row_pos = jnp.tile(position, per_head)
    key_pos = jnp.arange(prompt_len + slots)
    allowed = (key_pos[None, :] < prompt_len) | (key_pos[None, :] - prompt_len <= row_pos[:, None])
    query_heads = to_heads(resp_q[0, 0], KVH, HD)
    cotan_heads = to_heads(cotangent, KVH, HD)
    key_heads = to_heads(all_keys, KVH, HD)
    value_heads = to_heads(all_values, KVH, HD)

    def per_kv_head(head_ops):
        return head_terms(head_ops[0], head_ops[1], head_ops[2], head_ops[3], allowed, score_scale)

    output, grad_query, grad_keys, grad_values, row_max, row_sum, row_delta = lax.map(
        per_kv_head, (query_heads, cotan_heads, key_heads, value_heads)
    )
    attended = (from_heads(output, slots) * live_rows[:, None]).astype(jnp.bfloat16)
    grad_q = from_heads(grad_query, slots).astype(jnp.bfloat16)
    key_rows = from_heads(grad_keys, grad_keys.shape[1])
    value_rows = from_heads(grad_values, grad_values.shape[1])
    grad_resp_k = key_rows[key_rows.shape[0] - slots :].astype(jnp.bfloat16)
    grad_resp_v = value_rows[value_rows.shape[0] - slots :].astype(jnp.bfloat16)
    partial_term = jnp.concatenate([key_rows[:prompt_len], value_rows[:prompt_len]], axis=1)
    summed = lax.psum_scatter(partial_term, "member", scatter_dimension=0, tiled=True)
    row_width = prompt_k.shape[2]
    grad_prompt_k = summed[:, :row_width].astype(jnp.bfloat16)[None]
    grad_prompt_v = summed[:, row_width:].astype(jnp.bfloat16)[None]
    return (
        attended[None, None],
        grad_q[None, None],
        grad_resp_k[None, None],
        grad_resp_v[None, None],
        grad_prompt_k,
        grad_prompt_v,
    )


def solution(mesh):
    placed = (
        P("group", "member", None),
        P("group", "member", None),
        P("group", "member", None, None),
        P("group", "member", None, None),
        P("group", "member", None, None),
        P("group", "member", None, None),
        P("group", "member"),
        P("group", "member"),
    )
    return jax.shard_map(
        body,
        mesh=mesh,
        in_specs=placed,
        out_specs=(
            P("group", "member", None, None),
            P("group", "member", None, None),
            P("group", "member", None, None),
            P("group", "member", None, None),
            P("group", "member", None),
            P("group", "member", None),
        ),
        check_vma=False,
    )
```

profile of v0, /device:TPU:1, one launch (start us, length us, event | category | flops | bytes accessed | tf_op | source)
XLA Modules:
  0.0 357.4 jit_solution(7498258607502978287)
XLA Ops:
  9.3 81.4 %psum.15 = f32[]{:T(128)} all-reduce(f32[]{:T(128)S(6)} %convert_element_type.86), channel_id=1, replica_groups=mesh['group'=16,'member'=16] {'group','member'}, use_global_device_ids=true, to_apply=%region_1.0 | all-reduce | flops 1 | bytes 8 | tf_op jit(solution)/shard_map/psum | solution.py:51
  90.7 28.1 %psum.14 = f32[]{:T(128)} all-reduce(f32[]{:T(128)} %bitcast.12), channel_id=1, replica_groups=mesh['group'=16,'member'=16] {'member'}, use_global_device_ids=true, to_apply=%region_0.0 | all-reduce | flops 1 | bytes 8 | tf_op jit(solution)/shard_map/psum | solution.py:50
  120.6 1.9 copy.71
  122.5 1.8 reshape_squeeze.3
  129.5 2.9 copy.68
  132.4 4.0 %copy.70 = bf16[1,1024,1024]{1,2,0:T(8,128)(2,1)} copy(bf16[1,1024,1024]{2,1,0:T(8,128)(2,1)} %all-gather.5.cloned.1.call-done) | data formatting | bytes 4194304 | tf_op jit(solution)/shard_map/all_gather | solution.py:60
  136.4 3.7 %maximum_bitcast_fusion = (bf16[8,1152,128]{1,2,0:T(8,128)(2,1)}, bf16[8,1152,128]{1,2,0:T(8,128)(2,1)}) fusion(bf16[128,8,1,128]{0,3,1,2:T(8,128)(2,1)S(1)} %bitcast.163, bf16[1024,8,1,128]{0,3,1,2:T(8,128)(2,1)S(1)} %bitcast.151, bf16[128,8,1,128]{0,3,1,2:T(8,128)(2,1)} %bitcast.164, bf16[1024,8,1,128]{0,3,1,2:T(8,128)(2,1)} %bitcast.152), kind=kLoop, calls=%fused_computation.45 | loop fusion | flops 9437184 | bytes 9437184 | tf_op jit(solution)/shard_map/reshape | solution.py:14
  140.1 101.3 %while.17 = (s32[]{:T(128)}, f32[8,512,128]{1,2,0:T(8,128)}, bf16[8,512,128]{2,1,0:T(8,128)(2,1)}, f32[8,1152,128]{2,1,0:T(8,128)}, f32[8,1152,128]{2,1,0:T(8,12...) while((s32[]{:T(128)}, f32[8,512,128]{1,2,0:T(8,128)}, ...), condition=%wide.region_6.7_spmd.clone, body=%wide.region_2.6_spmd.clone.sunk | while | flops 916994560 | bytes 19959560 | solution.py:77
  140.2 1.8 fusion.62
  142.6 2.4 bitcast_dynamic-update-slice_fusion.2
  145.0 1.7 fusion.64
  146.7 2.1 fusion.65
  148.8 1.7 fusion.67
  150.5 2.3 fusion.66
  152.9 1.8 fusion.62
  155.3 2.4 bitcast_dynamic-update-slice_fusion.2
  157.8 1.7 fusion.64
  159.4 2.1 fusion.65
  161.5 1.7 fusion.67
  163.2 2.3 fusion.66
  165.6 1.8 fusion.62
  168.0 2.4 bitcast_dynamic-update-slice_fusion.2
  170.4 1.7 fusion.64
  172.1 2.1 fusion.65
  174.2 1.6 fusion.67
  175.9 2.2 fusion.66
  178.2 1.8 fusion.62
  180.6 2.4 bitcast_dynamic-update-slice_fusion.2
  183.0 1.7 fusion.64
  184.7 2.1 fusion.65
  186.8 1.6 fusion.67
  188.5 2.3 fusion.66
  190.9 1.8 fusion.62
  193.2 2.4 bitcast_dynamic-update-slice_fusion.2
  195.7 1.7 fusion.64
  197.4 2.1 fusion.65
  199.5 1.7 fusion.67
  201.1 2.2 fusion.66
  203.5 1.8 fusion.62
  205.9 2.4 bitcast_dynamic-update-slice_fusion.2
  208.3 1.7 fusion.64
  210.0 2.1 fusion.65
  212.1 1.7 fusion.67
  213.8 2.2 fusion.66
  216.2 1.8 fusion.62
  218.5 2.4 bitcast_dynamic-update-slice_fusion.2
  221.0 1.7 fusion.64
  222.7 2.1 fusion.65
  224.8 1.6 fusion.67
  226.4 2.3 fusion.66
  228.8 1.8 fusion.62
  231.2 2.4 bitcast_dynamic-update-slice_fusion.2
  233.7 1.7 fusion.64
  235.3 2.1 fusion.65
  237.4 1.7 fusion.67
  239.1 2.3 fusion.66
  241.4 2.5 slice.41
  243.9 2.4 copy.84
  247.6 2.4 copy.83
  251.1 3.8 %pad_maximum_fusion = f32[1024,2048]{1,0:T(8,128)} fusion(f32[1024,1024]{1,0:T(8,128)S(1)} %bitcast.148, f32[1024,1024]{1,0:T(8,128)S(1)} %bitcast.149), kind=kLoop, calls=%fused_computation.42 | loop fusion | flops 2097152 | bytes 16777216 | tf_op jit(solution)/shard_map/concatenate | solution.py:86
  261.6 2.0 reshape.156
  263.6 2.8 copy.79
  266.4 2.1 reshape.157
  269.7 79.4 %reduce-scatter.2.cloned.1.call-done = f32[64,2048]{1,0:T(8,128)} async-done(((f32[1024,2048]{1,0:T(8,128)}), f32[64,2048]{1,0:T(8,128)}) %reduce-scatter.2.cloned.1.call-update) | async-done | bytes 524304 | tf_op jit(solution)/shard_map/reduce_scatter | solution.py:87
  (78 shorter events, 24.1 us)
Async XLA Ops:
  7.2 122.4 %all-gather.3.cloned.1.call-start = ((), (), s32[]{:S(2)}) async-start(), calls=%async_computation.1 | async-start | bytes 2228224 | tf_op jit(solution)/shard_map/all_gather | solution.py:59
  7.9 124.5 %all-gather.5.cloned.1.call-start = ((), (), s32[]{:S(2)}) async-start(), calls=%async_computation.2 | async-start | bytes 2228224 | tf_op jit(solution)/shard_map/all_gather | solution.py:60
  8.6 340.4 %reduce-scatter.2.cloned.1.call-start = ((), (), s32[]{:S(2)}) async-start(), calls=%async_computation.3 | async-start | bytes 8912896 | tf_op jit(solution)/shard_map/reduce_scatter | solution.py:87
  120.6 5.1 %copy-start = (bf16[1,1,128,4096]{3,2,1,0:T(8,128)(2,1)S(1)}, bf16[1,1,128,4096]{3,2,1,0:T(8,128)(2,1)}, u32[]{:S(2)}) copy-start(bf16[1,1,128,4096]{3,2,1,0:T(8,128)(2,1)} %param.15) | copy-start | bytes 3145732
  243.9 3.5 slice-start
  246.3 1.0 slice-start.1
  254.9 4.3 %copy-start.1 = (bf16[8,512,128]{2,1,0:T(8,128)(2,1)S(1)}, bf16[8,512,128]{2,1,0:T(8,128)(2,1)}, u32[]{:S(2)}) copy-start(bf16[8,512,128]{2,1,0:T(8,128)(2,1)} %get-tuple-element.62) | copy-start | bytes 3145732
Sparse Core Ops, SparseCore 0:
  9.9 40.8 all-gather.2
  52.6 36.4 all-gather.4
  255.0 93.9 reduce-scatter.1
where the time goes:
time: 360 us; the launch traced here: 357 us
  blocking collectives  109 us (30%)
  matrix products  95.4 us (26%)
  waiting for transfers between devices  80.8 us (22%)
  local copies, waits for them, and re-layouts  40 us (11%)
  between operations  16.7 us (5%)
  other arithmetic  14.7 us (4%)
    psum x1, blocking collectives, body(): token_total = lax.psum(own_tokens, ('group', 'member'))  81.4 us
    reduce_scatter x1, waiting for transfers between devices, body(): lax.psum_scatter(partial_term, 'member', scatter_dimension=0, tiled=True)  79.4 us
    psum x1, blocking collectives, body(): reward_total = lax.psum(reward, 'member')  28.1 us
    dot_general x8, matrix products, head_terms(): output = jnp.dot(probs_low, all_values, preferred_element_type=jnp.float32)  19.2 us
    dot_general x8, matrix products, head_terms(): jnp.dot(dscores.T, queries, preferred_element_type=jnp.float32)  18.1 us
    dot_general x8, matrix products, head_terms(): jnp.dot(dscores, all_keys, preferred_element_type=jnp.float32) * score_scale  16.8 us
    dot_general x8, matrix products, head_terms(): jnp.dot(queries, all_keys.T, preferred_element_type=jnp.float32)  14.6 us
    dot_general x8, matrix products, head_terms(): jnp.dot(cotangent, all_values.T, preferred_element_type=jnp.float32)  13.5 us
  transfers between devices with their start and end apart: 3, of which 1 were waited for; matrix products, arithmetic and copies ran while one was open for 7% of the time, Pallas kernels for 0%

commit v1 on v0

v1 whole, which is shorter than its diff:
```python
import functools

import jax
import jax.numpy as jnp
from jax import lax
from jax.experimental import pallas as pl
from jax.experimental.pallas import tpu as pltpu
from jax.sharding import Mesh
from jax.sharding import PartitionSpec as P

BF16 = jnp.bfloat16
F32 = jnp.float32
KVH = 8
HD = 128
LOG2E = 1.4426950408889634
NT = (((1,), (1,)), ((), ()))
NN = (((1,), (0,)), ((), ()))


def dot(a, b, dims=NN):
    return lax.dot_general(a, b, dims, preferred_element_type=F32)


def step(values, axis, by):
    size = lax.axis_size(axis)
    return lax.ppermute(values, axis, [(i, (i + by) % size) for i in range(size)])


def heads_to_rows(wide):
    return jnp.concatenate([wide[:, i * HD : (i + 1) * HD] for i in range(wide.shape[1] // HD)], axis=0)


def response_terms(queries, upstream, length, advantage, keys, values, keys_t, values_t, scale):
    slots = queries.shape[0]
    prompt_len = keys.shape[0] - slots
    token = lax.broadcasted_iota(jnp.int32, (slots, HD), 0).astype(F32)
    live = token < length
    weight = jnp.where(live, jnp.broadcast_to(advantage, live.shape), 0.0)
    per_head = queries.shape[1] // HD
    q_rows = heads_to_rows(queries)
    cot = [(upstream[:, i * HD : (i + 1) * HD].astype(F32) * weight).astype(BF16) for i in range(per_head)]
    cot_rows = jnp.concatenate(cot, axis=0)
    rows = q_rows.shape[0]
    scores = dot(keys, q_rows, NT)
    key_pos = lax.broadcasted_iota(jnp.int32, (slots, rows), 0)
    row_pos = lax.broadcasted_iota(jnp.int32, (slots, rows), 1) % slots
    tail = jnp.where(key_pos <= row_pos, scores[prompt_len:], -jnp.inf)
    scores = jnp.concatenate([scores[:prompt_len], tail], axis=0)
    row_max = jnp.max(scores, axis=0, keepdims=True)
    raised = jnp.exp2((scores - row_max) * (scale * LOG2E))
    row_sum = jnp.sum(raised, axis=0, keepdims=True)
    probs = raised * (1.0 / row_sum)
    probs_low = probs.astype(BF16)
    output_t = dot(values_t, probs_low)
    dprobs = dot(values, cot_rows, NT)
    cot_t = cot_rows.astype(F32).T
    delta = jnp.sum(cot_t * output_t, axis=0, keepdims=True)
    dscores = (probs * (dprobs - delta)).astype(BF16)
    grad_q_t = dot(keys_t, dscores) * scale
    grad_keys = dot(dscores, q_rows) * scale
    grad_values = dot(probs_low, cot_rows)
    attended = [jnp.where(live, output_t[:, i * slots : (i + 1) * slots].T, 0.0).astype(BF16) for i in range(per_head)]
    grad_q = [grad_q_t[:, i * slots : (i + 1) * slots].T.astype(BF16) for i in range(per_head)]
    return attended, grad_q, grad_keys, grad_values


def attention_kernel(scale, side_ref, *refs):
    blocks, far, far_z = refs[:6], refs[6:8], refs[8:10]
    q_own, g_own, k_own, v_own, q_sib, g_sib, k_sib, v_sib = refs[10:18]
    att_out, gq_out, gk_out, gv_out, sib_out = refs[18:23]
    parts = refs[23:31]
    keys_scr, values_scr = refs[31:33]
    slots = q_own.shape[2]
    rows = far[0].shape[0]
    per_head = q_own.shape[3] // HD
    held = [(b[0:rows], b[rows : 2 * rows], b[2 * rows :]) for b in blocks]
    held[4:4] = [(far[0][...], far[1][0:rows], far[1][rows:])]
    held.append((far_z[0][...], far_z[1][0:rows], far_z[1][rows:]))
    for i, (k, v, _) in enumerate(held):
        keys_scr[i * rows : (i + 1) * rows] = k
        values_scr[i * rows : (i + 1) * rows] = v
    prompt_len = len(held) * rows
    facts = [scal.astype(F32) for _, _, scal in held]
    total = sum(facts[1:], facts[0])
    members = 2.0 * len(held)
    reward = lambda f, at: f[at + 1 : at + 2] + f[at + 2 : at + 3] + f[at + 3 : at + 4]
    reward_mean = (reward(total, 0) + reward(total, 8)) * (1.0 / members)

    grads = []
    for at, q, g, rk, rv in ((0, q_own[0, 0], g_own[0, 0], k_own[0, 0], v_own[0, 0]), (8, q_sib[...], g_sib[...], k_sib[...], v_sib[...])):
        keys_scr[prompt_len:] = rk
        values_scr[prompt_len:] = rv
        keys, values = keys_scr[...], values_scr[...]
        length = facts[0][at : at + 1]
        advantage = reward(facts[0], at) - reward_mean
        attended, grad_q, grad_keys, grad_values = response_terms(
            q, g, length, advantage, keys, values, keys.T, values.T, scale
        )
        gk, gv = grad_keys[prompt_len:].astype(BF16), grad_values[prompt_len:].astype(BF16)
        for i in range(per_head):
            cols = slice(i * HD, (i + 1) * HD)
            if at == 0:
                att_out[0, 0, :, cols] = attended[i]
                gq_out[0, 0, :, cols] = grad_q[i]
            else:
                sib_out[:, cols] = attended[i]
                sib_out[:, (per_head + i) * HD : (per_head + i + 1) * HD] = grad_q[i]
        if at == 0:
            gk_out[0, 0] = gk
            gv_out[0, 0] = gv
        else:
            sib_out[:, 2 * per_head * HD : (2 * per_head + 1) * HD] = gk
            sib_out[:, (2 * per_head + 1) * HD :] = gv
        grads.append((grad_keys, grad_values))
    grad_keys = grads[0][0][:prompt_len] + grads[1][0][:prompt_len]
    grad_values = grads[0][1][:prompt_len] + grads[1][1][:prompt_len]
    for i, part in enumerate(parts):
        part[0:rows] = grad_keys[i * rows : (i + 1) * rows].astype(part.dtype)
        part[rows:] = grad_values[i * rows : (i + 1) * rows].astype(part.dtype)


def attention(side, blocks, far, far_z, resp_q, out_grad, resp_k, resp_v, packed, kv_heads):
    _, _, slots, width = resp_q.shape
    rows = far[0].shape[0]
    per_head = width // (KVH * HD)
    wide = per_head * HD
    whole = lambda a: pl.BlockSpec((a.shape[0], HD), lambda h, s: (0, h))
    own = lambda w: pl.BlockSpec((1, 1, slots, w), lambda h, s: (0, 0, 0, s[0] * kv_heads + h))
    at = lambda w, first: pl.BlockSpec((slots, w), lambda h, s: (0, first + h))
    in_specs = [whole(a) for a in (*blocks, *far, *far_z)]
    in_specs += [own(wide), own(wide), own(HD), own(HD)]
    in_specs += [at(wide, 0), at(wide, kv_heads), at(HD, 2 * kv_heads * per_head), at(HD, 2 * kv_heads * per_head + kv_heads)]
    sib_wide = 2 * wide + 2 * HD
    out_specs = [own(wide), own(wide), own(HD), own(HD), at(sib_wide, 0)]
    out_shape = [jax.ShapeDtypeStruct(a.shape, BF16) for a in (resp_q, out_grad, resp_k, resp_v)]
    out_shape.append(jax.ShapeDtypeStruct((slots, kv_heads * sib_wide), BF16))
    for i in range(8):
        out_specs.append(pl.BlockSpec((2 * rows, HD), lambda h, s: (0, h)))
        out_shape.append(jax.ShapeDtypeStruct((2 * rows, kv_heads * HD), F32 if i == 0 else BF16))
    keys = 8 * rows + slots
    return pl.pallas_call(
        functools.partial(attention_kernel, float(HD) ** -0.5),
        grid_spec=pltpu.PrefetchScalarGridSpec(
            num_scalar_prefetch=1,
            grid=(kv_heads,),
            in_specs=in_specs,
            out_specs=out_specs,
            scratch_shapes=[pltpu.VMEM((keys, HD), BF16), pltpu.VMEM((keys, HD), BF16)],
        ),
        out_shape=out_shape,
        compiler_params=pltpu.CompilerParams(vmem_limit_bytes=56 * 2**20),
        cost_estimate=pl.CostEstimate(flops=7_000_000_000, bytes_accessed=16_000_000, transcendentals=5_000_000),
    )(side, *blocks, *far, *far_z, resp_q, out_grad, resp_k, resp_v, packed, packed, packed, packed)


def body(prompt_k, prompt_v, resp_q, resp_k, resp_v, out_grad, lengths, rewards):
    side = lax.axis_index("core")
    other = 1 - side
    slots, width = resp_q.shape[2:]
    kv_heads = KVH // 2
    half = prompt_k.shape[2] // 2
    rows = prompt_k.shape[1]
    devices = 1
    for axis in ("x", "zh", "y", "zl", "core"):
        devices *= lax.axis_size(axis)

    reward = rewards[0, 0]
    high = lax.reduce_precision(reward, 8, 7)
    middle = lax.reduce_precision(reward - high, 8, 7)
    low = reward - high - middle
    facts = jnp.stack([lengths[0, 0].astype(F32), high, middle, low, 0.0, 0.0, 0.0, 0.0])
    facts = jnp.broadcast_to(facts[:, None], (8, half)).astype(BF16)

    def half_of(a, which):
        return lax.dynamic_slice_in_dim(a, which * (a.shape[1] // 2), a.shape[1] // 2, 1)

    my_k, my_v = half_of(prompt_k[0], side), half_of(prompt_v[0], side)
    give = jnp.concatenate([half_of(prompt_k[0], other), half_of(prompt_v[0], other), facts, facts], axis=0)
    got = step(give, "core", 1)
    mine = jnp.concatenate([my_k, got[:rows], my_v, got[rows : 2 * rows], facts, got[2 * rows : 2 * rows + 8]], axis=0)
    packed = jnp.concatenate([half_of(a[0, 0], other) for a in (resp_q, out_grad, resp_k, resp_v)], axis=1)
    packed = step(packed, "core", 1)

    pair = 2 * rows
    near_z = step(mine, "zl", 1)
    below = step(mine, "y", 1)
    above = step(mine, "y", -1)
    below_z = step(near_z, "y", 1)
    above_z = step(near_z, "y", -1)
    far = (step(below[:pair], "y", 1), step(above[pair:], "y", -1))
    far_z = (step(far[0], "zl", 1), step(far[1], "zl", 1))

    tokens = sum(b[2 * pair : 2 * pair + 1, :HD].astype(F32) + b[2 * pair + 8 : 2 * pair + 9, :HD].astype(F32)
                 for b in (mine, near_z, below, above, below_z, above_z))
    tokens += sum(b[pair : pair + 1, :HD].astype(F32) + b[pair + 8 : pair + 9, :HD].astype(F32) for b in (far[1], far_z[1]))

    outs = attention(
        side.reshape(1).astype(jnp.int32),
        (mine, near_z, above, below, above_z, below_z),
        far, far_z, resp_q, out_grad, resp_k, resp_v, packed, kv_heads,
    )
    attended, grad_q, grad_rk, grad_rv, for_sib = outs[:5]
    p_own, p_near, p_above, p_below, p_far, p_above_z, p_below_z, p_far_z = outs[5:]

    for axis in ("x", "zh"):
        tokens = tokens + sum(step(tokens, axis, by) for by in range(1, lax.axis_size(axis)))
    factor = jnp.float32(slots * devices) / tokens[0, 0]

    def added(*terms):
        return sum(t.astype(F32) for t in terms).astype(BF16)

    from_z = step(p_far_z, "zl", 1)
    from_below = step(p_above_z, "y", 1)
    from_above = step(p_below_z, "y", -1)
    from_sib = step(for_sib, "core", 1)
    far_sum = added(p_far, from_z)
    near_sum = added(p_near, from_below, from_above)
    far_k = step(far_sum[:pair], "y", 1)
    far_v = step(far_sum[pair:], "y", -1)
    above_sum = jnp.concatenate([added(p_above[:pair], far_k), p_above[pair:]], axis=0)
    below_sum = jnp.concatenate([p_below[:pair], added(p_below[pair:], far_v)], axis=0)
    last = (step(near_sum, "zl", 1), step(above_sum, "y", 1), step(below_sum, "y", -1))
    total = p_own + sum(t.astype(F32) for t in last)
    total = total * factor
    keep = jnp.concatenate([total[:rows], total[pair : pair + rows]], axis=1).astype(BF16)
    pass_on = jnp.concatenate([total[rows:pair], total[pair + rows :]], axis=1).astype(BF16)
    passed = step(pass_on, "core", 1)

    def merge(own, got):
        return jnp.where(side == 0, jnp.concatenate([own, got], axis=1), jnp.concatenate([got, own], axis=1))

    sib_heads = from_sib.reshape(slots, kv_heads, -1)
    wide = width // KVH
    def fill(buffer, got, scaled):
        got = got.reshape(slots, -1)
        whole = lax.dynamic_update_slice(buffer[0, 0], got, (0, other * got.shape[1]))
        if scaled:
            whole = (whole.astype(F32) * factor).astype(BF16)
        return whole[None, None]

    attended = fill(attended, sib_heads[:, :, :wide], False)
    grad_q = fill(grad_q, sib_heads[:, :, wide : 2 * wide], True)
    grad_rk = fill(grad_rk, sib_heads[:, :, 2 * wide : 2 * wide + HD], True)
    grad_rv = fill(grad_rv, sib_heads[:, :, 2 * wide + HD :], True)
    grad_pk = merge(keep[:, :half], passed[:, :half])[None]
    grad_pv = merge(keep[:, half:], passed[:, half:])[None]
    return attended, grad_q, grad_rk, grad_rv, grad_pk, grad_pv


def solution(mesh):
    parts = Mesh(mesh.devices.reshape(4, 4, 4, 2, 2), ("x", "zh", "y", "zl", "core"))
    group, member = ("x", "zh"), ("y", "zl", "core")
    rank3, rank4, rank2 = P(group, member, None), P(group, member, None, None), P(group, member)
    return jax.shard_map(
        body,
        mesh=parts,
        in_specs=(rank3, rank3, rank4, rank4, rank4, rank4, rank2, rank2),
        out_specs=(rank4, rank4, rank4, rank4, rank3, rank3),
        check_vma=False,
    )
```

time: 360 us -> 121 us (0.34)
  blocking collectives: 109 us -> 0 us
  matrix products: 95.4 us -> 0 us
  waiting for transfers between devices: 80.8 us -> 32.7 us
  starting transfers between devices: 0.11 us -> 42.7 us
  local copies, waits for them, and re-layouts: 40 us -> 11.2 us
  Pallas kernels: 0 us -> 22.4 us
  between operations: 16.7 us -> 6.34 us
  other arithmetic: 14.7 us -> 5.73 us
    psum x2 -> x0, blocking collectives: 109 us -> none  [the longest x1 81.4 us: body(): token_total = lax.psum(own_tokens, ('group', 'member'))]
    dot_general x48 -> x0, matrix products: 95.4 us -> none  [the longest x8 19.2 us: head_terms(): output = jnp.dot(probs_low, all_values, preferred_element_type=jnp.float32)]
    reduce_scatter x1 -> x0, waiting for transfers between devices: 79.4 us -> none  [body(): lax.psum_scatter(partial_term, 'member', scatter_dimension=0, tiled=True)]
    ppermute x0 -> x27, starting transfers between devices: none -> 42.7 us  [step(): lax.ppermute(values, axis, [(i, (i + by) % size) for i in range(size)])]
    ppermute x0 -> x27, waiting for transfers between devices: none -> 32.7 us  [step(): lax.ppermute(values, axis, [(i, (i + by) % size) for i in range(size)])]
    pallas_call x0 -> x1, Pallas kernels: none -> 22.4 us  [attention(): pl.pallas_call(functools.partial(attention_kernel, float(HD) ** (-0.5)),...]
    slice x8 -> x7, local copies, waits for them, and re-layouts: 10.2 us -> 2.39 us  [the longest x1 0.98 us: body(): p_below[:pair]]
    all_gather x2 -> x0, local copies, waits for them, and re-layouts: 6.81 us -> none  [the longest x1 3.95 us: body(): lax.all_gather(prompt_v, 'member', axis=1, tiled=True)]
  transfers between devices with their start and end apart: 3 -> 27, of which waited for: 1 -> 8; matrix products, arithmetic and copies ran while one was open for 7% -> 6% of each run, Pallas kernels for 0% -> 0%
where the time goes in v1:
time: 121 us
  starting transfers between devices  42.7 us (35%)
  waiting for transfers between devices  32.7 us (27%)
  Pallas kernels  22.4 us (19%)
  local copies, waits for them, and re-layouts  11.2 us (9%)
  between operations  6.34 us (5%)
  other arithmetic  5.73 us (5%)
    ppermute x27, starting transfers between devices, step(): lax.ppermute(values, axis, [(i, (i + by) % size) for i in range(size)])  42.7 us
    ppermute x27, waiting for transfers between devices, step(): lax.ppermute(values, axis, [(i, (i + by) % size) for i in range(size)])  32.7 us
    pallas_call x1, Pallas kernels, attention(): pl.pallas_call(functools.partial(attention_kernel, float(HD) ** (-0.5)),...  22.4 us
    dynamic_slice x6, local copies, waits for them, and re-layouts, half_of(): lax.dynamic_slice_in_dim(a, which * (a.shape[1] // 2), a.shape[1] // 2, 1)  3.63 us
    unnamed x52, local copies, waits for them, and re-layouts  3.44 us
    broadcast_in_dim x3, other arithmetic, fill(): return whole[None, None]  2.69 us
  transfers between devices with their start and end apart: 27, of which 8 were waited for; matrix products, arithmetic and copies ran while one was open for 6% of the time, Pallas kernels for 0%

profile of v1, /device:TPU:1, one launch (start us, length us, event | category | flops | bytes accessed | tf_op | source)
XLA Modules:
  0.0 121.0 jit_solution(1000334548645866988)
XLA Ops:
  0.6 0.0 copy-start.7
  5.7 0.9 dynamic-slice_bitcast_fusion.5
  6.6 0.8 dynamic-slice_bitcast_fusion.4
  7.4 0.1 stack.24
  7.5 0.1 broadcast_in_dim.22
  7.6 3.3 %collective-permute-start = (bf16[144,512]{1,0:T(8,128)(2,1)S(1)}, bf16[144,512]{1,0:T(8,128)(2,1)S(1)}, u32[]{:S(2)}, u32[]{:S(2)}) collective-permute-start(bf16[144,512]{1,0:T(8,128)(2,1)S(1)} %pad_maximum_fusion.3), channel_id=1, source_target_pairs={{0,1},{1,0},{2,3},{3,2},{4,5},{5,4},{6,7},{7,6},{8,9},{9,8},{10,11... | collective-permute-start | bytes 442376 | tf_op jit(solution)/shard_map/ppermute | solution.py:26
  11.0 0.9 dynamic-slice_bitcast_fusion.3
  11.9 0.9 dynamic-slice_bitcast_fusion.2
  13.0 0.1 pad_maximum_fusion
  13.1 0.1 collective-permute-start.10
  13.2 0.7 copy-done.9
  13.9 0.0 copy-done.10
  13.9 0.1 constant_dynamic-update-slice_fusion.1
  14.0 1.0 collective-permute-start.2
  15.0 1.6 %collective-permute-start.1 = (bf16[272,512]{1,0:T(8,128)(2,1)S(1)}, bf16[272,512]{1,0:T(8,128)(2,1)S(1)}, u32[]{:S(2)}, u32[]{:S(2)}) collective-permute-start(bf16[272,512]{1,0:T(8,128)(2,1)S(1)} %constant_dynamic-update-slice_fusion.refs_0_), channel_id=1, source_target_pairs={{0,2},{2,0},{1,3},{3,1},{4,6},{6,4},{5,7},{7,5},{8,10},{10,8},{9,1... | collective-permute-start | bytes 835592 | tf_op jit(solution)/shard_map/ppermute | solution.py:26
  16.7 5.6 %collective-permute-done.2.refs_2_ = bf16[272,512]{1,0:T(8,128)(2,1)S(1)} collective-permute-done((bf16[272,512]{1,0:T(8,128)(2,1)S(1)}, bf16[272,512]{1,0:T(8,128)(2,1)S(1)}, u32[]{:S(2)}, u32[]{:S(2)}) %collective-permute-start.2) | collective-permute-done | bytes 278560 | tf_op jit(solution)/shard_map/ppermute | solution.py:26
  22.3 2.3 %collective-permute-start.7 = (bf16[144,512]{1,0:T(8,128)(2,1)S(1)}, bf16[144,512]{1,0:T(8,128)(2,1)S(1)}, u32[]{:S(2)}, u32[]{:S(2)}) collective-permute-start(bf16[144,512]{1,0:T(8,128)(2,1)S(1)} %slice.161), channel_id=1, source_target_pairs={{0,12},{4,0},{8,4},{12,8},{1,13},{5,1},{9,5},{13,9},{2,14},{6,2},{... | collective-permute-start | bytes 442376 | tf_op jit(solution)/shard_map/ppermute | solution.py:26
  24.6 2.7 %collective-permute-start.4 = (bf16[272,512]{1,0:T(8,128)(2,1)S(1)}, bf16[272,512]{1,0:T(8,128)(2,1)S(1)}, u32[]{:S(2)}, u32[]{:S(2)}) collective-permute-start(bf16[272,512]{1,0:T(8,128)(2,1)S(1)} %collective-permute-done.1.refs_1_), channel_id=1, source_target_pairs={{0,12},{4,0},{8,4},{12,8},{1,13},{5,1},{9,5},{13,9},{2,14},{6,2},{... | collective-permute-start | bytes 835592 | tf_op jit(solution)/shard_map/ppermute | solution.py:26
  27.3 0.1 collective-permute-start.6
  27.4 1.7 %collective-permute-start.9 = (bf16[144,512]{1,0:T(8,128)(2,1)S(1)}, bf16[144,512]{1,0:T(8,128)(2,1)S(1)}, u32[]{:S(2)}, u32[]{:S(2)}) collective-permute-start(bf16[144,512]{1,0:T(8,128)(2,1)S(1)} %collective-permute-done.7.refs_7_), channel_id=1, source_target_pairs={{0,2},{2,0},{1,3},{3,1},{4,6},{6,4},{5,7},{7,5},{8,10},{10,8},{9,1... | collective-permute-start | bytes 442376 | tf_op jit(solution)/shard_map/ppermute | solution.py:26
  29.1 6.6 %collective-permute-done.6.refs_6_ = bf16[128,512]{1,0:T(8,128)(2,1)S(1)} collective-permute-done((bf16[128,512]{1,0:T(8,128)(2,1)S(1)}, bf16[128,512]{1,0:T(8,128)(2,1)S(1)}, u32[]{:S(2)}, u32[]{:S(2)}) %collective-permute-start.6) | collective-permute-done | bytes 131104 | tf_op jit(solution)/shard_map/ppermute | solution.py:26
  35.7 1.6 %collective-permute-start.8 = (bf16[128,512]{1,0:T(8,128)(2,1)S(1)}, bf16[128,512]{1,0:T(8,128)(2,1)S(1)}, u32[]{:S(2)}, u32[]{:S(2)}) collective-permute-start(bf16[128,512]{1,0:T(8,128)(2,1)S(1)} %collective-permute-done.6.refs_6_), channel_id=1, source_target_pairs={{0,2},{2,0},{1,3},{3,1},{4,6},{6,4},{5,7},{7,5},{8,10},{10,8},{9,1... | collective-permute-start | bytes 393224 | tf_op jit(solution)/shard_map/ppermute | solution.py:26
  37.3 2.4 %collective-permute-done.8.refs_8_ = bf16[128,512]{1,0:T(8,128)(2,1)S(1)} collective-permute-done((bf16[128,512]{1,0:T(8,128)(2,1)S(1)}, bf16[128,512]{1,0:T(8,128)(2,1)S(1)}, u32[]{:S(2)}, u32[]{:S(2)}) %collective-permute-start.8) | collective-permute-done | bytes 131104 | tf_op jit(solution)/shard_map/ppermute | solution.py:26
  39.8 0.5 copy-done.22
  40.3 0.1 copy-done.17
  40.4 0.1 copy-done.18
  40.5 0.0 copy-done.15
  40.6 22.4 %shard_map.127 = (bf16[1,1,128,4096]{3,2,1,0:T(8,128)(2,1)}, bf16[1,1,128,4096]{3,2,1,0:T(8,128)(2,1)}, bf16[1,1,128,1024]{3,2,1,0:T(8,128)(2,1)}, bf16[1,1,128,...) custom-call(s32[1]{0:T(128)} %bitcast.side_ref, ...), custom_call_target="tpu_custom_call" | custom-call | flops 7000000000 | bytes 16000000 | tf_op jit(solution)/shard_map/pallas_call | solution.py:141
  63.0 1.5 %collective-permute-start.21 = (bf16[256,512]{1,0:T(8,128)(2,1)}, bf16[256,512]{1,0:T(8,128)(2,1)S(1)}, u32[]{:S(2)}, u32[]{:S(2)}) collective-permute-start(bf16[256,512]{1,0:T(8,128)(2,1)} %get-tuple-element.30), channel_id=1, source_target_pairs={{0,2},{2,0},{1,3},{3,1},{4,6},{6,4},{5,7},{7,5},{8,10},{10,8},{9,1... | collective-permute-start | bytes 786440 | tf_op jit(solution)/shard_map/ppermute | solution.py:26
  64.5 0.7 fusion.5
  65.3 2.6 %collective-permute-start.14 = (f32[1,128]{1,0:T(1,128)S(1)}, f32[1,128]{1,0:T(1,128)S(1)}, u32[]{:S(2)}, u32[]{:S(2)}) collective-permute-start(f32[1,128]{1,0:T(1,128)S(1)} %fusion.5), channel_id=1, source_target_pairs={{0,192},{64,0},{128,64},{192,128},{1,193},{65,1},{129,65},{193,129... | collective-permute-start | bytes 1544 | tf_op jit(solution)/shard_map/ppermute | solution.py:26
  67.8 0.5 collective-permute-start.13
  68.3 0.6 collective-permute-start.12
  68.9 0.9 slice.147
  69.9 1.0 slice.148
  70.9 0.1 collective-permute-start.18
  71.0 2.7 %collective-permute-start.19 = (bf16[256,512]{1,0:T(8,128)(2,1)}, bf16[256,512]{1,0:T(8,128)(2,1)S(1)}, u32[]{:S(2)}, u32[]{:S(2)}) collective-permute-start(bf16[256,512]{1,0:T(8,128)(2,1)} %get-tuple-element.27), channel_id=1, source_target_pairs={{0,12},{4,0},{8,4},{12,8},{1,13},{5,1},{9,5},{13,9},{2,14},{6,2},{... | collective-permute-start | bytes 786440 | tf_op jit(solution)/shard_map/ppermute | solution.py:26
  73.6 1.0 add_convert_fusion
  74.7 2.9 %collective-permute-done.18 = bf16[256,512]{1,0:T(8,128)(2,1)S(1)} collective-permute-done((bf16[256,512]{1,0:T(8,128)(2,1)}, bf16[256,512]{1,0:T(8,128)(2,1)S(1)}, u32[]{:S(2)}, u32[]{:S(2)}) %collective-permute-start.18) | collective-permute-done | bytes 262176 | tf_op jit(solution)/shard_map/ppermute | solution.py:26
  77.6 0.1 add_convert_fusion.1
  77.7 0.1 collective-permute-start.20
  77.8 4.8 %collective-permute-done.24 = bf16[128,512]{1,0:T(8,128)(2,1)S(1)} collective-permute-done((bf16[128,512]{1,0:T(8,128)(2,1)S(1)}, bf16[128,512]{1,0:T(8,128)(2,1)S(1)}, u32[]{:S(2)}, u32[]{:S(2)}) %collective-permute-start.24) | collective-permute-done | bytes 131104 | tf_op jit(solution)/shard_map/ppermute | solution.py:26
  82.7 5.0 %collective-permute-done.22 = bf16[128,512]{1,0:T(8,128)(2,1)S(1)} collective-permute-done((bf16[128,512]{1,0:T(8,128)(2,1)S(1)}, bf16[128,512]{1,0:T(8,128)(2,1)S(1)}, u32[]{:S(2)}, u32[]{:S(2)}) %collective-permute-start.22) | collective-permute-done | bytes 131104 | tf_op jit(solution)/shard_map/ppermute | solution.py:26
  87.8 1.8 %collective-permute-start.23 = (bf16[256,512]{1,0:T(8,128)(2,1)S(1)}, bf16[256,512]{1,0:T(8,128)(2,1)S(1)}, u32[]{:S(2)}, u32[]{:S(2)}) collective-permute-start(bf16[256,512]{1,0:T(8,128)(2,1)S(1)} %pad_maximum_fusion.1), channel_id=1, source_target_pairs={{0,4},{4,8},{8,12},{12,0},{1,5},{5,9},{9,13},{13,1},{2,6},{6,10},{... | collective-permute-start | bytes 786440 | tf_op jit(solution)/shard_map/ppermute | solution.py:26
  89.5 5.2 %collective-permute-start.17 = (f32[1,128]{1,0:T(1,128)S(1)}, f32[1,128]{1,0:T(1,128)S(1)}, u32[]{:S(2)}, u32[]{:S(2)}) collective-permute-start(f32[1,128]{1,0:T(1,128)S(1)} %add_add_fusion.1), channel_id=1, source_target_pairs={{0,48},{16,0},{32,16},{48,32},{1,49},{17,1},{33,17},{49,33},{2,50}... | collective-permute-start | bytes 1544 | tf_op jit(solution)/shard_map/ppermute | solution.py:26
  94.7 1.2 collective-permute-start.16
  95.9 2.1 %collective-permute-start.15 = (f32[1,128]{1,0:T(1,128)S(1)}, f32[1,128]{1,0:T(1,128)S(1)}, u32[]{:S(2)}, u32[]{:S(2)}) collective-permute-start(f32[1,128]{1,0:T(1,128)S(1)} %add_add_fusion.1), channel_id=1, source_target_pairs={{0,16},{16,32},{32,48},{48,0},{1,17},{17,33},{33,49},{49,1},{2,18}... | collective-permute-start | bytes 1544 | tf_op jit(solution)/shard_map/ppermute | solution.py:26
  98.0 3.0 %collective-permute-done.16 = f32[1,128]{1,0:T(1,128)S(1)} collective-permute-done((f32[1,128]{1,0:T(1,128)S(1)}, f32[1,128]{1,0:T(1,128)S(1)}, u32[]{:S(2)}, u32[]{:S(2)}) %collective-permute-start.16) | collective-permute-done | bytes 544 | tf_op jit(solution)/shard_map/ppermute | solution.py:26
  101.0 9.8 %collective-permute-start.11 = (bf16[128,5120]{1,0:T(8,128)(2,1)}, bf16[128,5120]{1,0:T(8,128)(2,1)S(1)}, u32[]{:S(2)}, u32[]{:S(2)}) collective-permute-start(bf16[128,5120]{1,0:T(8,128)(2,1)} %get-tuple-element.20), channel_id=1, source_target_pairs={{0,1},{1,0},{2,3},{3,2},{4,5},{5,4},{6,7},{7,6},{8,9},{9,8},{10,11... | collective-permute-start | bytes 3932168 | tf_op jit(solution)/shard_map/ppermute | solution.py:26
  110.9 0.1 multiply_convert_fusion.1
  111.1 0.1 collective-permute-start.26
  111.2 2.4 %collective-permute-done.26 = bf16[64,1024]{1,0:T(8,128)(2,1)S(1)} collective-permute-done((bf16[64,1024]{1,0:T(8,128)(2,1)S(1)}, bf16[64,1024]{1,0:T(8,128)(2,1)S(1)}, u32[]{:S(2)}, u32[]{:S(2)}) %collective-permute-start.26) | collective-permute-done | bytes 131104 | tf_op jit(solution)/shard_map/ppermute | solution.py:26
  113.7 0.8 maximum_select_fusion
  114.5 1.0 reshape.161
  115.5 0.1 fusion.18
  115.6 0.4 fusion.19
  115.9 0.1 copy.14
  116.1 0.7 copy-done
  116.9 1.2 fusion
  118.1 0.8 fusion.2
  118.9 0.8 fusion.1
  119.6 0.4 broadcast_in_dim.23
  120.0 0.1 constant_dynamic-update-slice_fusion.3
  120.1 1.0 copy-done.20
  (84 shorter events, 0.6 us)
Async XLA Ops:
  0.6 12.2 %copy-start.6 = (bf16[1,1,128,4096]{3,2,1,0:T(8,128)(2,1)S(1)}, bf16[1,1,128,4096]{3,2,1,0:T(8,128)(2,1)}, u32[]{:S(2)}) copy-start(bf16[1,1,128,4096]{3,2,1,0:T(8,128)(2,1)} %refs_10_.1) | copy-start | bytes 3145732
  0.6 12.2 %copy-start.7 = (bf16[1,1,128,4096]{3,2,1,0:T(8,128)(2,1)S(1)}, bf16[1,1,128,4096]{3,2,1,0:T(8,128)(2,1)}, u32[]{:S(2)}) copy-start(bf16[1,1,128,4096]{3,2,1,0:T(8,128)(2,1)} %refs_11_.1) | copy-start | bytes 3145732
  7.6 6.2 %collective-permute-start = (bf16[144,512]{1,0:T(8,128)(2,1)S(1)}, bf16[144,512]{1,0:T(8,128)(2,1)S(1)}, u32[]{:S(2)}, u32[]{:S(2)}) collective-permute-start(bf16[144,512]{1,0:T(8,128)(2,1)S(1)} %pad_maximum_fusion.3), channel_id=1, source_target_pairs={{0,1},{1,0},{2,3},{3,2},{4,5},{5,4},{6,7},{7,6},{8,9},{9,8},{10,11... | collective-permute-start | bytes 442376 | tf_op jit(solution)/shard_map/ppermute | solution.py:26
  12.9 0.9 copy-start.9
  12.9 1.0 copy-start.10
  13.1 26.7 %collective-permute-start.10 = (bf16[128,5120]{1,0:T(8,128)(2,1)S(1)}, bf16[128,5120]{1,0:T(8,128)(2,1)}, u32[]{:S(2)}, u32[]{:S(2)}) collective-permute-start(bf16[128,5120]{1,0:T(8,128)(2,1)S(1)} %pad_maximum_fusion), channel_id=1, source_target_pairs={{0,1},{1,0},{2,3},{3,2},{4,5},{5,4},{6,7},{7,6},{8,9},{9,8},{10,11... | collective-permute-start | bytes 3932168 | tf_op jit(solution)/shard_map/ppermute | solution.py:26
  14.0 25.7 %copy-start.13 = (bf16[272,512]{1,0:T(8,128)(2,1)}, bf16[272,512]{1,0:T(8,128)(2,1)S(1)}, u32[]{:S(2)}) copy-start(bf16[272,512]{1,0:T(8,128)(2,1)S(1)} %constant_dynamic-update-slice_fusion.refs_0_) | copy-start | bytes 835588
  14.0 8.3 %collective-permute-start.2 = (bf16[272,512]{1,0:T(8,128)(2,1)S(1)}, bf16[272,512]{1,0:T(8,128)(2,1)S(1)}, u32[]{:S(2)}, u32[]{:S(2)}) collective-permute-start(bf16[272,512]{1,0:T(8,128)(2,1)S(1)} %constant_dynamic-update-slice_fusion.refs_0_), channel_id=1, source_target_pairs={{0,12},{4,0},{8,4},{12,8},{1,13},{5,1},{9,5},{13,9},{2,14},{6,2},{... | collective-permute-start | bytes 835592 | tf_op jit(solution)/shard_map/ppermute | solution.py:26
  15.0 9.6 %collective-permute-start.1 = (bf16[272,512]{1,0:T(8,128)(2,1)S(1)}, bf16[272,512]{1,0:T(8,128)(2,1)S(1)}, u32[]{:S(2)}, u32[]{:S(2)}) collective-permute-start(bf16[272,512]{1,0:T(8,128)(2,1)S(1)} %constant_dynamic-update-slice_fusion.refs_0_), channel_id=1, source_target_pairs={{0,2},{2,0},{1,3},{3,1},{4,6},{6,4},{5,7},{7,5},{8,10},{10,8},{9,1... | collective-permute-start | bytes 835592 | tf_op jit(solution)/shard_map/ppermute | solution.py:26
  16.7 10.6 %collective-permute-start.3 = (bf16[272,512]{1,0:T(8,128)(2,1)S(1)}, bf16[272,512]{1,0:T(8,128)(2,1)S(1)}, u32[]{:S(2)}, u32[]{:S(2)}) collective-permute-start(bf16[272,512]{1,0:T(8,128)(2,1)S(1)} %constant_dynamic-update-slice_fusion.refs_0_), channel_id=1, source_target_pairs={{0,4},{4,8},{8,12},{12,0},{1,5},{5,9},{9,13},{13,1},{2,6},{6,10},{... | collective-permute-start | bytes 835592 | tf_op jit(solution)/shard_map/ppermute | solution.py:26
  22.3 17.5 %copy-start.11 = (bf16[272,512]{1,0:T(8,128)(2,1)}, bf16[272,512]{1,0:T(8,128)(2,1)S(1)}, u32[]{:S(2)}) copy-start(bf16[272,512]{1,0:T(8,128)(2,1)S(1)} %collective-permute-done.2.refs_2_) | copy-start | bytes 835588
  22.3 5.1 %collective-permute-start.7 = (bf16[144,512]{1,0:T(8,128)(2,1)S(1)}, bf16[144,512]{1,0:T(8,128)(2,1)S(1)}, u32[]{:S(2)}, u32[]{:S(2)}) collective-permute-start(bf16[144,512]{1,0:T(8,128)(2,1)S(1)} %slice.161), channel_id=1, source_target_pairs={{0,12},{4,0},{8,4},{12,8},{1,13},{5,1},{9,5},{13,9},{2,14},{6,2},{... | collective-permute-start | bytes 442376 | tf_op jit(solution)/shard_map/ppermute | solution.py:26
  24.6 15.2 %copy-start.16 = (bf16[272,512]{1,0:T(8,128)(2,1)}, bf16[272,512]{1,0:T(8,128)(2,1)S(1)}, u32[]{:S(2)}) copy-start(bf16[272,512]{1,0:T(8,128)(2,1)S(1)} %collective-permute-done.1.refs_1_) | copy-start | bytes 835588
  24.6 15.1 %collective-permute-start.5 = (bf16[272,512]{1,0:T(8,128)(2,1)S(1)}, bf16[272,512]{1,0:T(8,128)(2,1)S(1)}, u32[]{:S(2)}, u32[]{:S(2)}) collective-permute-start(bf16[272,512]{1,0:T(8,128)(2,1)S(1)} %collective-permute-done.1.refs_1_), channel_id=1, source_target_pairs={{0,4},{4,8},{8,12},{12,0},{1,5},{5,9},{9,13},{13,1},{2,6},{6,10},{... | collective-permute-start | bytes 835592 | tf_op jit(solution)/shard_map/ppermute | solution.py:26
  24.6 15.1 %collective-permute-start.4 = (bf16[272,512]{1,0:T(8,128)(2,1)S(1)}, bf16[272,512]{1,0:T(8,128)(2,1)S(1)}, u32[]{:S(2)}, u32[]{:S(2)}) collective-permute-start(bf16[272,512]{1,0:T(8,128)(2,1)S(1)} %collective-permute-done.1.refs_1_), channel_id=1, source_target_pairs={{0,12},{4,0},{8,4},{12,8},{1,13},{5,1},{9,5},{13,9},{2,14},{6,2},{... | collective-permute-start | bytes 835592 | tf_op jit(solution)/shard_map/ppermute | solution.py:26
  27.3 12.5 %copy-start.12 = (bf16[272,512]{1,0:T(8,128)(2,1)}, bf16[272,512]{1,0:T(8,128)(2,1)S(1)}, u32[]{:S(2)}) copy-start(bf16[272,512]{1,0:T(8,128)(2,1)S(1)} %collective-permute-done.3.refs_3_) | copy-start | bytes 835588
  27.3 8.4 %collective-permute-start.6 = (bf16[128,512]{1,0:T(8,128)(2,1)S(1)}, bf16[128,512]{1,0:T(8,128)(2,1)S(1)}, u32[]{:S(2)}, u32[]{:S(2)}) collective-permute-start(bf16[128,512]{1,0:T(8,128)(2,1)S(1)} %slice.160), channel_id=1, source_target_pairs={{0,4},{4,8},{8,12},{12,0},{1,5},{5,9},{9,13},{13,1},{2,6},{6,10},{... | collective-permute-start | bytes 393224 | tf_op jit(solution)/shard_map/ppermute | solution.py:26
  27.4 12.4 %copy-start.14 = (bf16[144,512]{1,0:T(8,128)(2,1)}, bf16[144,512]{1,0:T(8,128)(2,1)S(1)}, u32[]{:S(2)}) copy-start(bf16[144,512]{1,0:T(8,128)(2,1)S(1)} %collective-permute-done.7.refs_7_) | copy-start | bytes 442372
  27.4 12.3 %collective-permute-start.9 = (bf16[144,512]{1,0:T(8,128)(2,1)S(1)}, bf16[144,512]{1,0:T(8,128)(2,1)S(1)}, u32[]{:S(2)}, u32[]{:S(2)}) collective-permute-start(bf16[144,512]{1,0:T(8,128)(2,1)S(1)} %collective-permute-done.7.refs_7_), channel_id=1, source_target_pairs={{0,2},{2,0},{1,3},{3,1},{4,6},{6,4},{5,7},{7,5},{8,10},{10,8},{9,1... | collective-permute-start | bytes 442376 | tf_op jit(solution)/shard_map/ppermute | solution.py:26
  35.7 4.1 %copy-start.21 = (bf16[128,512]{1,0:T(8,128)(2,1)}, bf16[128,512]{1,0:T(8,128)(2,1)S(1)}, u32[]{:S(2)}) copy-start(bf16[128,512]{1,0:T(8,128)(2,1)S(1)} %collective-permute-done.6.refs_6_) | copy-start | bytes 393220
  35.7 4.0 %collective-permute-start.8 = (bf16[128,512]{1,0:T(8,128)(2,1)S(1)}, bf16[128,512]{1,0:T(8,128)(2,1)S(1)}, u32[]{:S(2)}, u32[]{:S(2)}) collective-permute-start(bf16[128,512]{1,0:T(8,128)(2,1)S(1)} %collective-permute-done.6.refs_6_), channel_id=1, source_target_pairs={{0,2},{2,0},{1,3},{3,1},{4,6},{6,4},{5,7},{7,5},{8,10},{10,8},{9,1... | collective-permute-start | bytes 393224 | tf_op jit(solution)/shard_map/ppermute | solution.py:26
  39.7 0.7 copy-start.22
  39.7 0.8 copy-start.17
  39.7 0.8 copy-start.18
  39.7 0.8 copy-start.15
  63.0 14.6 %copy-start.8 = (bf16[256,512]{1,0:T(8,128)(2,1)S(1)}, bf16[256,512]{1,0:T(8,128)(2,1)}, u32[]{:S(2)}) copy-start(bf16[256,512]{1,0:T(8,128)(2,1)} %get-tuple-element.25) | copy-start | bytes 786436
  63.0 8.0 %collective-permute-start.21 = (bf16[256,512]{1,0:T(8,128)(2,1)}, bf16[256,512]{1,0:T(8,128)(2,1)S(1)}, u32[]{:S(2)}, u32[]{:S(2)}) collective-permute-start(bf16[256,512]{1,0:T(8,128)(2,1)} %get-tuple-element.30), channel_id=1, source_target_pairs={{0,2},{2,0},{1,3},{3,1},{4,6},{6,4},{5,7},{7,5},{8,10},{10,8},{9,1... | collective-permute-start | bytes 786440 | tf_op jit(solution)/shard_map/ppermute | solution.py:26
  65.3 22.5 %collective-permute-start.14 = (f32[1,128]{1,0:T(1,128)S(1)}, f32[1,128]{1,0:T(1,128)S(1)}, u32[]{:S(2)}, u32[]{:S(2)}) collective-permute-start(f32[1,128]{1,0:T(1,128)S(1)} %fusion.5), channel_id=1, source_target_pairs={{0,192},{64,0},{128,64},{192,128},{1,193},{65,1},{129,65},{193,129... | collective-permute-start | bytes 1544 | tf_op jit(solution)/shard_map/ppermute | solution.py:26
  67.8 21.7 %collective-permute-start.13 = (f32[1,128]{1,0:T(1,128)S(1)}, f32[1,128]{1,0:T(1,128)S(1)}, u32[]{:S(2)}, u32[]{:S(2)}) collective-permute-start(f32[1,128]{1,0:T(1,128)S(1)} %fusion.5), channel_id=1, source_target_pairs={{0,128},{64,192},{128,0},{192,64},{1,129},{65,193},{129,1},{193,65... | collective-permute-start | bytes 1544 | tf_op jit(solution)/shard_map/ppermute | solution.py:26
  68.3 21.2 %collective-permute-start.12 = (f32[1,128]{1,0:T(1,128)S(1)}, f32[1,128]{1,0:T(1,128)S(1)}, u32[]{:S(2)}, u32[]{:S(2)}) collective-permute-start(f32[1,128]{1,0:T(1,128)S(1)} %fusion.5), channel_id=1, source_target_pairs={{0,64},{64,128},{128,192},{192,0},{1,65},{65,129},{129,193},{193,1... | collective-permute-start | bytes 1544 | tf_op jit(solution)/shard_map/ppermute | solution.py:26
  69.9 12.8 %copy-start.5 = (bf16[256,512]{1,0:T(8,128)(2,1)S(1)}, bf16[256,512]{1,0:T(8,128)(2,1)}, u32[]{:S(2)}) copy-start(bf16[256,512]{1,0:T(8,128)(2,1)} %get-tuple-element.31) | copy-start | bytes 786436
  70.9 6.7 %collective-permute-start.18 = (bf16[256,512]{1,0:T(8,128)(2,1)}, bf16[256,512]{1,0:T(8,128)(2,1)S(1)}, u32[]{:S(2)}, u32[]{:S(2)}) collective-permute-start(bf16[256,512]{1,0:T(8,128)(2,1)} %get-tuple-element.26), channel_id=1, source_target_pairs={{0,4},{4,8},{8,12},{12,0},{1,5},{5,9},{9,13},{13,1},{2,6},{6,10},{... | collective-permute-start | bytes 786440 | tf_op jit(solution)/shard_map/ppermute | solution.py:26
  71.0 6.6 %collective-permute-start.19 = (bf16[256,512]{1,0:T(8,128)(2,1)}, bf16[256,512]{1,0:T(8,128)(2,1)S(1)}, u32[]{:S(2)}, u32[]{:S(2)}) collective-permute-start(bf16[256,512]{1,0:T(8,128)(2,1)} %get-tuple-element.27), channel_id=1, source_target_pairs={{0,12},{4,0},{8,4},{12,8},{1,13},{5,1},{9,5},{13,9},{2,14},{6,2},{... | collective-permute-start | bytes 786440 | tf_op jit(solution)/shard_map/ppermute | solution.py:26
  74.6 13.1 %copy-start.4 = (bf16[256,512]{1,0:T(8,128)(2,1)S(1)}, bf16[256,512]{1,0:T(8,128)(2,1)}, u32[]{:S(2)}) copy-start(bf16[256,512]{1,0:T(8,128)(2,1)} %get-tuple-element.28) | copy-start | bytes 786436
  77.6 5.1 %collective-permute-start.24 = (bf16[128,512]{1,0:T(8,128)(2,1)S(1)}, bf16[128,512]{1,0:T(8,128)(2,1)S(1)}, u32[]{:S(2)}, u32[]{:S(2)}) collective-permute-start(bf16[128,512]{1,0:T(8,128)(2,1)S(1)} %get-tuple-element.41), channel_id=1, source_target_pairs={{0,12},{4,0},{8,4},{12,8},{1,13},{5,1},{9,5},{13,9},{2,14},{6,2},{... | collective-permute-start | bytes 393224 | tf_op jit(solution)/shard_map/ppermute | solution.py:26
  77.6 33.3 %copy-start.1 = (f32[256,512]{1,0:T(8,128)S(1)}, f32[256,512]{1,0:T(8,128)}, u32[]{:S(2)}) copy-start(f32[256,512]{1,0:T(8,128)} %get-tuple-element.24) | copy-start | bytes 1572868
  77.7 33.2 %collective-permute-start.20 = (bf16[256,512]{1,0:T(8,128)(2,1)S(1)}, bf16[256,512]{1,0:T(8,128)(2,1)S(1)}, u32[]{:S(2)}, u32[]{:S(2)}) collective-permute-start(bf16[256,512]{1,0:T(8,128)(2,1)S(1)} %add_convert_fusion.1), channel_id=1, source_target_pairs={{0,2},{2,0},{1,3},{3,1},{4,6},{6,4},{5,7},{7,5},{8,10},{10,8},{9,1... | collective-permute-start | bytes 786440 | tf_op jit(solution)/shard_map/ppermute | solution.py:26
  82.6 5.0 %collective-permute-start.22 = (bf16[128,512]{1,0:T(8,128)(2,1)S(1)}, bf16[128,512]{1,0:T(8,128)(2,1)S(1)}, u32[]{:S(2)}, u32[]{:S(2)}) collective-permute-start(bf16[128,512]{1,0:T(8,128)(2,1)S(1)} %get-tuple-element.40), channel_id=1, source_target_pairs={{0,4},{4,8},{8,12},{12,0},{1,5},{5,9},{9,13},{13,1},{2,6},{6,10},{... | collective-permute-start | bytes 393224 | tf_op jit(solution)/shard_map/ppermute | solution.py:26
  87.7 23.2 %collective-permute-start.25 = (bf16[256,512]{1,0:T(8,128)(2,1)S(1)}, bf16[256,512]{1,0:T(8,128)(2,1)S(1)}, u32[]{:S(2)}, u32[]{:S(2)}) collective-permute-start(bf16[256,512]{1,0:T(8,128)(2,1)S(1)} %pad_maximum_fusion.2), channel_id=1, source_target_pairs={{0,12},{4,0},{8,4},{12,8},{1,13},{5,1},{9,5},{13,9},{2,14},{6,2},{... | collective-permute-start | bytes 786440 | tf_op jit(solution)/shard_map/ppermute | solution.py:26
  87.8 23.2 %collective-permute-start.23 = (bf16[256,512]{1,0:T(8,128)(2,1)S(1)}, bf16[256,512]{1,0:T(8,128)(2,1)S(1)}, u32[]{:S(2)}, u32[]{:S(2)}) collective-permute-start(bf16[256,512]{1,0:T(8,128)(2,1)S(1)} %pad_maximum_fusion.1), channel_id=1, source_target_pairs={{0,4},{4,8},{8,12},{12,0},{1,5},{5,9},{9,13},{13,1},{2,6},{6,10},{... | collective-permute-start | bytes 786440 | tf_op jit(solution)/shard_map/ppermute | solution.py:26
  89.5 6.4 %collective-permute-start.17 = (f32[1,128]{1,0:T(1,128)S(1)}, f32[1,128]{1,0:T(1,128)S(1)}, u32[]{:S(2)}, u32[]{:S(2)}) collective-permute-start(f32[1,128]{1,0:T(1,128)S(1)} %add_add_fusion.1), channel_id=1, source_target_pairs={{0,48},{16,0},{32,16},{48,32},{1,49},{17,1},{33,17},{49,33},{2,50}... | collective-permute-start | bytes 1544 | tf_op jit(solution)/shard_map/ppermute | solution.py:26
  94.7 6.3 %collective-permute-start.16 = (f32[1,128]{1,0:T(1,128)S(1)}, f32[1,128]{1,0:T(1,128)S(1)}, u32[]{:S(2)}, u32[]{:S(2)}) collective-permute-start(f32[1,128]{1,0:T(1,128)S(1)} %add_add_fusion.1), channel_id=1, source_target_pairs={{0,32},{16,48},{32,0},{48,16},{1,33},{17,49},{33,1},{49,17},{2,34}... | collective-permute-start | bytes 1544 | tf_op jit(solution)/shard_map/ppermute | solution.py:26
  95.9 14.9 %collective-permute-start.15 = (f32[1,128]{1,0:T(1,128)S(1)}, f32[1,128]{1,0:T(1,128)S(1)}, u32[]{:S(2)}, u32[]{:S(2)}) collective-permute-start(f32[1,128]{1,0:T(1,128)S(1)} %add_add_fusion.1), channel_id=1, source_target_pairs={{0,16},{16,32},{32,48},{48,0},{1,17},{17,33},{33,49},{49,1},{2,18}... | collective-permute-start | bytes 1544 | tf_op jit(solution)/shard_map/ppermute | solution.py:26
  101.0 13.4 %collective-permute-start.11 = (bf16[128,5120]{1,0:T(8,128)(2,1)}, bf16[128,5120]{1,0:T(8,128)(2,1)S(1)}, u32[]{:S(2)}, u32[]{:S(2)}) collective-permute-start(bf16[128,5120]{1,0:T(8,128)(2,1)} %get-tuple-element.20), channel_id=1, source_target_pairs={{0,1},{1,0},{2,3},{3,2},{4,5},{5,4},{6,7},{7,6},{8,9},{9,8},{10,11... | collective-permute-start | bytes 3932168 | tf_op jit(solution)/shard_map/ppermute | solution.py:26
  111.1 2.5 %collective-permute-start.26 = (bf16[64,1024]{1,0:T(8,128)(2,1)S(1)}, bf16[64,1024]{1,0:T(8,128)(2,1)S(1)}, u32[]{:S(2)}, u32[]{:S(2)}) collective-permute-start(bf16[64,1024]{1,0:T(8,128)(2,1)S(1)} %pad_maximum_fusion.4), channel_id=1, source_target_pairs={{0,1},{1,0},{2,3},{3,2},{4,5},{5,4},{6,7},{7,6},{8,9},{9,8},{10,11... | collective-permute-start | bytes 393224 | tf_op jit(solution)/shard_map/ppermute | solution.py:26
  115.6 1.2 %copy-start = (bf16[1,1,128,4096]{3,2,1,0:T(8,128)(2,1)S(1)}, bf16[1,1,128,4096]{3,2,1,0:T(8,128)(2,1)}, u32[]{:S(2)}) copy-start(bf16[1,1,128,4096]{3,2,1,0:T(8,128)(2,1)} %get-tuple-element.21) | copy-start | bytes 3145732
  116.8 1.2 copy-start.2
  116.9 1.2 copy-start.3
  118.1 1.9 %copy-start.19 = (bf16[1,1,128,4096]{3,2,1,0:T(8,128)(2,1)S(1)}, bf16[1,1,128,4096]{3,2,1,0:T(8,128)(2,1)}, u32[]{:S(2)}) copy-start(bf16[1,1,128,4096]{3,2,1,0:T(8,128)(2,1)} %get-tuple-element.19) | copy-start | bytes 3145732
  120.1 1.0 copy-start.20

commit v2 on v0

v2 whole, which is shorter than its diff:
```python
import functools

import jax
import jax.numpy as jnp
from jax import lax
from jax.experimental import pallas as pl
from jax.experimental.pallas import tpu as pltpu
from jax.sharding import Mesh
from jax.sharding import PartitionSpec as P

BF16 = jnp.bfloat16
F32 = jnp.float32
KVH = 8
HD = 128
S_BLOCK, BLOCK, O_BLOCK, D_BLOCK = 384, 128, 1152, 384
VMEM = 40 * 2**20
LOG2E = 1.4426950408889634
NT = (((1,), (1,)), ((), ()))
NN = (((1,), (0,)), ((), ()))


def dot(a, b, dims=NN):
    return lax.dot_general(a, b, dims, preferred_element_type=F32)


def step(values, axis, by):
    size = lax.axis_size(axis)
    return lax.ppermute(values, axis, [(i, (i + by) % size) for i in range(size)])


def heads_to_rows(wide):
    return jnp.concatenate([wide[:, i * HD : (i + 1) * HD] for i in range(wide.shape[1] // HD)], axis=0)


def tree(op, parts):
    while len(parts) > 1:
        parts = [op(*parts[i : i + 2]) if i + 1 < len(parts) else parts[i] for i in range(0, len(parts), 2)]
    return parts[0]


def response_steps(facts, queries, upstream, keys, values, keys_t, values_t, e_scr, p_scr, d_scr, q_all, c_all, cols, att, grad, scale):
    length, advantage = facts
    slots = queries.shape[0]
    key_count = e_scr.shape[0]
    prompt_len = key_count - slots
    token = lax.broadcasted_iota(jnp.int32, (slots, HD), 0).astype(F32)
    live = token < length
    weight = jnp.where(live, jnp.broadcast_to(advantage, live.shape), 0.0)
    per_head = queries.shape[1] // HD
    q_rows = heads_to_rows(queries)
    cot = [(upstream[:, i * HD : (i + 1) * HD].astype(F32) * weight).astype(BF16) for i in range(per_head)]
    cot_rows = jnp.concatenate(cot, axis=0)
    q_all[cols] = q_rows
    c_all[cols] = cot_rows
    groups = lambda a: [a[i : i + 8] for i in range(0, a.shape[0], 8)]
    tops, sums = [], []
    for first in range(0, key_count, S_BLOCK):
        scores = dot(keys[first : first + S_BLOCK], q_rows, NT)
        if first + S_BLOCK > prompt_len:
            key_pos = lax.broadcasted_iota(jnp.int32, scores.shape, 0) + (first - prompt_len)
            row_pos = lax.broadcasted_iota(jnp.int32, scores.shape, 1) % slots
            scores = jnp.where(key_pos <= row_pos, scores, -jnp.inf)
        e_scr[first : first + S_BLOCK] = scores
        tops.append(tree(jnp.maximum, groups(scores)))
        yield
    yield "S"
    row_max = jnp.max(tree(jnp.maximum, tops), axis=0, keepdims=True) * (scale * LOG2E)
    for first in range(0, key_count, BLOCK):
        raised = jnp.exp2(e_scr[first : first + BLOCK] * (scale * LOG2E) - row_max)
        e_scr[first : first + BLOCK] = raised
        sums.append(tree(jnp.add, groups(raised)))
        yield
    yield "E"
    inverse = 1.0 / jnp.sum(tree(jnp.add, sums), axis=0, keepdims=True)
    output_t = None
    for first in range(0, key_count, O_BLOCK):
        for at in range(first, first + O_BLOCK, BLOCK):
            p_scr[at : at + BLOCK, cols] = (e_scr[at : at + BLOCK] * inverse).astype(BF16)
        term = dot(values_t[:, first : first + O_BLOCK], p_scr[first : first + O_BLOCK, cols])
        output_t = term if output_t is None else output_t + term
        yield
    yield "O"
    cot_t = cot_rows.astype(F32).T
    delta = jnp.sum(cot_t * output_t, axis=0, keepdims=True)
    for i in range(per_head):
        att[:, i * HD : (i + 1) * HD] = jnp.where(live, output_t[:, i * slots : (i + 1) * slots].T, 0.0).astype(BF16)
    for first in range(0, key_count, D_BLOCK):
        dprobs = dot(values[first : first + D_BLOCK], cot_rows, NT)
        probs = e_scr[first : first + D_BLOCK] * inverse
        d_scr[first : first + D_BLOCK, cols] = (probs * (dprobs - delta)).astype(BF16)
        yield
    yield "D"
    grad_q_t = dot(keys_t[...], d_scr[:, cols]) * scale
    for i in range(per_head):
        grad[:, i * HD : (i + 1) * HD] = grad_q_t[:, i * slots : (i + 1) * slots].T.astype(BF16)
    wide = per_head * HD
    grad[:, wide : wide + HD] = (dot(d_scr[prompt_len:, cols], q_rows) * scale).astype(BF16)
    grad[:, wide + HD :] = dot(p_scr[prompt_len:, cols], cot_rows).astype(BF16)
    yield "G"


def run(steps, until):
    for mark in steps:
        yield
        if mark == until:
            return


def turns(*runs):
    runs = list(runs)
    while runs:
        for r in list(runs):
            try:
                next(r)
            except StopIteration:
                runs.remove(r)


def prep_kernel(k_in, v_in, length_in, reward_in, keep, give, side_out):
    rows, width = k_in.shape[1:]
    half = width // 2
    reward = jnp.broadcast_to(reward_in[...], (16, half))
    length = jnp.broadcast_to(length_in[...].astype(F32), (16, half))
    high = reward.astype(BF16).astype(F32)
    middle = (reward - high).astype(BF16).astype(F32)
    row = lax.broadcasted_iota(jnp.int32, (16, half), 0) % 8
    facts = length
    for at, value in ((1, high), (2, middle), (3, reward - high - middle)):
        facts = jnp.where(row == at, value, facts)
    facts = jnp.where(row < 4, facts, 0.0).astype(BF16)

    def write(mine, other):
        for out, cols in ((mine, slice(0, half)), (other, slice(half, width))):
            out[0:rows] = k_in[0, :, cols]
            out[rows : 2 * rows] = v_in[0, :, cols]
            out[2 * rows :] = facts

    side = lax.axis_index("core")
    side_out[0] = side.astype(jnp.int32)
    pl.when(side == 0)(lambda: write(keep, give))
    pl.when(side != 0)(lambda: write(give, keep))


def prep(prompt_k, prompt_v, lengths, rewards):
    _, rows, width = prompt_k.shape
    whole = lambda shape: pl.BlockSpec(shape, lambda i: (0,) * len(shape))
    out = jax.ShapeDtypeStruct((2 * rows + 16, width // 2), BF16)
    return pl.pallas_call(
        prep_kernel,
        grid=(1,),
        in_specs=[whole(a.shape) for a in (prompt_k, prompt_v, lengths, rewards)],
        out_specs=[whole(out.shape), whole(out.shape), pl.BlockSpec(memory_space=pltpu.SMEM)],
        out_shape=[out, out, jax.ShapeDtypeStruct((1,), jnp.int32)],
        cost_estimate=pl.CostEstimate(flops=0, bytes_accessed=500_000, transcendentals=0),
        name="prep",
    )(prompt_k, prompt_v, lengths, rewards)


def pack_kernel(side_ref, *refs):
    inputs, out, sems = refs[:4], refs[4], refs[5]
    other = 1 - side_ref[0]
    copies, first = [], 0
    for i, a in enumerate(inputs):
        half = a.shape[3] // 2
        source = a.at[0, 0, :, pl.ds(pl.multiple_of(other * half, HD), half)]
        copies.append(pltpu.make_async_copy(source, out.at[:, first : first + half], sems.at[i]))
        first += half
    for copy in copies:
        copy.start()
    for copy in copies:
        copy.wait()


def pack(side, *inputs):
    width = sum(a.shape[3] for a in inputs) // 2
    return pl.pallas_call(
        pack_kernel,
        in_specs=[pl.BlockSpec(memory_space=pltpu.SMEM)] + [pl.BlockSpec(memory_space=pl.ANY)] * 4,
        out_specs=pl.BlockSpec(memory_space=pltpu.VMEM),
        out_shape=jax.ShapeDtypeStruct((inputs[0].shape[2], width), BF16),
        scratch_shapes=[pltpu.SemaphoreType.DMA((4,))],
        cost_estimate=pl.CostEstimate(flops=0, bytes_accessed=100_000, transcendentals=0),
        name="pack",
    )(side, *inputs)


def attention_kernel(scale, side_ref, *refs):
    blocks, parts = refs[:8], refs[19:25]
    q_own, g_own, k_own, v_own, q_sib, g_sib, k_sib, v_sib, own_att, own_grad, sib_out = refs[8:19]
    k_scr, v_scr, kt_scr, vt_scr, e_scr, p_scr, d_scr, q_all, c_all = refs[25:]
    slots, wide = q_own.shape[2:]
    rows = (blocks[0].shape[0] - 16) // 2
    parts = [(part, at) for part in parts for at in range(0, part.shape[0], 2 * rows)]
    prompt_len = len(blocks) * rows
    keys = [block[0:rows] for block in blocks]
    values = [block[rows : 2 * rows] for block in blocks]
    facts = [block[2 * rows :].astype(F32) for block in blocks]
    total = sum(facts[1:], facts[0])
    reward = lambda f, at: f[at + 1 : at + 2] + f[at + 2 : at + 3] + f[at + 3 : at + 4]
    reward_mean = (reward(total, 0) + reward(total, 8)) * (0.5 / len(blocks))
    keys, values = jnp.concatenate(keys, axis=0), jnp.concatenate(values, axis=0)
    keys_t, values_t = keys.T, values.T
    own = (0, q_own[0, 0], g_own[0, 0], k_own[0, 0], v_own[0, 0], own_att, own_grad)
    sib = (8, q_sib[...], g_sib[...], k_sib[...], v_sib[...], sib_out.at[:, :wide], sib_out.at[:, wide:])
    steps = []
    for n, (at, q, g, rk, rv, att, grad) in enumerate((own, sib)):
        for scr, shared, mine in ((k_scr, keys, rk), (v_scr, values, rv)):
            scr[n, :prompt_len] = shared
            scr[n, prompt_len:] = mine
        for scr, shared, mine in ((kt_scr, keys_t, rk), (vt_scr, values_t, rv)):
            scr[n, :, :prompt_len] = shared
            scr[n, :, prompt_len:] = mine.T
        cols = slice(n * (wide // HD) * slots, (n + 1) * (wide // HD) * slots)
        known = (facts[0][at : at + 1], reward(facts[0], at) - reward_mean)
        steps.append(response_steps(
            known, q, g, k_scr.at[n], v_scr.at[n], kt_scr.at[n], vt_scr.at[n], e_scr.at[n], p_scr, d_scr, q_all, c_all, cols, att, grad, scale
        ))
    a, b = steps
    turns(run(a, "S"))
    turns(run(a, "E"), run(b, "S"))
    turns(run(a, "O"), run(b, "E"))
    turns(run(a, "D"), run(b, "O"))
    turns(run(a, "G"), run(b, "D"))
    turns(run(b, "G"))
    for i, (part, at) in enumerate(parts):
        here = slice(i * rows, (i + 1) * rows)
        part[at : at + rows] = (dot(d_scr[here], q_all[...]) * scale).astype(part.dtype)
        part[at + rows : at + 2 * rows] = dot(p_scr[here], c_all[...]).astype(part.dtype)


def attention(side, blocks, resp_q, out_grad, resp_k, resp_v, packed, kv_heads):
    slots, width = resp_q.shape[2:]
    wide = width // KVH
    own = lambda w: pl.BlockSpec((1, 1, slots, w), lambda h, s: (0, 0, 0, s[0] * kv_heads + h))
    column = lambda n, w: pl.BlockSpec((n, w), lambda h, s: (0, h))
    theirs = lambda w, first: pl.BlockSpec((slots, w), lambda h, s: (0, first * kv_heads + h))
    widths = (wide, wide + 2 * HD, 2 * wide + 2 * HD)
    results = [jax.ShapeDtypeStruct((slots, kv_heads * w), BF16) for w in widths]
    height = blocks[0].shape[0] - 16
    heights = (height, height, 2 * height, 2 * height, height, height)
    parts = [jax.ShapeDtypeStruct((n, kv_heads * HD), BF16 if i else F32) for i, n in enumerate(heights)]
    keys = len(blocks) * height // 2 + slots
    rows = wide // HD * slots
    return pl.pallas_call(
        functools.partial(attention_kernel, float(HD) ** -0.5),
        grid_spec=pltpu.PrefetchScalarGridSpec(
            num_scalar_prefetch=1,
            grid=(kv_heads,),
            in_specs=[column(b.shape[0], HD) for b in blocks]
            + [own(wide), own(wide), own(HD), own(HD)]
            + [theirs(wide, 0), theirs(wide, 1), theirs(HD, 2 * wide // HD), theirs(HD, 2 * wide // HD + 1)],
            out_specs=[column(slots, w) for w in widths] + [column(n, HD) for n in heights],
            scratch_shapes=[pltpu.VMEM((2, keys, HD), BF16)] * 2
            + [pltpu.VMEM((2, HD, keys), BF16)] * 2
            + [pltpu.VMEM((2, keys, rows), F32)]
            + [pltpu.VMEM((keys, 2 * rows), BF16)] * 2
            + [pltpu.VMEM((2 * rows, HD), BF16)] * 2,
        ),
        out_shape=results + parts,
        compiler_params=pltpu.CompilerParams(vmem_limit_bytes=VMEM),
        cost_estimate=pl.CostEstimate(flops=14_000_000_000, bytes_accessed=12_000_000, transcendentals=5_000_000),
        name="attention",
    )(side, *blocks, resp_q, out_grad, resp_k, resp_v, *[packed] * 4)


def place_kernel(kv_heads, side_ref, own, sib, att):
    wide, block = att.shape[3] // kv_heads, sib.shape[1] // kv_heads
    mine = pl.program_id(0) == side_ref[0]

    @pl.when(mine)
    def _():
        att[0, 0] = own[...]

    @pl.when(jnp.logical_not(mine))
    def _():
        for h in range(kv_heads):
            att[0, 0, :, h * wide : (h + 1) * wide] = sib[:, h * block : h * block + wide]


def finish_kernel(kv_heads, count, side_ref, own, sib, total, passed, tokens, gq, gk, gv, gpk, gpv):
    wide = gq.shape[3] // kv_heads
    rows = gpk.shape[1]
    factor = count / tokens[0:1, 0:1]
    scaled = lambda values: (values.astype(F32) * factor).astype(BF16)

    def write(held):
        block = held.shape[1] // kv_heads
        for h in range(kv_heads):
            head = scaled(held[:, (h + 1) * block - wide - 2 * HD : (h + 1) * block])
            gq[0, 0, :, h * wide : (h + 1) * wide] = head[:, 0:wide]
            gk[0, 0, :, h * HD : (h + 1) * HD] = head[:, wide : wide + HD]
            gv[0, 0, :, h * HD : (h + 1) * HD] = head[:, wide + HD :]

    mine = pl.program_id(0) == side_ref[0]

    @pl.when(mine)
    def _():
        write(own)
        gpk[0] = scaled(total[0:rows])
        gpv[0] = scaled(total[2 * rows : 3 * rows])

    @pl.when(jnp.logical_not(mine))
    def _():
        write(sib)
        gpk[0] = scaled(passed[0:rows])
        gpv[0] = scaled(passed[rows:])


def halves(kernel, side, inputs, shapes, name):
    out = lambda a: pl.BlockSpec((*a.shape[:-1], a.shape[-1] // 2), lambda j, s: (0,) * (len(a.shape) - 1) + (j,))
    count = len(inputs)

    def copied(side_ref, *refs):
        sources, outs, held, sems = refs[:count], refs[count:-count - 1], refs[-count - 1 : -1], refs[-1]

        @pl.when(pl.program_id(0) == 0)
        def _():
            copies = [pltpu.make_async_copy(a, b, sems.at[i]) for i, (a, b) in enumerate(zip(sources, held))]
            for copy in copies:
                copy.start()
            for copy in copies:
                copy.wait()

        kernel(side_ref, *held, *outs)

    return pl.pallas_call(
        copied,
        grid_spec=pltpu.PrefetchScalarGridSpec(
            num_scalar_prefetch=1,
            grid=(2,),
            in_specs=[pl.BlockSpec(memory_space=pl.ANY)] * count,
            out_specs=[out(a) for a in shapes],
            scratch_shapes=[pltpu.VMEM(a.shape, a.dtype) for a in inputs] + [pltpu.SemaphoreType.DMA((count,))],
        ),
        out_shape=[jax.ShapeDtypeStruct(a.shape, BF16) for a in shapes],
        compiler_params=pltpu.CompilerParams(vmem_limit_bytes=VMEM),
        cost_estimate=pl.CostEstimate(flops=0, bytes_accessed=2_000_000, transcendentals=0),
        name=name,
    )(side, *inputs)


def body(prompt_k, prompt_v, resp_q, resp_k, resp_v, out_grad, lengths, rewards):
    slots = resp_q.shape[2]
    kv_heads = KVH // 2
    rows, width = prompt_k.shape[1:]
    pair = 2 * rows
    devices = 1
    for axis in ("x", "zh", "y", "zl", "core"):
        devices *= lax.axis_size(axis)

    keep, give, side = prep(prompt_k, prompt_v, lengths, rewards)
    got = step(give, "core", 1)
    mine = jnp.concatenate(
        [keep[:rows], got[:rows], keep[rows:pair], got[rows:pair], keep[pair : pair + 8], got[pair : pair + 8]], axis=0
    )

    tie = lax.optimization_barrier
    near_z = step(mine, "zl", 1)
    far = step(mine, "y", 2)
    below = step(mine, "y", 1)
    above = step(mine, "y", -1)
    packed = step(pack(side, resp_q, out_grad, resp_k, resp_v), "core", 1)
    near_z, packed = tie((near_z, packed))
    below_z = step(near_z, "y", 1)
    above_z = step(near_z, "y", -1)
    far_z = step(far, "zl", 1)
    blocks = (mine, near_z, above, above_z, below, below_z, far, far_z)

    tokens = sum(b[2 * pair + i : 2 * pair + i + 1, :HD].astype(F32) for b in blocks for i in (0, 8))
    tokens = jnp.broadcast_to(tokens, (8, HD))
    next_z = step(tokens, "zh", 1)
    tokens = tokens + next_z + step(tokens, "zh", -1)

    own_att, own_grad, for_sib, *parts = attention(
        side, blocks, resp_q, out_grad, resp_k, resp_v, packed, kv_heads
    )
    tokens, next_z, for_sib, *parts = tie((tokens, next_z, for_sib, *parts))
    p_own, p_near, p_above, p_below, p_far, p_far_z = parts
    height = p_far.shape[0]

    def added(*terms):
        return sum(t.astype(F32) for t in terms)

    from_z = step(p_far_z, "zl", 1)
    from_below = step(p_above, "y", 1)
    from_above = step(p_below, "y", -1)
    from_sib = step(for_sib, "core", 1)
    tokens = tokens + step(next_z, "zh", 1)
    from_z, from_below, from_above, from_sib, tokens = tie((from_z, from_below, from_above, from_sib, tokens))
    from_far = step(added(p_far, from_z).astype(BF16), "y", 2)
    from_near = step(added(p_near, from_below[height:], from_above[height:]).astype(BF16), "zl", 1)
    tokens = tokens + step(tokens, "x", 1) + step(tokens, "x", -1) + step(tokens, "x", 2)
    [attended] = halves(functools.partial(place_kernel, kv_heads), side, (own_att, from_sib), (resp_q,), "place")
    from_far, from_near, attended, tokens = tie((from_far, from_near, attended, tokens))
    total = added(p_own, from_below[:height], from_above[:height], from_far, from_near)
    pass_on = jnp.concatenate([total[rows:pair], total[pair + rows :]], axis=0).astype(BF16)
    passed = step(pass_on, "core", 1)
    grad_q, grad_rk, grad_rv, grad_pk, grad_pv = halves(
        functools.partial(finish_kernel, kv_heads, float(slots * devices)),
        side,
        (own_grad, from_sib, total, passed, tokens),
        (resp_q, resp_k, resp_v, prompt_k, prompt_v),
        "finish",
    )
    return attended, grad_q, grad_rk, grad_rv, grad_pk, grad_pv


def solution(mesh):
    parts = Mesh(mesh.devices.reshape(4, 4, 4, 2, 2), ("x", "zh", "y", "zl", "core"))
    group, member = ("x", "zh"), ("y", "zl", "core")
    rank3, rank4, rank2 = P(group, member, None), P(group, member, None, None), P(group, member)
    return jax.shard_map(
        body,
        mesh=parts,
        in_specs=(rank3, rank3, rank4, rank4, rank4, rank4, rank2, rank2),
        out_specs=(rank4, rank4, rank4, rank4, rank3, rank3),
        check_vma=False,
    )
```

time: 360 us -> 92.2 us (0.26)
  blocking collectives: 109 us -> 0 us
  matrix products: 95.4 us -> 0 us
  waiting for transfers between devices: 80.8 us -> 25.9 us
  local copies, waits for them, and re-layouts: 40 us -> 0.07 us
  starting transfers between devices: 0.11 us -> 32.9 us
  Pallas kernels: 0 us -> 30.5 us
  between operations: 16.7 us -> 2.31 us
  other arithmetic: 14.7 us -> 0.39 us
    psum x2 -> x0, blocking collectives: 109 us -> none  [the longest x1 81.4 us: body(): token_total = lax.psum(own_tokens, ('group', 'member'))]
    dot_general x48 -> x0, matrix products: 95.4 us -> none  [the longest x8 19.2 us: head_terms(): output = jnp.dot(probs_low, all_values, preferred_element_type=jnp.float32)]
    reduce_scatter x1 -> x0, waiting for transfers between devices: 79.4 us -> none  [body(): lax.psum_scatter(partial_term, 'member', scatter_dimension=0, tiled=True)]
    ppermute x0 -> x22, starting transfers between devices: none -> 32.9 us  [step(): lax.ppermute(values, axis, [(i, (i + by) % size) for i in range(size)])]
    pallas_call x0 -> x5, Pallas kernels: none -> 30.5 us  [the longest x1 21.2 us: attention(): pl.pallas_call(functools.partial(attention_kernel, float(HD) ** (-0.5)),...]
    ppermute x0 -> x22, waiting for transfers between devices: none -> 25.9 us  [step(): lax.ppermute(values, axis, [(i, (i + by) % size) for i in range(size)])]
    slice x8 -> x1, local copies, waits for them, and re-layouts: 10.2 us -> 0.01 us  [body(): total[rows:pair]]
    reshape x3 -> x0, local copies, waits for them, and re-layouts: 6.86 us -> none  [the longest x2 4.75 us: from_heads(): shaped = blocks.reshape(kv_heads, per_head, row_count, head_size)]
  transfers between devices with their start and end apart: 3 -> 22, of which waited for: 1 -> 7; matrix products, arithmetic and copies ran while one was open for 7% -> 0% of each run, Pallas kernels for 0% -> 28%
where the time goes in v2:
time: 92.2 us; the launch traced here: 92 us
  starting transfers between devices  32.9 us (36%)
  Pallas kernels  30.5 us (33%)
  waiting for transfers between devices  25.9 us (28%)
  between operations  2.31 us (3%)
    ppermute x22, starting transfers between devices, step(): lax.ppermute(values, axis, [(i, (i + by) % size) for i in range(size)])  32.9 us
    ppermute x22, waiting for transfers between devices, step(): lax.ppermute(values, axis, [(i, (i + by) % size) for i in range(size)])  25.9 us
    pallas_call x1, Pallas kernels, attention(): pl.pallas_call(functools.partial(attention_kernel, float(HD) ** (-0.5)),...  21.2 us
    pallas_call x2, Pallas kernels, halves(): pl.pallas_call(copied, grid_spec=pltpu.PrefetchScalarGridSpec(num_scalar_...  4.23 us
    pallas_call x1, Pallas kernels, pack(): pl.pallas_call(pack_kernel, in_specs=[pl.BlockSpec(memory_space=pltpu.SME...  3.22 us
  transfers between devices with their start and end apart: 22, of which 7 were waited for; matrix products, arithmetic and copies ran while one was open for 0% of the time, Pallas kernels for 28%

profile of v2, /device:TPU:1, one launch (start us, length us, event | category | flops | bytes accessed | tf_op | source)
XLA Modules:
  0.0 92.0 jit_solution(4813548607846123131)
XLA Ops:
  1.9 1.8 %prep.1 = (bf16[144,512]{1,0:T(8,128)(2,1)}, bf16[144,512]{1,0:T(8,128)(2,1)}, s32[1]{0:T(128)}) custom-call(bf16[1,64,1024]{2,1,0:T(8,128)(2,1)} %k_in.1, bf16[1,64,1024]{2,1,0:T(8,128)(2,1)} %v_in.1, s32[1,1]{1,0:T(1,128)S(6)} %copy.19.length_in, f32[1,1]{1,0:T(1,128)S(6)} %copy.20.reward_in), custom_call_target="tpu_custom_call" | custom-call | bytes 500000 | tf_op jit(solution)/shard_map/prep/pallas_call | solution.py:148
  3.7 3.3 %collective-permute-start = (bf16[144,512]{1,0:T(8,128)(2,1)}, bf16[144,512]{1,0:T(8,128)(2,1)S(1)}, u32[]{:S(2)}, u32[]{:S(2)}) collective-permute-start(bf16[144,512]{1,0:T(8,128)(2,1)} %get-tuple-element.44), channel_id=1, source_target_pairs={{0,1},{1,0},{2,3},{3,2},{4,5},{5,4},{6,7},{7,6},{8,9},{9,8},{10,11... | collective-permute-start | bytes 442376 | tf_op jit(solution)/shard_map/ppermute | solution.py:28
  7.0 0.0 copy-start.4
  7.0 0.0 copy-start
  7.0 0.0 copy-start.1
  7.0 0.0 copy-start.2
  7.0 0.0 copy-start.3
  7.1 3.2 %pack.1 = bf16[128,5120]{1,0:T(8,128)(2,1)} custom-call(s32[1]{0:T(128)} %get-tuple-element.45.side_ref, bf16[1,1,128,4096]{3,2,1,0:T(8,128)(2,1)} %refs_8_.1, bf16[1,1,128,4096]{3,2,1,0:T(8,128)(2,1)} %refs_9_.1, bf16[1,1,128,1024]{3,2,1,0:T(8,128)(2,1)} %refs_10_.1, bf16[1,1,128,1024]{3,2,1,0:T(8,128)(2,1)} %refs_11_.1), custom_call_target="tpu_custom_call" | custom-call | bytes 100000 | tf_op jit(solution)/shard_map/pack/pallas_call | solution.py:176
  10.3 0.1 collective-permute-start.2
  10.4 0.0 copy-done.4
  10.4 0.0 collective-permute-done
  10.5 1.3 %collective-permute-start.7 = (bf16[272,512]{1,0:T(8,128)(2,1)S(1)}, bf16[272,512]{1,0:T(8,128)(2,1)S(1)}, u32[]{:S(2)}, u32[]{:S(2)}) collective-permute-start(bf16[272,512]{1,0:T(8,128)(2,1)S(1)} %constant_dynamic-update-slice_fusion.refs_0_), channel_id=1, source_target_pairs={{0,8},{4,12},{8,0},{12,4},{1,9},{5,13},{9,1},{13,5},{2,10},{6,14},... | collective-permute-start | bytes 835592 | tf_op jit(solution)/shard_map/ppermute | solution.py:28
  11.7 1.6 %collective-permute-start.1 = (bf16[272,512]{1,0:T(8,128)(2,1)S(1)}, bf16[272,512]{1,0:T(8,128)(2,1)S(1)}, u32[]{:S(2)}, u32[]{:S(2)}) collective-permute-start(bf16[272,512]{1,0:T(8,128)(2,1)S(1)} %constant_dynamic-update-slice_fusion.refs_0_), channel_id=1, source_target_pairs={{0,2},{2,0},{1,3},{3,1},{4,6},{6,4},{5,7},{7,5},{8,10},{10,8},{9,1... | collective-permute-start | bytes 835592 | tf_op jit(solution)/shard_map/ppermute | solution.py:28
  13.4 0.4 collective-permute-start.5
  13.8 2.3 %collective-permute-start.3 = (bf16[272,512]{1,0:T(8,128)(2,1)S(1)}, bf16[272,512]{1,0:T(8,128)(2,1)S(1)}, u32[]{:S(2)}, u32[]{:S(2)}) collective-permute-start(bf16[272,512]{1,0:T(8,128)(2,1)S(1)} %constant_dynamic-update-slice_fusion.refs_0_), channel_id=1, source_target_pairs={{0,12},{4,0},{8,4},{12,8},{1,13},{5,1},{9,5},{13,9},{2,14},{6,2},{... | collective-permute-start | bytes 835592 | tf_op jit(solution)/shard_map/ppermute | solution.py:28
  16.1 3.8 %collective-permute-done.7.refs_6_ = bf16[272,512]{1,0:T(8,128)(2,1)S(1)} collective-permute-done((bf16[272,512]{1,0:T(8,128)(2,1)S(1)}, bf16[272,512]{1,0:T(8,128)(2,1)S(1)}, u32[]{:S(2)}, u32[]{:S(2)}) %collective-permute-start.7) | collective-permute-done | bytes 278560 | tf_op jit(solution)/shard_map/ppermute | solution.py:28
  19.9 0.0 collective-permute-start.8
  19.9 0.0 collective-permute-done.1.refs_1_
  19.9 0.0 collective-permute-done.2.refs_12_.refs_13_.refs_14_.refs_15_
  19.9 1.2 %collective-permute-start.6 = (bf16[272,512]{1,0:T(8,128)(2,1)S(1)}, bf16[272,512]{1,0:T(8,128)(2,1)S(1)}, u32[]{:S(2)}, u32[]{:S(2)}) collective-permute-start(bf16[272,512]{1,0:T(8,128)(2,1)S(1)} %collective-permute-done.1.refs_1_), channel_id=1, source_target_pairs={{0,4},{4,8},{8,12},{12,0},{1,5},{5,9},{9,13},{13,1},{2,6},{6,10},{... | collective-permute-start | bytes 835592 | tf_op jit(solution)/shard_map/ppermute | solution.py:28
  21.1 1.6 %collective-permute-start.4 = (bf16[272,512]{1,0:T(8,128)(2,1)S(1)}, bf16[272,512]{1,0:T(8,128)(2,1)S(1)}, u32[]{:S(2)}, u32[]{:S(2)}) collective-permute-start(bf16[272,512]{1,0:T(8,128)(2,1)S(1)} %collective-permute-done.1.refs_1_), channel_id=1, source_target_pairs={{0,12},{4,0},{8,4},{12,8},{1,13},{5,1},{9,5},{13,9},{2,14},{6,2},{... | collective-permute-start | bytes 835592 | tf_op jit(solution)/shard_map/ppermute | solution.py:28
  22.6 4.0 %collective-permute-done.5.refs_4_ = bf16[272,512]{1,0:T(8,128)(2,1)S(1)} collective-permute-done((bf16[272,512]{1,0:T(8,128)(2,1)S(1)}, bf16[272,512]{1,0:T(8,128)(2,1)S(1)}, u32[]{:S(2)}, u32[]{:S(2)}) %collective-permute-start.5) | collective-permute-done | bytes 278560 | tf_op jit(solution)/shard_map/ppermute | solution.py:28
  26.6 0.0 collective-permute-done.3.refs_2_
  26.6 0.0 collective-permute-done.8.refs_7_
  26.6 6.0 %collective-permute-done.6.refs_5_ = bf16[272,512]{1,0:T(8,128)(2,1)S(1)} collective-permute-done((bf16[272,512]{1,0:T(8,128)(2,1)S(1)}, bf16[272,512]{1,0:T(8,128)(2,1)S(1)}, u32[]{:S(2)}, u32[]{:S(2)}) %collective-permute-start.6) | collective-permute-done | bytes 278560 | tf_op jit(solution)/shard_map/ppermute | solution.py:28
  32.6 0.0 collective-permute-done.4.refs_3_
  32.6 3.9 %collective-permute-start.10 = (f32[8,128]{1,0:T(8,128)S(1)}, f32[8,128]{1,0:T(8,128)S(1)}, u32[]{:S(2)}, u32[]{:S(2)}) collective-permute-start(f32[8,128]{1,0:T(8,128)S(1)} %broadcast_in_dim.8), channel_id=1, source_target_pairs={{0,48},{16,0},{32,16},{48,32},{1,49},{17,1},{33,17},{49,33},{2,50}... | collective-permute-start | bytes 12296 | tf_op jit(solution)/shard_map/ppermute | solution.py:28
  36.5 0.0 collective-permute-start.9
  36.5 0.0 copy-done
  36.5 0.0 copy-done.1
  36.5 0.0 copy-done.2
  36.5 0.0 copy-done.3
  36.5 21.2 %attention.1 = (bf16[128,2048]{1,0:T(8,128)(2,1)S(1)}, bf16[128,3072]{1,0:T(8,128)(2,1)S(1)}, bf16[128,5120]{1,0:T(8,128)(2,1)S(1)}, f32[256,512]{1,0:T(8,128)S(...) custom-call(s32[1]{0:T(128)} %get-tuple-element.45.side_ref, ...), custom_call_target="tpu_custom_call" | custom-call | flops 14000000000 | bytes 12000000 | tf_op jit(solution)/shard_map/attention/pallas_call | solution.py:244
  57.8 0.0 collective-permute-done.10
  57.8 0.0 collective-permute-done.9
  57.8 1.7 %collective-permute-start.14 = (bf16[128,5120]{1,0:T(8,128)(2,1)S(1)}, bf16[128,5120]{1,0:T(8,128)(2,1)S(1)}, u32[]{:S(2)}, u32[]{:S(2)}) collective-permute-start(bf16[128,5120]{1,0:T(8,128)(2,1)S(1)} %get-tuple-element.59), channel_id=1, source_target_pairs={{0,1},{1,0},{2,3},{3,2},{4,5},{5,4},{6,7},{7,6},{8,9},{9,8},{10,11... | collective-permute-start | bytes 3932168 | tf_op jit(solution)/shard_map/ppermute | solution.py:28
  59.5 1.1 %collective-permute-start.12 = (bf16[512,512]{1,0:T(8,128)(2,1)S(1)}, bf16[512,512]{1,0:T(8,128)(2,1)S(1)}, u32[]{:S(2)}, u32[]{:S(2)}) collective-permute-start(bf16[512,512]{1,0:T(8,128)(2,1)S(1)} %get-tuple-element.57), channel_id=1, source_target_pairs={{0,4},{4,8},{8,12},{12,0},{1,5},{5,9},{9,13},{13,1},{2,6},{6,10},{... | collective-permute-start | bytes 1572872 | tf_op jit(solution)/shard_map/ppermute | solution.py:28
  60.6 1.6 %collective-permute-start.13 = (bf16[512,512]{1,0:T(8,128)(2,1)S(1)}, bf16[512,512]{1,0:T(8,128)(2,1)S(1)}, u32[]{:S(2)}, u32[]{:S(2)}) collective-permute-start(bf16[512,512]{1,0:T(8,128)(2,1)S(1)} %get-tuple-element.58), channel_id=1, source_target_pairs={{0,12},{4,0},{8,4},{12,8},{1,13},{5,1},{9,5},{13,9},{2,14},{6,2},{... | collective-permute-start | bytes 1572872 | tf_op jit(solution)/shard_map/ppermute | solution.py:28
  62.2 0.7 collective-permute-start.11
  62.9 1.7 %collective-permute-start.15 = (f32[8,128]{1,0:T(8,128)S(1)}, f32[8,128]{1,0:T(8,128)S(1)}, u32[]{:S(2)}, u32[]{:S(2)}) collective-permute-start(f32[8,128]{1,0:T(8,128)S(1)} %collective-permute-done.9), channel_id=1, source_target_pairs={{0,16},{16,32},{32,48},{48,0},{1,17},{17,33},{33,49},{49,1},{2,18}... | collective-permute-start | bytes 12296 | tf_op jit(solution)/shard_map/ppermute | solution.py:28
  64.7 7.7 %collective-permute-done.15 = f32[8,128]{1,0:T(8,128)S(1)} collective-permute-done((f32[8,128]{1,0:T(8,128)S(1)}, f32[8,128]{1,0:T(8,128)S(1)}, u32[]{:S(2)}, u32[]{:S(2)}) %collective-permute-start.15) | collective-permute-done | bytes 4128 | tf_op jit(solution)/shard_map/ppermute | solution.py:28
  72.4 0.0 collective-permute-done.11
  72.4 1.8 %collective-permute-done.12 = bf16[512,512]{1,0:T(8,128)(2,1)S(1)} collective-permute-done((bf16[512,512]{1,0:T(8,128)(2,1)S(1)}, bf16[512,512]{1,0:T(8,128)(2,1)S(1)}, u32[]{:S(2)}, u32[]{:S(2)}) %collective-permute-start.12) | collective-permute-done | bytes 524320 | tf_op jit(solution)/shard_map/ppermute | solution.py:28
  74.2 0.0 collective-permute-done.13
  74.2 0.0 collective-permute-done.14.refs_1_
  74.2 0.1 add_convert_fusion
  74.3 0.8 collective-permute-start.17
  75.1 0.1 add_convert_fusion.1
  75.2 2.1 %collective-permute-start.16 = (bf16[256,512]{1,0:T(8,128)(2,1)S(1)}, bf16[256,512]{1,0:T(8,128)(2,1)S(1)}, u32[]{:S(2)}, u32[]{:S(2)}) collective-permute-start(bf16[256,512]{1,0:T(8,128)(2,1)S(1)} %add_convert_fusion.1), channel_id=1, source_target_pairs={{0,8},{4,12},{8,0},{12,4},{1,9},{5,13},{9,1},{13,5},{2,10},{6,14},... | collective-permute-start | bytes 786440 | tf_op jit(solution)/shard_map/ppermute | solution.py:28
  77.3 2.7 %collective-permute-start.20 = (f32[8,128]{1,0:T(8,128)S(1)}, f32[8,128]{1,0:T(8,128)S(1)}, u32[]{:S(2)}, u32[]{:S(2)}) collective-permute-start(f32[8,128]{1,0:T(8,128)S(1)} %add.101), channel_id=1, source_target_pairs={{0,128},{64,192},{128,0},{192,64},{1,129},{65,193},{129,1},{193,65... | collective-permute-start | bytes 12296 | tf_op jit(solution)/shard_map/ppermute | solution.py:28
  80.0 0.9 collective-permute-start.19
  80.9 0.6 collective-permute-start.18
  81.5 1.7 %place.1 = bf16[1,1,128,4096]{3,2,1,0:T(8,128)(2,1)} custom-call(s32[1]{0:T(128)} %get-tuple-element.45.side_ref, bf16[128,2048]{1,0:T(8,128)(2,1)S(1)} %get-tuple-element.66.refs_0_, bf16[128,5120]{1,0:T(8,128)(2,1)S(1)} %collective-permute-done.14.refs_1_), custom_call_target="tpu_custom_call" | custom-call | bytes 2000000 | tf_op jit(solution)/shard_map/place/pallas_call | solution.py:326
  83.3 0.0 collective-permute-done.20
  83.3 0.0 collective-permute-done.19
  83.3 1.6 %collective-permute-done.18 = f32[8,128]{1,0:T(8,128)S(1)} collective-permute-done((f32[8,128]{1,0:T(8,128)S(1)}, f32[8,128]{1,0:T(8,128)S(1)}, u32[]{:S(2)}, u32[]{:S(2)}) %collective-permute-start.18) | collective-permute-done | bytes 4128 | tf_op jit(solution)/shard_map/ppermute | solution.py:28
  84.9 0.0 collective-permute-done.17
  84.9 0.0 collective-permute-done.16
  84.9 0.2 fusion.16
  85.1 3.2 %collective-permute-start.21 = (bf16[128,512]{1,0:T(8,128)(2,1)S(1)}, bf16[128,512]{1,0:T(8,128)(2,1)S(1)}, u32[]{:S(2)}, u32[]{:S(2)}) collective-permute-start(bf16[128,512]{1,0:T(8,128)(2,1)S(1)} %pad_maximum_fusion), channel_id=1, source_target_pairs={{0,1},{1,0},{2,3},{3,2},{4,5},{5,4},{6,7},{7,6},{8,9},{9,8},{10,11... | collective-permute-start | bytes 393224 | tf_op jit(solution)/shard_map/ppermute | solution.py:28
  88.4 1.0 %collective-permute-done.21.refs_3_ = bf16[128,512]{1,0:T(8,128)(2,1)S(1)} collective-permute-done((bf16[128,512]{1,0:T(8,128)(2,1)S(1)}, bf16[128,512]{1,0:T(8,128)(2,1)S(1)}, u32[]{:S(2)}, u32[]{:S(2)}) %collective-permute-start.21) | collective-permute-done | bytes 131104 | tf_op jit(solution)/shard_map/ppermute | solution.py:28
  89.3 2.5 %finish.1 = (bf16[1,1,128,4096]{3,2,1,0:T(8,128)(2,1)}, bf16[1,1,128,1024]{3,2,1,0:T(8,128)(2,1)}, bf16[1,1,128,1024]{3,2,1,0:T(8,128)(2,1)}, bf16[1,64,1024]{2,1,0:T(8,128)(2,1)}, bf16[1,64,1024]{2,1,0:T(8,128)(2,1)}) custom-call(s32[1]{0:T(128)} %get-tuple-element.45.side_ref, bf16[128,3072]{1,0:T(8,128)(2,1)S(1)} %get-tuple-element.70.refs_0_, ...), custom_call_target="tpu_custom_call" | custom-call | bytes 2000000 | tf_op jit(solution)/shard_map/finish/pallas_call | solution.py:326
  (13 shorter events, 0.1 us)
Async XLA Ops:
  3.7 6.7 %collective-permute-start = (bf16[144,512]{1,0:T(8,128)(2,1)}, bf16[144,512]{1,0:T(8,128)(2,1)S(1)}, u32[]{:S(2)}, u32[]{:S(2)}) collective-permute-start(bf16[144,512]{1,0:T(8,128)(2,1)} %get-tuple-element.44), channel_id=1, source_target_pairs={{0,1},{1,0},{2,3},{3,2},{4,5},{5,4},{6,7},{7,6},{8,9},{9,8},{10,11... | collective-permute-start | bytes 442376 | tf_op jit(solution)/shard_map/ppermute | solution.py:28
  7.0 3.4 %copy-start.4 = (bf16[144,512]{1,0:T(8,128)(2,1)S(1)}, bf16[144,512]{1,0:T(8,128)(2,1)}, u32[]{:S(2)}) copy-start(bf16[144,512]{1,0:T(8,128)(2,1)} %get-tuple-element.43) | copy-start | bytes 442372
  7.0 29.5 %copy-start = (bf16[1,1,128,4096]{3,2,1,0:T(8,128)(2,1)S(1)}, bf16[1,1,128,4096]{3,2,1,0:T(8,128)(2,1)}, u32[]{:S(2)}) copy-start(bf16[1,1,128,4096]{3,2,1,0:T(8,128)(2,1)} %refs_8_.1) | copy-start | bytes 3145732
  7.0 29.5 %copy-start.1 = (bf16[1,1,128,4096]{3,2,1,0:T(8,128)(2,1)S(1)}, bf16[1,1,128,4096]{3,2,1,0:T(8,128)(2,1)}, u32[]{:S(2)}) copy-start(bf16[1,1,128,4096]{3,2,1,0:T(8,128)(2,1)} %refs_9_.1) | copy-start | bytes 3145732
  7.0 29.5 %copy-start.2 = (bf16[1,1,128,1024]{3,2,1,0:T(8,128)(2,1)S(1)}, bf16[1,1,128,1024]{3,2,1,0:T(8,128)(2,1)}, u32[]{:S(2)}) copy-start(bf16[1,1,128,1024]{3,2,1,0:T(8,128)(2,1)} %refs_10_.1) | copy-start | bytes 786436
  7.0 29.5 %copy-start.3 = (bf16[1,1,128,1024]{3,2,1,0:T(8,128)(2,1)S(1)}, bf16[1,1,128,1024]{3,2,1,0:T(8,128)(2,1)}, u32[]{:S(2)}) copy-start(bf16[1,1,128,1024]{3,2,1,0:T(8,128)(2,1)} %refs_11_.1) | copy-start | bytes 786436
  10.3 9.6 %collective-permute-start.2 = (bf16[128,5120]{1,0:T(8,128)(2,1)}, bf16[128,5120]{1,0:T(8,128)(2,1)S(1)}, u32[]{:S(2)}, u32[]{:S(2)}) collective-permute-start(bf16[128,5120]{1,0:T(8,128)(2,1)} %pack.1), channel_id=1, source_target_pairs={{0,1},{1,0},{2,3},{3,2},{4,5},{5,4},{6,7},{7,6},{8,9},{9,8},{10,11... | collective-permute-start | bytes 3932168 | tf_op jit(solution)/shard_map/ppermute | solution.py:28
  10.5 9.4 %collective-permute-start.7 = (bf16[272,512]{1,0:T(8,128)(2,1)S(1)}, bf16[272,512]{1,0:T(8,128)(2,1)S(1)}, u32[]{:S(2)}, u32[]{:S(2)}) collective-permute-start(bf16[272,512]{1,0:T(8,128)(2,1)S(1)} %constant_dynamic-update-slice_fusion.refs_0_), channel_id=1, source_target_pairs={{0,8},{4,12},{8,0},{12,4},{1,9},{5,13},{9,1},{13,5},{2,10},{6,14},... | collective-permute-start | bytes 835592 | tf_op jit(solution)/shard_map/ppermute | solution.py:28
  11.7 8.1 %collective-permute-start.1 = (bf16[272,512]{1,0:T(8,128)(2,1)S(1)}, bf16[272,512]{1,0:T(8,128)(2,1)S(1)}, u32[]{:S(2)}, u32[]{:S(2)}) collective-permute-start(bf16[272,512]{1,0:T(8,128)(2,1)S(1)} %constant_dynamic-update-slice_fusion.refs_0_), channel_id=1, source_target_pairs={{0,2},{2,0},{1,3},{3,1},{4,6},{6,4},{5,7},{7,5},{8,10},{10,8},{9,1... | collective-permute-start | bytes 835592 | tf_op jit(solution)/shard_map/ppermute | solution.py:28
  13.4 13.2 %collective-permute-start.5 = (bf16[272,512]{1,0:T(8,128)(2,1)S(1)}, bf16[272,512]{1,0:T(8,128)(2,1)S(1)}, u32[]{:S(2)}, u32[]{:S(2)}) collective-permute-start(bf16[272,512]{1,0:T(8,128)(2,1)S(1)} %constant_dynamic-update-slice_fusion.refs_0_), channel_id=1, source_target_pairs={{0,4},{4,8},{8,12},{12,0},{1,5},{5,9},{9,13},{13,1},{2,6},{6,10},{... | collective-permute-start | bytes 835592 | tf_op jit(solution)/shard_map/ppermute | solution.py:28
  13.8 12.8 %collective-permute-start.3 = (bf16[272,512]{1,0:T(8,128)(2,1)S(1)}, bf16[272,512]{1,0:T(8,128)(2,1)S(1)}, u32[]{:S(2)}, u32[]{:S(2)}) collective-permute-start(bf16[272,512]{1,0:T(8,128)(2,1)S(1)} %constant_dynamic-update-slice_fusion.refs_0_), channel_id=1, source_target_pairs={{0,12},{4,0},{8,4},{12,8},{1,13},{5,1},{9,5},{13,9},{2,14},{6,2},{... | collective-permute-start | bytes 835592 | tf_op jit(solution)/shard_map/ppermute | solution.py:28
  19.9 6.8 %collective-permute-start.8 = (bf16[272,512]{1,0:T(8,128)(2,1)S(1)}, bf16[272,512]{1,0:T(8,128)(2,1)S(1)}, u32[]{:S(2)}, u32[]{:S(2)}) collective-permute-start(bf16[272,512]{1,0:T(8,128)(2,1)S(1)} %collective-permute-done.7.refs_6_), channel_id=1, source_target_pairs={{0,2},{2,0},{1,3},{3,1},{4,6},{6,4},{5,7},{7,5},{8,10},{10,8},{9,1... | collective-permute-start | bytes 835592 | tf_op jit(solution)/shard_map/ppermute | solution.py:28
  19.9 12.7 %collective-permute-start.6 = (bf16[272,512]{1,0:T(8,128)(2,1)S(1)}, bf16[272,512]{1,0:T(8,128)(2,1)S(1)}, u32[]{:S(2)}, u32[]{:S(2)}) collective-permute-start(bf16[272,512]{1,0:T(8,128)(2,1)S(1)} %collective-permute-done.1.refs_1_), channel_id=1, source_target_pairs={{0,4},{4,8},{8,12},{12,0},{1,5},{5,9},{9,13},{13,1},{2,6},{6,10},{... | collective-permute-start | bytes 835592 | tf_op jit(solution)/shard_map/ppermute | solution.py:28
  21.1 11.5 %collective-permute-start.4 = (bf16[272,512]{1,0:T(8,128)(2,1)S(1)}, bf16[272,512]{1,0:T(8,128)(2,1)S(1)}, u32[]{:S(2)}, u32[]{:S(2)}) collective-permute-start(bf16[272,512]{1,0:T(8,128)(2,1)S(1)} %collective-permute-done.1.refs_1_), channel_id=1, source_target_pairs={{0,12},{4,0},{8,4},{12,8},{1,13},{5,1},{9,5},{13,9},{2,14},{6,2},{... | collective-permute-start | bytes 835592 | tf_op jit(solution)/shard_map/ppermute | solution.py:28
  32.6 25.2 %collective-permute-start.10 = (f32[8,128]{1,0:T(8,128)S(1)}, f32[8,128]{1,0:T(8,128)S(1)}, u32[]{:S(2)}, u32[]{:S(2)}) collective-permute-start(f32[8,128]{1,0:T(8,128)S(1)} %broadcast_in_dim.8), channel_id=1, source_target_pairs={{0,48},{16,0},{32,16},{48,32},{1,49},{17,1},{33,17},{49,33},{2,50}... | collective-permute-start | bytes 12296 | tf_op jit(solution)/shard_map/ppermute | solution.py:28
  36.5 21.3 %collective-permute-start.9 = (f32[8,128]{1,0:T(8,128)S(1)}, f32[8,128]{1,0:T(8,128)S(1)}, u32[]{:S(2)}, u32[]{:S(2)}) collective-permute-start(f32[8,128]{1,0:T(8,128)S(1)} %broadcast_in_dim.8), channel_id=1, source_target_pairs={{0,16},{16,32},{32,48},{48,0},{1,17},{17,33},{33,49},{49,1},{2,18}... | collective-permute-start | bytes 12296 | tf_op jit(solution)/shard_map/ppermute | solution.py:28
  57.8 16.4 %collective-permute-start.14 = (bf16[128,5120]{1,0:T(8,128)(2,1)S(1)}, bf16[128,5120]{1,0:T(8,128)(2,1)S(1)}, u32[]{:S(2)}, u32[]{:S(2)}) collective-permute-start(bf16[128,5120]{1,0:T(8,128)(2,1)S(1)} %get-tuple-element.59), channel_id=1, source_target_pairs={{0,1},{1,0},{2,3},{3,2},{4,5},{5,4},{6,7},{7,6},{8,9},{9,8},{10,11... | collective-permute-start | bytes 3932168 | tf_op jit(solution)/shard_map/ppermute | solution.py:28
  59.5 14.7 %collective-permute-start.12 = (bf16[512,512]{1,0:T(8,128)(2,1)S(1)}, bf16[512,512]{1,0:T(8,128)(2,1)S(1)}, u32[]{:S(2)}, u32[]{:S(2)}) collective-permute-start(bf16[512,512]{1,0:T(8,128)(2,1)S(1)} %get-tuple-element.57), channel_id=1, source_target_pairs={{0,4},{4,8},{8,12},{12,0},{1,5},{5,9},{9,13},{13,1},{2,6},{6,10},{... | collective-permute-start | bytes 1572872 | tf_op jit(solution)/shard_map/ppermute | solution.py:28
  60.6 13.6 %collective-permute-start.13 = (bf16[512,512]{1,0:T(8,128)(2,1)S(1)}, bf16[512,512]{1,0:T(8,128)(2,1)S(1)}, u32[]{:S(2)}, u32[]{:S(2)}) collective-permute-start(bf16[512,512]{1,0:T(8,128)(2,1)S(1)} %get-tuple-element.58), channel_id=1, source_target_pairs={{0,12},{4,0},{8,4},{12,8},{1,13},{5,1},{9,5},{13,9},{2,14},{6,2},{... | collective-permute-start | bytes 1572872 | tf_op jit(solution)/shard_map/ppermute | solution.py:28
  62.2 10.2 %collective-permute-start.11 = (bf16[256,512]{1,0:T(8,128)(2,1)S(1)}, bf16[256,512]{1,0:T(8,128)(2,1)S(1)}, u32[]{:S(2)}, u32[]{:S(2)}) collective-permute-start(bf16[256,512]{1,0:T(8,128)(2,1)S(1)} %get-tuple-element.56), channel_id=1, source_target_pairs={{0,2},{2,0},{1,3},{3,1},{4,6},{6,4},{5,7},{7,5},{8,10},{10,8},{9,1... | collective-permute-start | bytes 786440 | tf_op jit(solution)/shard_map/ppermute | solution.py:28
  62.9 9.5 %collective-permute-start.15 = (f32[8,128]{1,0:T(8,128)S(1)}, f32[8,128]{1,0:T(8,128)S(1)}, u32[]{:S(2)}, u32[]{:S(2)}) collective-permute-start(f32[8,128]{1,0:T(8,128)S(1)} %collective-permute-done.9), channel_id=1, source_target_pairs={{0,16},{16,32},{32,48},{48,0},{1,17},{17,33},{33,49},{49,1},{2,18}... | collective-permute-start | bytes 12296 | tf_op jit(solution)/shard_map/ppermute | solution.py:28
  74.3 10.6 %collective-permute-start.17 = (bf16[256,512]{1,0:T(8,128)(2,1)S(1)}, bf16[256,512]{1,0:T(8,128)(2,1)S(1)}, u32[]{:S(2)}, u32[]{:S(2)}) collective-permute-start(bf16[256,512]{1,0:T(8,128)(2,1)S(1)} %add_convert_fusion), channel_id=1, source_target_pairs={{0,2},{2,0},{1,3},{3,1},{4,6},{6,4},{5,7},{7,5},{8,10},{10,8},{9,1... | collective-permute-start | bytes 786440 | tf_op jit(solution)/shard_map/ppermute | solution.py:28
  75.2 9.7 %collective-permute-start.16 = (bf16[256,512]{1,0:T(8,128)(2,1)S(1)}, bf16[256,512]{1,0:T(8,128)(2,1)S(1)}, u32[]{:S(2)}, u32[]{:S(2)}) collective-permute-start(bf16[256,512]{1,0:T(8,128)(2,1)S(1)} %add_convert_fusion.1), channel_id=1, source_target_pairs={{0,8},{4,12},{8,0},{12,4},{1,9},{5,13},{9,1},{13,5},{2,10},{6,14},... | collective-permute-start | bytes 786440 | tf_op jit(solution)/shard_map/ppermute | solution.py:28
  77.3 6.0 %collective-permute-start.20 = (f32[8,128]{1,0:T(8,128)S(1)}, f32[8,128]{1,0:T(8,128)S(1)}, u32[]{:S(2)}, u32[]{:S(2)}) collective-permute-start(f32[8,128]{1,0:T(8,128)S(1)} %add.101), channel_id=1, source_target_pairs={{0,128},{64,192},{128,0},{192,64},{1,129},{65,193},{129,1},{193,65... | collective-permute-start | bytes 12296 | tf_op jit(solution)/shard_map/ppermute | solution.py:28
  80.0 3.2 %collective-permute-start.19 = (f32[8,128]{1,0:T(8,128)S(1)}, f32[8,128]{1,0:T(8,128)S(1)}, u32[]{:S(2)}, u32[]{:S(2)}) collective-permute-start(f32[8,128]{1,0:T(8,128)S(1)} %add.101), channel_id=1, source_target_pairs={{0,192},{64,0},{128,64},{192,128},{1,193},{65,1},{129,65},{193,129... | collective-permute-start | bytes 12296 | tf_op jit(solution)/shard_map/ppermute | solution.py:28
  80.9 4.0 %collective-permute-start.18 = (f32[8,128]{1,0:T(8,128)S(1)}, f32[8,128]{1,0:T(8,128)S(1)}, u32[]{:S(2)}, u32[]{:S(2)}) collective-permute-start(f32[8,128]{1,0:T(8,128)S(1)} %add.101), channel_id=1, source_target_pairs={{0,64},{64,128},{128,192},{192,0},{1,65},{65,129},{129,193},{193,1... | collective-permute-start | bytes 12296 | tf_op jit(solution)/shard_map/ppermute | solution.py:28
  85.1 4.2 %collective-permute-start.21 = (bf16[128,512]{1,0:T(8,128)(2,1)S(1)}, bf16[128,512]{1,0:T(8,128)(2,1)S(1)}, u32[]{:S(2)}, u32[]{:S(2)}) collective-permute-start(bf16[128,512]{1,0:T(8,128)(2,1)S(1)} %pad_maximum_fusion), channel_id=1, source_target_pairs={{0,1},{1,0},{2,3},{3,2},{4,5},{5,4},{6,7},{7,6},{8,9},{9,8},{10,11... | collective-permute-start | bytes 393224 | tf_op jit(solution)/shard_map/ppermute | solution.py:28

commit v3 on v2

--- a/solution.py
+++ b/solution.py
@@ -26,6 +26,12 @@
 def step(values, axis, by):
     size = lax.axis_size(axis)
     return lax.ppermute(values, axis, [(i, (i + by) % size) for i in range(size)])
+
+
+def swap(values, x, zh):
+    rows, columns = lax.axis_size("x"), lax.axis_size("zh")
+    pairs = [(i * columns + j, (i ^ x) * columns + (j ^ zh)) for i in range(rows) for j in range(columns)]
+    return lax.ppermute(values, ("x", "zh"), pairs)
 
 
 def heads_to_rows(wide):
@@ -185,12 +191,11 @@
 
 
 def attention_kernel(scale, side_ref, *refs):
-    blocks, parts = refs[:8], refs[19:25]
+    blocks, parts = refs[:8], refs[19:27]
     q_own, g_own, k_own, v_own, q_sib, g_sib, k_sib, v_sib, own_att, own_grad, sib_out = refs[8:19]
-    k_scr, v_scr, kt_scr, vt_scr, e_scr, p_scr, d_scr, q_all, c_all = refs[25:]
+    k_scr, v_scr, kt_scr, vt_scr, e_scr, p_scr, d_scr, q_all, c_all = refs[27:]
     slots, wide = q_own.shape[2:]
     rows = (blocks[0].shape[0] - 16) // 2
-    parts = [(part, at) for part in parts for at in range(0, part.shape[0], 2 * rows)]
     prompt_len = len(blocks) * rows
     keys = [block[0:rows] for block in blocks]
     values = [block[rows : 2 * rows] for block in blocks]
@@ -222,10 +227,10 @@
     turns(run(a, "D"), run(b, "O"))
     turns(run(a, "G"), run(b, "D"))
     turns(run(b, "G"))
-    for i, (part, at) in enumerate(parts):
+    for i, part in enumerate(parts):
         here = slice(i * rows, (i + 1) * rows)
-        part[at : at + rows] = (dot(d_scr[here], q_all[...]) * scale).astype(part.dtype)
-        part[at + rows : at + 2 * rows] = dot(p_scr[here], c_all[...]).astype(part.dtype)
+        part[0:rows] = (dot(d_scr[here], q_all[...]) * scale).astype(part.dtype)
+        part[rows:] = dot(p_scr[here], c_all[...]).astype(part.dtype)
 
 
 def attention(side, blocks, resp_q, out_grad, resp_k, resp_v, packed, kv_heads):
@@ -237,8 +242,7 @@
     widths = (wide, wide + 2 * HD, 2 * wide + 2 * HD)
     results = [jax.ShapeDtypeStruct((slots, kv_heads * w), BF16) for w in widths]
     height = blocks[0].shape[0] - 16
-    heights = (height, height, 2 * height, 2 * height, height, height)
-    parts = [jax.ShapeDtypeStruct((n, kv_heads * HD), BF16 if i else F32) for i, n in enumerate(heights)]
+    parts = [jax.ShapeDtypeStruct((height, kv_heads * HD), BF16 if i else F32) for i in range(len(blocks))]
     keys = len(blocks) * height // 2 + slots
     rows = wide // HD * slots
     return pl.pallas_call(
@@ -249,7 +253,7 @@
             in_specs=[column(b.shape[0], HD) for b in blocks]
             + [own(wide), own(wide), own(HD), own(HD)]
             + [theirs(wide, 0), theirs(wide, 1), theirs(HD, 2 * wide // HD), theirs(HD, 2 * wide // HD + 1)],
-            out_specs=[column(slots, w) for w in widths] + [column(n, HD) for n in heights],
+            out_specs=[column(slots, w) for w in widths] + [column(height, HD)] * len(parts),
             scratch_shapes=[pltpu.VMEM((2, keys, HD), BF16)] * 2
             + [pltpu.VMEM((2, HD, keys), BF16)] * 2
             + [pltpu.VMEM((2, keys, rows), F32)]
@@ -368,31 +372,35 @@
 
     tokens = sum(b[2 * pair + i : 2 * pair + i + 1, :HD].astype(F32) for b in blocks for i in (0, 8))
     tokens = jnp.broadcast_to(tokens, (8, HD))
-    next_z = step(tokens, "zh", 1)
-    tokens = tokens + next_z + step(tokens, "zh", -1)
+    tokens = tokens + swap(tokens, 1, 0) + swap(tokens, 0, 1) + swap(tokens, 1, 1)
 
     own_att, own_grad, for_sib, *parts = attention(
         side, blocks, resp_q, out_grad, resp_k, resp_v, packed, kv_heads
     )
-    tokens, next_z, for_sib, *parts = tie((tokens, next_z, for_sib, *parts))
-    p_own, p_near, p_above, p_below, p_far, p_far_z = parts
-    height = p_far.shape[0]
+    tokens, for_sib, *parts = tie((tokens, for_sib, *parts))
+    p_own, p_near, p_above, p_above_z, p_below, p_below_z, p_far, p_far_z = parts
 
     def added(*terms):
         return sum(t.astype(F32) for t in terms)
 
     from_z = step(p_far_z, "zl", 1)
+    from_below_z = step(p_above_z, "y", 1)
+    from_above_z = step(p_below_z, "y", -1)
+    from_sib = step(for_sib, "core", 1)
+    tokens = tokens + swap(tokens, 3, 0)
+    from_z, from_below_z, from_above_z, from_sib, tokens, p_above, p_below = tie(
+        (from_z, from_below_z, from_above_z, from_sib, tokens, p_above, p_below)
+    )
     from_below = step(p_above, "y", 1)
     from_above = step(p_below, "y", -1)
-    from_sib = step(for_sib, "core", 1)
-    tokens = tokens + step(next_z, "zh", 1)
-    from_z, from_below, from_above, from_sib, tokens = tie((from_z, from_below, from_above, from_sib, tokens))
     from_far = step(added(p_far, from_z).astype(BF16), "y", 2)
-    from_near = step(added(p_near, from_below[height:], from_above[height:]).astype(BF16), "zl", 1)
-    tokens = tokens + step(tokens, "x", 1) + step(tokens, "x", -1) + step(tokens, "x", 2)
+    from_near = step(added(p_near, from_below_z, from_above_z).astype(BF16), "zl", 1)
+    tokens = tokens + swap(tokens, 0, 3)
     [attended] = halves(functools.partial(place_kernel, kv_heads), side, (own_att, from_sib), (resp_q,), "place")
-    from_far, from_near, attended, tokens = tie((from_far, from_near, attended, tokens))
-    total = added(p_own, from_below[:height], from_above[:height], from_far, from_near)
+    from_far, from_near, from_below, from_above, attended, tokens = tie(
+        (from_far, from_near, from_below, from_above, attended, tokens)
+    )
+    total = added(p_own, from_below, from_above, from_far, from_near)
     pass_on = jnp.concatenate([total[rows:pair], total[pair + rows :]], axis=0).astype(BF16)
     passed = step(pass_on, "core", 1)
     grad_q, grad_rk, grad_rv, grad_pk, grad_pv = halves(

time: 92.2 us -> 89.8 us (0.974)
  waiting for transfers between devices: 25.9 us -> 22.5 us
    ppermute x0 -> x5, starting transfers between devices: none -> 11.3 us  [swap(): return lax.ppermute(values, ('x', 'zh'), pairs)]
    ppermute x22 -> x18, starting transfers between devices: 32.9 us -> 22.2 us  [step(): lax.ppermute(values, axis, [(i, (i + by) % size) for i in range(size)])]
    ppermute x22 -> x18, waiting for transfers between devices: 25.9 us -> 21 us  [step(): lax.ppermute(values, axis, [(i, (i + by) % size) for i in range(size)])]
    ppermute x0 -> x5, waiting for transfers between devices: none -> 1.49 us  [swap(): return lax.ppermute(values, ('x', 'zh'), pairs)]
  transfers between devices with their start and end apart: 22 -> 23, of which waited for: 7 -> 8; matrix products, arithmetic and copies ran while one was open for 0% -> 0% of each run, Pallas kernels for 28% -> 29%
where the time goes in v3:
time: 89.8 us; the launch traced here: 89.6 us
  starting transfers between devices  33.6 us (37%)
  Pallas kernels  30.8 us (34%)
  waiting for transfers between devices  22.5 us (25%)
  between operations  2.31 us (3%)
    ppermute x18, starting transfers between devices, step(): lax.ppermute(values, axis, [(i, (i + by) % size) for i in range(size)])  22.2 us
    pallas_call x1, Pallas kernels, attention(): pl.pallas_call(functools.partial(attention_kernel, float(HD) ** (-0.5)),...  21.3 us
    ppermute x18, waiting for transfers between devices, step(): lax.ppermute(values, axis, [(i, (i + by) % size) for i in range(size)])  21 us
    ppermute x5, starting transfers between devices, swap(): return lax.ppermute(values, ('x', 'zh'), pairs)  11.3 us
    pallas_call x2, Pallas kernels, halves(): pl.pallas_call(copied, grid_spec=pltpu.PrefetchScalarGridSpec(num_scalar_...  4.46 us
    pallas_call x1, Pallas kernels, pack(): pl.pallas_call(pack_kernel, in_specs=[pl.BlockSpec(memory_space=pltpu.SME...  3.21 us
  transfers between devices with their start and end apart: 23, of which 8 were waited for; matrix products, arithmetic and copies ran while one was open for 0% of the time, Pallas kernels for 29%

profile of v3, /device:TPU:1, one launch (start us, length us, event | category | flops | bytes accessed | tf_op | source)
XLA Modules:
  0.0 89.6 jit_solution(177495540657277345)
XLA Ops:
  1.9 1.8 %prep.1 = (bf16[144,512]{1,0:T(8,128)(2,1)}, bf16[144,512]{1,0:T(8,128)(2,1)}, s32[1]{0:T(128)}) custom-call(bf16[1,64,1024]{2,1,0:T(8,128)(2,1)} %k_in.1, bf16[1,64,1024]{2,1,0:T(8,128)(2,1)} %v_in.1, s32[1,1]{1,0:T(1,128)S(6)} %copy.19.length_in, f32[1,1]{1,0:T(1,128)S(6)} %copy.20.reward_in), custom_call_target="tpu_custom_call" | custom-call | bytes 500000 | tf_op jit(solution)/shard_map/prep/pallas_call | solution.py:154
  3.7 3.3 %collective-permute-start = (bf16[144,512]{1,0:T(8,128)(2,1)}, bf16[144,512]{1,0:T(8,128)(2,1)S(1)}, u32[]{:S(2)}, u32[]{:S(2)}) collective-permute-start(bf16[144,512]{1,0:T(8,128)(2,1)} %get-tuple-element.51), channel_id=1, source_target_pairs={{0,1},{1,0},{2,3},{3,2},{4,5},{5,4},{6,7},{7,6},{8,9},{9,8},{10,11... | collective-permute-start | bytes 442376 | tf_op jit(solution)/shard_map/ppermute | solution.py:28
  7.0 0.0 copy-start.4
  7.0 0.0 copy-start
  7.0 0.0 copy-start.1
  7.0 0.0 copy-start.2
  7.0 0.0 copy-start.3
  7.1 3.2 %pack.1 = bf16[128,5120]{1,0:T(8,128)(2,1)} custom-call(s32[1]{0:T(128)} %get-tuple-element.52.side_ref, bf16[1,1,128,4096]{3,2,1,0:T(8,128)(2,1)} %refs_8_.1, bf16[1,1,128,4096]{3,2,1,0:T(8,128)(2,1)} %refs_9_.1, bf16[1,1,128,1024]{3,2,1,0:T(8,128)(2,1)} %refs_10_.1, bf16[1,1,128,1024]{3,2,1,0:T(8,128)(2,1)} %refs_11_.1), custom_call_target="tpu_custom_call" | custom-call | bytes 100000 | tf_op jit(solution)/shard_map/pack/pallas_call | solution.py:182
  10.3 0.1 collective-permute-start.2
  10.4 0.0 copy-done.4
  10.4 0.0 collective-permute-done
  10.5 1.3 %collective-permute-start.7 = (bf16[272,512]{1,0:T(8,128)(2,1)S(1)}, bf16[272,512]{1,0:T(8,128)(2,1)S(1)}, u32[]{:S(2)}, u32[]{:S(2)}) collective-permute-start(bf16[272,512]{1,0:T(8,128)(2,1)S(1)} %constant_dynamic-update-slice_fusion.refs_0_), channel_id=1, source_target_pairs={{0,8},{4,12},{8,0},{12,4},{1,9},{5,13},{9,1},{13,5},{2,10},{6,14},... | collective-permute-start | bytes 835592 | tf_op jit(solution)/shard_map/ppermute | solution.py:28
  11.8 1.6 %collective-permute-start.1 = (bf16[272,512]{1,0:T(8,128)(2,1)S(1)}, bf16[272,512]{1,0:T(8,128)(2,1)S(1)}, u32[]{:S(2)}, u32[]{:S(2)}) collective-permute-start(bf16[272,512]{1,0:T(8,128)(2,1)S(1)} %constant_dynamic-update-slice_fusion.refs_0_), channel_id=1, source_target_pairs={{0,2},{2,0},{1,3},{3,1},{4,6},{6,4},{5,7},{7,5},{8,10},{10,8},{9,1... | collective-permute-start | bytes 835592 | tf_op jit(solution)/shard_map/ppermute | solution.py:28
  13.4 0.4 collective-permute-start.5
  13.8 2.3 %collective-permute-start.3 = (bf16[272,512]{1,0:T(8,128)(2,1)S(1)}, bf16[272,512]{1,0:T(8,128)(2,1)S(1)}, u32[]{:S(2)}, u32[]{:S(2)}) collective-permute-start(bf16[272,512]{1,0:T(8,128)(2,1)S(1)} %constant_dynamic-update-slice_fusion.refs_0_), channel_id=1, source_target_pairs={{0,12},{4,0},{8,4},{12,8},{1,13},{5,1},{9,5},{13,9},{2,14},{6,2},{... | collective-permute-start | bytes 835592 | tf_op jit(solution)/shard_map/ppermute | solution.py:28
  16.1 3.8 %collective-permute-done.7.refs_6_ = bf16[272,512]{1,0:T(8,128)(2,1)S(1)} collective-permute-done((bf16[272,512]{1,0:T(8,128)(2,1)S(1)}, bf16[272,512]{1,0:T(8,128)(2,1)S(1)}, u32[]{:S(2)}, u32[]{:S(2)}) %collective-permute-start.7) | collective-permute-done | bytes 278560 | tf_op jit(solution)/shard_map/ppermute | solution.py:28
  19.9 0.0 collective-permute-start.8
  19.9 0.0 collective-permute-done.1.refs_1_
  19.9 0.0 collective-permute-done.2.refs_12_.refs_13_.refs_14_.refs_15_
  19.9 1.2 %collective-permute-start.6 = (bf16[272,512]{1,0:T(8,128)(2,1)S(1)}, bf16[272,512]{1,0:T(8,128)(2,1)S(1)}, u32[]{:S(2)}, u32[]{:S(2)}) collective-permute-start(bf16[272,512]{1,0:T(8,128)(2,1)S(1)} %collective-permute-done.1.refs_1_), channel_id=1, source_target_pairs={{0,4},{4,8},{8,12},{12,0},{1,5},{5,9},{9,13},{13,1},{2,6},{6,10},{... | collective-permute-start | bytes 835592 | tf_op jit(solution)/shard_map/ppermute | solution.py:28
  21.1 1.6 %collective-permute-start.4 = (bf16[272,512]{1,0:T(8,128)(2,1)S(1)}, bf16[272,512]{1,0:T(8,128)(2,1)S(1)}, u32[]{:S(2)}, u32[]{:S(2)}) collective-permute-start(bf16[272,512]{1,0:T(8,128)(2,1)S(1)} %collective-permute-done.1.refs_1_), channel_id=1, source_target_pairs={{0,12},{4,0},{8,4},{12,8},{1,13},{5,1},{9,5},{13,9},{2,14},{6,2},{... | collective-permute-start | bytes 835592 | tf_op jit(solution)/shard_map/ppermute | solution.py:28
  22.7 4.0 %collective-permute-done.5.refs_4_ = bf16[272,512]{1,0:T(8,128)(2,1)S(1)} collective-permute-done((bf16[272,512]{1,0:T(8,128)(2,1)S(1)}, bf16[272,512]{1,0:T(8,128)(2,1)S(1)}, u32[]{:S(2)}, u32[]{:S(2)}) %collective-permute-start.5) | collective-permute-done | bytes 278560 | tf_op jit(solution)/shard_map/ppermute | solution.py:28
  26.6 0.0 collective-permute-done.3.refs_2_
  26.6 0.0 collective-permute-done.8.refs_7_
  26.6 6.0 %collective-permute-done.6.refs_5_ = bf16[272,512]{1,0:T(8,128)(2,1)S(1)} collective-permute-done((bf16[272,512]{1,0:T(8,128)(2,1)S(1)}, bf16[272,512]{1,0:T(8,128)(2,1)S(1)}, u32[]{:S(2)}, u32[]{:S(2)}) %collective-permute-start.6) | collective-permute-done | bytes 278560 | tf_op jit(solution)/shard_map/ppermute | solution.py:28
  32.6 0.0 collective-permute-done.4.refs_3_
  32.6 0.1 collective-permute-start.10
  32.7 0.9 %collective-permute-start.11 = (f32[8,128]{1,0:T(8,128)S(1)}, f32[8,128]{1,0:T(8,128)S(1)}, u32[]{:S(2)}, u32[]{:S(2)}) collective-permute-start(f32[8,128]{1,0:T(8,128)S(1)} %broadcast_in_dim.8), channel_id=1, source_target_pairs={{0,80},{16,64},{32,112},{48,96},{64,16},{80,0},{96,48},{112,32},{1... | collective-permute-start | bytes 12296 | tf_op jit(solution)/shard_map/ppermute | solution.py:34
  33.7 2.6 %collective-permute-start.9 = (f32[8,128]{1,0:T(8,128)S(1)}, f32[8,128]{1,0:T(8,128)S(1)}, u32[]{:S(2)}, u32[]{:S(2)}) collective-permute-start(f32[8,128]{1,0:T(8,128)S(1)} %broadcast_in_dim.8), channel_id=1, source_target_pairs={{0,64},{16,80},{32,96},{48,112},{64,0},{80,16},{96,32},{112,48},{1... | collective-permute-start | bytes 12296 | tf_op jit(solution)/shard_map/ppermute | solution.py:34
  36.3 0.0 copy-done
  36.3 0.0 copy-done.1
  36.3 0.0 copy-done.2
  36.3 0.0 copy-done.3
  36.3 21.3 %attention.1 = (bf16[128,2048]{1,0:T(8,128)(2,1)S(1)}, bf16[128,3072]{1,0:T(8,128)(2,1)S(1)}, bf16[128,5120]{1,0:T(8,128)(2,1)S(1)}, f32[256,512]{1,0:T(8,128)S(...) custom-call(s32[1]{0:T(128)} %get-tuple-element.52.side_ref, ...), custom_call_target="tpu_custom_call" | custom-call | flops 14000000000 | bytes 12000000 | tf_op jit(solution)/shard_map/attention/pallas_call | solution.py:248
  57.6 0.0 collective-permute-done.10
  57.6 0.0 collective-permute-done.11
  57.7 0.0 collective-permute-done.9
  57.7 1.4 %collective-permute-start.15 = (bf16[128,5120]{1,0:T(8,128)(2,1)S(1)}, bf16[128,5120]{1,0:T(8,128)(2,1)S(1)}, u32[]{:S(2)}, u32[]{:S(2)}) collective-permute-start(bf16[128,5120]{1,0:T(8,128)(2,1)S(1)} %get-tuple-element.68), channel_id=1, source_target_pairs={{0,1},{1,0},{2,3},{3,2},{4,5},{5,4},{6,7},{7,6},{8,9},{9,8},{10,11... | collective-permute-start | bytes 3932168 | tf_op jit(solution)/shard_map/ppermute | solution.py:28
  59.1 0.7 collective-permute-start.12
  59.9 1.1 %collective-permute-start.13 = (bf16[256,512]{1,0:T(8,128)(2,1)S(1)}, bf16[256,512]{1,0:T(8,128)(2,1)S(1)}, u32[]{:S(2)}, u32[]{:S(2)}) collective-permute-start(bf16[256,512]{1,0:T(8,128)(2,1)S(1)} %get-tuple-element.66), channel_id=1, source_target_pairs={{0,4},{4,8},{8,12},{12,0},{1,5},{5,9},{9,13},{13,1},{2,6},{6,10},{... | collective-permute-start | bytes 786440 | tf_op jit(solution)/shard_map/ppermute | solution.py:28
  60.9 1.6 %collective-permute-start.14 = (bf16[256,512]{1,0:T(8,128)(2,1)S(1)}, bf16[256,512]{1,0:T(8,128)(2,1)S(1)}, u32[]{:S(2)}, u32[]{:S(2)}) collective-permute-start(bf16[256,512]{1,0:T(8,128)(2,1)S(1)} %get-tuple-element.67), channel_id=1, source_target_pairs={{0,12},{4,0},{8,4},{12,8},{1,13},{5,1},{9,5},{13,9},{2,14},{6,2},{... | collective-permute-start | bytes 786440 | tf_op jit(solution)/shard_map/ppermute | solution.py:28
  62.5 2.5 %collective-permute-start.16 = (f32[8,128]{1,0:T(8,128)S(1)}, f32[8,128]{1,0:T(8,128)S(1)}, u32[]{:S(2)}, u32[]{:S(2)}) collective-permute-start(f32[8,128]{1,0:T(8,128)S(1)} %add_add_fusion), channel_id=1, source_target_pairs={{0,192},{16,208},{32,224},{48,240},{64,128},{80,144},{96,160},{112... | collective-permute-start | bytes 12296 | tf_op jit(solution)/shard_map/ppermute | solution.py:34
  65.0 1.5 %collective-permute-done.16 = f32[8,128]{1,0:T(8,128)S(1)} collective-permute-done((f32[8,128]{1,0:T(8,128)S(1)}, f32[8,128]{1,0:T(8,128)S(1)}, u32[]{:S(2)}, u32[]{:S(2)}) %collective-permute-start.16) | collective-permute-done | bytes 4128 | tf_op jit(solution)/shard_map/ppermute | solution.py:34
  66.5 0.5 collective-permute-done.12
  67.0 1.6 %collective-permute-done.13 = bf16[256,512]{1,0:T(8,128)(2,1)S(1)} collective-permute-done((bf16[256,512]{1,0:T(8,128)(2,1)S(1)}, bf16[256,512]{1,0:T(8,128)(2,1)S(1)}, u32[]{:S(2)}, u32[]{:S(2)}) %collective-permute-start.13) | collective-permute-done | bytes 262176 | tf_op jit(solution)/shard_map/ppermute | solution.py:28
  68.6 0.0 collective-permute-done.14
  68.6 0.0 collective-permute-done.15.refs_1_
  68.6 0.1 add_convert_fusion
  68.7 0.8 collective-permute-start.18
  69.5 0.1 add_convert_fusion.1
  69.6 1.5 %collective-permute-start.17 = (bf16[256,512]{1,0:T(8,128)(2,1)S(1)}, bf16[256,512]{1,0:T(8,128)(2,1)S(1)}, u32[]{:S(2)}, u32[]{:S(2)}) collective-permute-start(bf16[256,512]{1,0:T(8,128)(2,1)S(1)} %add_convert_fusion.1), channel_id=1, source_target_pairs={{0,8},{4,12},{8,0},{12,4},{1,9},{5,13},{9,1},{13,5},{2,10},{6,14},... | collective-permute-start | bytes 786440 | tf_op jit(solution)/shard_map/ppermute | solution.py:28
  71.1 1.5 %collective-permute-start.19 = (bf16[256,512]{1,0:T(8,128)(2,1)S(1)}, bf16[256,512]{1,0:T(8,128)(2,1)S(1)}, u32[]{:S(2)}, u32[]{:S(2)}) collective-permute-start(bf16[256,512]{1,0:T(8,128)(2,1)S(1)} %get-tuple-element.76), channel_id=1, source_target_pairs={{0,4},{4,8},{8,12},{12,0},{1,5},{5,9},{9,13},{13,1},{2,6},{6,10},{... | collective-permute-start | bytes 786440 | tf_op jit(solution)/shard_map/ppermute | solution.py:28
  72.6 1.2 %collective-permute-start.20 = (bf16[256,512]{1,0:T(8,128)(2,1)S(1)}, bf16[256,512]{1,0:T(8,128)(2,1)S(1)}, u32[]{:S(2)}, u32[]{:S(2)}) collective-permute-start(bf16[256,512]{1,0:T(8,128)(2,1)S(1)} %get-tuple-element.77), channel_id=1, source_target_pairs={{0,12},{4,0},{8,4},{12,8},{1,13},{5,1},{9,5},{13,9},{2,14},{6,2},{... | collective-permute-start | bytes 786440 | tf_op jit(solution)/shard_map/ppermute | solution.py:28
  73.8 5.2 %collective-permute-start.21 = (f32[8,128]{1,0:T(8,128)S(1)}, f32[8,128]{1,0:T(8,128)S(1)}, u32[]{:S(2)}, u32[]{:S(2)}) collective-permute-start(f32[8,128]{1,0:T(8,128)S(1)} %add.99), channel_id=1, source_target_pairs={{0,48},{16,32},{32,16},{48,0},{64,112},{80,96},{96,80},{112,64},{1... | collective-permute-start | bytes 12296 | tf_op jit(solution)/shard_map/ppermute | solution.py:34
  79.0 1.8 %place.1 = bf16[1,1,128,4096]{3,2,1,0:T(8,128)(2,1)} custom-call(s32[1]{0:T(128)} %get-tuple-element.52.side_ref, bf16[128,2048]{1,0:T(8,128)(2,1)S(1)} %get-tuple-element.78.refs_0_, bf16[128,5120]{1,0:T(8,128)(2,1)S(1)} %collective-permute-done.15.refs_1_), custom_call_target="tpu_custom_call" | custom-call | bytes 2000000 | tf_op jit(solution)/shard_map/place/pallas_call | solution.py:330
  80.9 0.0 collective-permute-done.21
  80.9 0.0 collective-permute-done.18
  80.9 0.0 collective-permute-done.17
  80.9 4.1 %collective-permute-done.19 = bf16[256,512]{1,0:T(8,128)(2,1)S(1)} collective-permute-done((bf16[256,512]{1,0:T(8,128)(2,1)S(1)}, bf16[256,512]{1,0:T(8,128)(2,1)S(1)}, u32[]{:S(2)}, u32[]{:S(2)}) %collective-permute-start.19) | collective-permute-done | bytes 262176 | tf_op jit(solution)/shard_map/ppermute | solution.py:28
  85.0 0.0 collective-permute-done.20
  85.0 0.2 fusion.16
  85.3 0.6 collective-permute-start.22
  85.9 1.0 %collective-permute-done.22.refs_3_ = bf16[128,512]{1,0:T(8,128)(2,1)S(1)} collective-permute-done((bf16[128,512]{1,0:T(8,128)(2,1)S(1)}, bf16[128,512]{1,0:T(8,128)(2,1)S(1)}, u32[]{:S(2)}, u32[]{:S(2)}) %collective-permute-start.22) | collective-permute-done | bytes 131104 | tf_op jit(solution)/shard_map/ppermute | solution.py:28
  86.9 2.6 %finish.1 = (bf16[1,1,128,4096]{3,2,1,0:T(8,128)(2,1)}, bf16[1,1,128,1024]{3,2,1,0:T(8,128)(2,1)}, bf16[1,1,128,1024]{3,2,1,0:T(8,128)(2,1)}, bf16[1,64,1024]{2,1,0:T(8,128)(2,1)}, bf16[1,64,1024]{2,1,0:T(8,128)(2,1)}) custom-call(s32[1]{0:T(128)} %get-tuple-element.52.side_ref, bf16[128,3072]{1,0:T(8,128)(2,1)S(1)} %get-tuple-element.82.refs_0_, ...), custom_call_target="tpu_custom_call" | custom-call | bytes 2000000 | tf_op jit(solution)/shard_map/finish/pallas_call | solution.py:330
  (13 shorter events, 0.1 us)
Async XLA Ops:
  3.7 6.7 %collective-permute-start = (bf16[144,512]{1,0:T(8,128)(2,1)}, bf16[144,512]{1,0:T(8,128)(2,1)S(1)}, u32[]{:S(2)}, u32[]{:S(2)}) collective-permute-start(bf16[144,512]{1,0:T(8,128)(2,1)} %get-tuple-element.51), channel_id=1, source_target_pairs={{0,1},{1,0},{2,3},{3,2},{4,5},{5,4},{6,7},{7,6},{8,9},{9,8},{10,11... | collective-permute-start | bytes 442376 | tf_op jit(solution)/shard_map/ppermute | solution.py:28
  7.0 3.4 %copy-start.4 = (bf16[144,512]{1,0:T(8,128)(2,1)S(1)}, bf16[144,512]{1,0:T(8,128)(2,1)}, u32[]{:S(2)}) copy-start(bf16[144,512]{1,0:T(8,128)(2,1)} %get-tuple-element.50) | copy-start | bytes 442372
  7.0 29.2 %copy-start = (bf16[1,1,128,4096]{3,2,1,0:T(8,128)(2,1)S(1)}, bf16[1,1,128,4096]{3,2,1,0:T(8,128)(2,1)}, u32[]{:S(2)}) copy-start(bf16[1,1,128,4096]{3,2,1,0:T(8,128)(2,1)} %refs_8_.1) | copy-start | bytes 3145732
  7.0 29.2 %copy-start.1 = (bf16[1,1,128,4096]{3,2,1,0:T(8,128)(2,1)S(1)}, bf16[1,1,128,4096]{3,2,1,0:T(8,128)(2,1)}, u32[]{:S(2)}) copy-start(bf16[1,1,128,4096]{3,2,1,0:T(8,128)(2,1)} %refs_9_.1) | copy-start | bytes 3145732
  7.0 29.2 %copy-start.2 = (bf16[1,1,128,1024]{3,2,1,0:T(8,128)(2,1)S(1)}, bf16[1,1,128,1024]{3,2,1,0:T(8,128)(2,1)}, u32[]{:S(2)}) copy-start(bf16[1,1,128,1024]{3,2,1,0:T(8,128)(2,1)} %refs_10_.1) | copy-start | bytes 786436
  7.0 29.2 %copy-start.3 = (bf16[1,1,128,1024]{3,2,1,0:T(8,128)(2,1)S(1)}, bf16[1,1,128,1024]{3,2,1,0:T(8,128)(2,1)}, u32[]{:S(2)}) copy-start(bf16[1,1,128,1024]{3,2,1,0:T(8,128)(2,1)} %refs_11_.1) | copy-start | bytes 786436
  10.3 9.6 %collective-permute-start.2 = (bf16[128,5120]{1,0:T(8,128)(2,1)}, bf16[128,5120]{1,0:T(8,128)(2,1)S(1)}, u32[]{:S(2)}, u32[]{:S(2)}) collective-permute-start(bf16[128,5120]{1,0:T(8,128)(2,1)} %pack.1), channel_id=1, source_target_pairs={{0,1},{1,0},{2,3},{3,2},{4,5},{5,4},{6,7},{7,6},{8,9},{9,8},{10,11... | collective-permute-start | bytes 3932168 | tf_op jit(solution)/shard_map/ppermute | solution.py:28
  10.5 9.4 %collective-permute-start.7 = (bf16[272,512]{1,0:T(8,128)(2,1)S(1)}, bf16[272,512]{1,0:T(8,128)(2,1)S(1)}, u32[]{:S(2)}, u32[]{:S(2)}) collective-permute-start(bf16[272,512]{1,0:T(8,128)(2,1)S(1)} %constant_dynamic-update-slice_fusion.refs_0_), channel_id=1, source_target_pairs={{0,8},{4,12},{8,0},{12,4},{1,9},{5,13},{9,1},{13,5},{2,10},{6,14},... | collective-permute-start | bytes 835592 | tf_op jit(solution)/shard_map/ppermute | solution.py:28
  11.8 8.1 %collective-permute-start.1 = (bf16[272,512]{1,0:T(8,128)(2,1)S(1)}, bf16[272,512]{1,0:T(8,128)(2,1)S(1)}, u32[]{:S(2)}, u32[]{:S(2)}) collective-permute-start(bf16[272,512]{1,0:T(8,128)(2,1)S(1)} %constant_dynamic-update-slice_fusion.refs_0_), channel_id=1, source_target_pairs={{0,2},{2,0},{1,3},{3,1},{4,6},{6,4},{5,7},{7,5},{8,10},{10,8},{9,1... | collective-permute-start | bytes 835592 | tf_op jit(solution)/shard_map/ppermute | solution.py:28
  13.4 13.2 %collective-permute-start.5 = (bf16[272,512]{1,0:T(8,128)(2,1)S(1)}, bf16[272,512]{1,0:T(8,128)(2,1)S(1)}, u32[]{:S(2)}, u32[]{:S(2)}) collective-permute-start(bf16[272,512]{1,0:T(8,128)(2,1)S(1)} %constant_dynamic-update-slice_fusion.refs_0_), channel_id=1, source_target_pairs={{0,4},{4,8},{8,12},{12,0},{1,5},{5,9},{9,13},{13,1},{2,6},{6,10},{... | collective-permute-start | bytes 835592 | tf_op jit(solution)/shard_map/ppermute | solution.py:28
  13.8 12.8 %collective-permute-start.3 = (bf16[272,512]{1,0:T(8,128)(2,1)S(1)}, bf16[272,512]{1,0:T(8,128)(2,1)S(1)}, u32[]{:S(2)}, u32[]{:S(2)}) collective-permute-start(bf16[272,512]{1,0:T(8,128)(2,1)S(1)} %constant_dynamic-update-slice_fusion.refs_0_), channel_id=1, source_target_pairs={{0,12},{4,0},{8,4},{12,8},{1,13},{5,1},{9,5},{13,9},{2,14},{6,2},{... | collective-permute-start | bytes 835592 | tf_op jit(solution)/shard_map/ppermute | solution.py:28
  19.9 6.7 %collective-permute-start.8 = (bf16[272,512]{1,0:T(8,128)(2,1)S(1)}, bf16[272,512]{1,0:T(8,128)(2,1)S(1)}, u32[]{:S(2)}, u32[]{:S(2)}) collective-permute-start(bf16[272,512]{1,0:T(8,128)(2,1)S(1)} %collective-permute-done.7.refs_6_), channel_id=1, source_target_pairs={{0,2},{2,0},{1,3},{3,1},{4,6},{6,4},{5,7},{7,5},{8,10},{10,8},{9,1... | collective-permute-start | bytes 835592 | tf_op jit(solution)/shard_map/ppermute | solution.py:28
  19.9 12.7 %collective-permute-start.6 = (bf16[272,512]{1,0:T(8,128)(2,1)S(1)}, bf16[272,512]{1,0:T(8,128)(2,1)S(1)}, u32[]{:S(2)}, u32[]{:S(2)}) collective-permute-start(bf16[272,512]{1,0:T(8,128)(2,1)S(1)} %collective-permute-done.1.refs_1_), channel_id=1, source_target_pairs={{0,4},{4,8},{8,12},{12,0},{1,5},{5,9},{9,13},{13,1},{2,6},{6,10},{... | collective-permute-start | bytes 835592 | tf_op jit(solution)/shard_map/ppermute | solution.py:28
  21.1 11.5 %collective-permute-start.4 = (bf16[272,512]{1,0:T(8,128)(2,1)S(1)}, bf16[272,512]{1,0:T(8,128)(2,1)S(1)}, u32[]{:S(2)}, u32[]{:S(2)}) collective-permute-start(bf16[272,512]{1,0:T(8,128)(2,1)S(1)} %collective-permute-done.1.refs_1_), channel_id=1, source_target_pairs={{0,12},{4,0},{8,4},{12,8},{1,13},{5,1},{9,5},{13,9},{2,14},{6,2},{... | collective-permute-start | bytes 835592 | tf_op jit(solution)/shard_map/ppermute | solution.py:28
  32.6 25.0 %collective-permute-start.10 = (f32[8,128]{1,0:T(8,128)S(1)}, f32[8,128]{1,0:T(8,128)S(1)}, u32[]{:S(2)}, u32[]{:S(2)}) collective-permute-start(f32[8,128]{1,0:T(8,128)S(1)} %broadcast_in_dim.8), channel_id=1, source_target_pairs={{0,16},{16,0},{32,48},{48,32},{64,80},{80,64},{96,112},{112,96},{1... | collective-permute-start | bytes 12296 | tf_op jit(solution)/shard_map/ppermute | solution.py:34
  32.7 24.9 %collective-permute-start.11 = (f32[8,128]{1,0:T(8,128)S(1)}, f32[8,128]{1,0:T(8,128)S(1)}, u32[]{:S(2)}, u32[]{:S(2)}) collective-permute-start(f32[8,128]{1,0:T(8,128)S(1)} %broadcast_in_dim.8), channel_id=1, source_target_pairs={{0,80},{16,64},{32,112},{48,96},{64,16},{80,0},{96,48},{112,32},{1... | collective-permute-start | bytes 12296 | tf_op jit(solution)/shard_map/ppermute | solution.py:34
  33.7 24.0 %collective-permute-start.9 = (f32[8,128]{1,0:T(8,128)S(1)}, f32[8,128]{1,0:T(8,128)S(1)}, u32[]{:S(2)}, u32[]{:S(2)}) collective-permute-start(f32[8,128]{1,0:T(8,128)S(1)} %broadcast_in_dim.8), channel_id=1, source_target_pairs={{0,64},{16,80},{32,96},{48,112},{64,0},{80,16},{96,32},{112,48},{1... | collective-permute-start | bytes 12296 | tf_op jit(solution)/shard_map/ppermute | solution.py:34
  57.7 10.9 %collective-permute-start.15 = (bf16[128,5120]{1,0:T(8,128)(2,1)S(1)}, bf16[128,5120]{1,0:T(8,128)(2,1)S(1)}, u32[]{:S(2)}, u32[]{:S(2)}) collective-permute-start(bf16[128,5120]{1,0:T(8,128)(2,1)S(1)} %get-tuple-element.68), channel_id=1, source_target_pairs={{0,1},{1,0},{2,3},{3,2},{4,5},{5,4},{6,7},{7,6},{8,9},{9,8},{10,11... | collective-permute-start | bytes 3932168 | tf_op jit(solution)/shard_map/ppermute | solution.py:28
  59.1 7.9 %collective-permute-start.12 = (bf16[256,512]{1,0:T(8,128)(2,1)S(1)}, bf16[256,512]{1,0:T(8,128)(2,1)S(1)}, u32[]{:S(2)}, u32[]{:S(2)}) collective-permute-start(bf16[256,512]{1,0:T(8,128)(2,1)S(1)} %get-tuple-element.65), channel_id=1, source_target_pairs={{0,2},{2,0},{1,3},{3,1},{4,6},{6,4},{5,7},{7,5},{8,10},{10,8},{9,1... | collective-permute-start | bytes 786440 | tf_op jit(solution)/shard_map/ppermute | solution.py:28
  59.9 8.7 %collective-permute-start.13 = (bf16[256,512]{1,0:T(8,128)(2,1)S(1)}, bf16[256,512]{1,0:T(8,128)(2,1)S(1)}, u32[]{:S(2)}, u32[]{:S(2)}) collective-permute-start(bf16[256,512]{1,0:T(8,128)(2,1)S(1)} %get-tuple-element.66), channel_id=1, source_target_pairs={{0,4},{4,8},{8,12},{12,0},{1,5},{5,9},{9,13},{13,1},{2,6},{6,10},{... | collective-permute-start | bytes 786440 | tf_op jit(solution)/shard_map/ppermute | solution.py:28
  60.9 7.7 %collective-permute-start.14 = (bf16[256,512]{1,0:T(8,128)(2,1)S(1)}, bf16[256,512]{1,0:T(8,128)(2,1)S(1)}, u32[]{:S(2)}, u32[]{:S(2)}) collective-permute-start(bf16[256,512]{1,0:T(8,128)(2,1)S(1)} %get-tuple-element.67), channel_id=1, source_target_pairs={{0,12},{4,0},{8,4},{12,8},{1,13},{5,1},{9,5},{13,9},{2,14},{6,2},{... | collective-permute-start | bytes 786440 | tf_op jit(solution)/shard_map/ppermute | solution.py:28
  62.5 4.0 %collective-permute-start.16 = (f32[8,128]{1,0:T(8,128)S(1)}, f32[8,128]{1,0:T(8,128)S(1)}, u32[]{:S(2)}, u32[]{:S(2)}) collective-permute-start(f32[8,128]{1,0:T(8,128)S(1)} %add_add_fusion), channel_id=1, source_target_pairs={{0,192},{16,208},{32,224},{48,240},{64,128},{80,144},{96,160},{112... | collective-permute-start | bytes 12296 | tf_op jit(solution)/shard_map/ppermute | solution.py:34
  68.7 12.2 %collective-permute-start.18 = (bf16[256,512]{1,0:T(8,128)(2,1)S(1)}, bf16[256,512]{1,0:T(8,128)(2,1)S(1)}, u32[]{:S(2)}, u32[]{:S(2)}) collective-permute-start(bf16[256,512]{1,0:T(8,128)(2,1)S(1)} %add_convert_fusion), channel_id=1, source_target_pairs={{0,2},{2,0},{1,3},{3,1},{4,6},{6,4},{5,7},{7,5},{8,10},{10,8},{9,1... | collective-permute-start | bytes 786440 | tf_op jit(solution)/shard_map/ppermute | solution.py:28
  69.6 11.3 %collective-permute-start.17 = (bf16[256,512]{1,0:T(8,128)(2,1)S(1)}, bf16[256,512]{1,0:T(8,128)(2,1)S(1)}, u32[]{:S(2)}, u32[]{:S(2)}) collective-permute-start(bf16[256,512]{1,0:T(8,128)(2,1)S(1)} %add_convert_fusion.1), channel_id=1, source_target_pairs={{0,8},{4,12},{8,0},{12,4},{1,9},{5,13},{9,1},{13,5},{2,10},{6,14},... | collective-permute-start | bytes 786440 | tf_op jit(solution)/shard_map/ppermute | solution.py:28
  71.1 13.9 %collective-permute-start.19 = (bf16[256,512]{1,0:T(8,128)(2,1)S(1)}, bf16[256,512]{1,0:T(8,128)(2,1)S(1)}, u32[]{:S(2)}, u32[]{:S(2)}) collective-permute-start(bf16[256,512]{1,0:T(8,128)(2,1)S(1)} %get-tuple-element.76), channel_id=1, source_target_pairs={{0,4},{4,8},{8,12},{12,0},{1,5},{5,9},{9,13},{13,1},{2,6},{6,10},{... | collective-permute-start | bytes 786440 | tf_op jit(solution)/shard_map/ppermute | solution.py:28
  72.6 12.4 %collective-permute-start.20 = (bf16[256,512]{1,0:T(8,128)(2,1)S(1)}, bf16[256,512]{1,0:T(8,128)(2,1)S(1)}, u32[]{:S(2)}, u32[]{:S(2)}) collective-permute-start(bf16[256,512]{1,0:T(8,128)(2,1)S(1)} %get-tuple-element.77), channel_id=1, source_target_pairs={{0,12},{4,0},{8,4},{12,8},{1,13},{5,1},{9,5},{13,9},{2,14},{6,2},{... | collective-permute-start | bytes 786440 | tf_op jit(solution)/shard_map/ppermute | solution.py:28
  73.8 7.1 %collective-permute-start.21 = (f32[8,128]{1,0:T(8,128)S(1)}, f32[8,128]{1,0:T(8,128)S(1)}, u32[]{:S(2)}, u32[]{:S(2)}) collective-permute-start(f32[8,128]{1,0:T(8,128)S(1)} %add.99), channel_id=1, source_target_pairs={{0,48},{16,32},{32,16},{48,0},{64,112},{80,96},{96,80},{112,64},{1... | collective-permute-start | bytes 12296 | tf_op jit(solution)/shard_map/ppermute | solution.py:34
  85.3 1.6 %collective-permute-start.22 = (bf16[128,512]{1,0:T(8,128)(2,1)S(1)}, bf16[128,512]{1,0:T(8,128)(2,1)S(1)}, u32[]{:S(2)}, u32[]{:S(2)}) collective-permute-start(bf16[128,512]{1,0:T(8,128)(2,1)S(1)} %pad_maximum_fusion), channel_id=1, source_target_pairs={{0,1},{1,0},{2,3},{3,2},{4,5},{5,4},{6,7},{7,6},{8,9},{9,8},{10,11... | collective-permute-start | bytes 393224 | tf_op jit(solution)/shard_map/ppermute | solution.py:28

commit v4 on v3

--- a/solution.py
+++ b/solution.py
@@ -370,9 +370,12 @@
     far_z = step(far, "zl", 1)
     blocks = (mine, near_z, above, above_z, below, below_z, far, far_z)
 
-    tokens = sum(b[2 * pair + i : 2 * pair + i + 1, :HD].astype(F32) for b in blocks for i in (0, 8))
+    tokens = sum(b[2 * pair + i : 2 * pair + i + 1, :HD].astype(F32) for b in (mine, above, below, far) for i in (0, 8))
     tokens = jnp.broadcast_to(tokens, (8, HD))
     tokens = tokens + swap(tokens, 1, 0) + swap(tokens, 0, 1) + swap(tokens, 1, 1)
+    below_z, above_z, far_z, tokens = tie((below_z, above_z, far_z, tokens))
+    blocks = (mine, near_z, above, above_z, below, below_z, far, far_z)
+    tokens = tokens + step(tokens, "zl", 1)
 
     own_att, own_grad, for_sib, *parts = attention(
         side, blocks, resp_q, out_grad, resp_k, resp_v, packed, kv_heads

time: 89.8 us -> 89.8 us (level)
    ppermute x18 -> x19, waiting for transfers between devices: 21 us -> 16.3 us  [step(): lax.ppermute(values, axis, [(i, (i + by) % size) for i in range(size)])]
    ppermute x5, waiting for transfers between devices: 1.49 us -> 5.56 us  [swap(): return lax.ppermute(values, ('x', 'zh'), pairs)]
    ppermute x18 -> x19, starting transfers between devices: 22.2 us -> 25.1 us  [step(): lax.ppermute(values, axis, [(i, (i + by) % size) for i in range(size)])]
    ppermute x5, starting transfers between devices: 11.3 us -> 9.15 us  [swap(): return lax.ppermute(values, ('x', 'zh'), pairs)]
  transfers between devices with their start and end apart: 23 -> 24, of which waited for: 8 -> 10; matrix products, arithmetic and copies ran while one was open for 0% -> 0% of each run, Pallas kernels for 29% -> 29%
where the time goes in v4:
time: 89.8 us; the launch traced here: 89.7 us
  starting transfers between devices  34.3 us (38%)
  Pallas kernels  30.8 us (34%)
  waiting for transfers between devices  21.8 us (24%)
  between operations  2.31 us (3%)
    ppermute x19, starting transfers between devices, step(): lax.ppermute(values, axis, [(i, (i + by) % size) for i in range(size)])  25.1 us
    pallas_call x1, Pallas kernels, attention(): pl.pallas_call(functools.partial(attention_kernel, float(HD) ** (-0.5)),...  21.3 us
    ppermute x19, waiting for transfers between devices, step(): lax.ppermute(values, axis, [(i, (i + by) % size) for i in range(size)])  16.3 us
    ppermute x5, starting transfers between devices, swap(): return lax.ppermute(values, ('x', 'zh'), pairs)  9.15 us
    ppermute x5, waiting for transfers between devices, swap(): return lax.ppermute(values, ('x', 'zh'), pairs)  5.56 us
    pallas_call x2, Pallas kernels, halves(): pl.pallas_call(copied, grid_spec=pltpu.PrefetchScalarGridSpec(num_scalar_...  4.46 us
    pallas_call x1, Pallas kernels, pack(): pl.pallas_call(pack_kernel, in_specs=[pl.BlockSpec(memory_space=pltpu.SME...  3.21 us
  transfers between devices with their start and end apart: 24, of which 10 were waited for; matrix products, arithmetic and copies ran while one was open for 0% of the time, Pallas kernels for 29%

profile of v4, /device:TPU:1, one launch (start us, length us, event | category | flops | bytes accessed | tf_op | source)
XLA Modules:
  0.0 89.7 jit_solution(8658662274080734906)
XLA Ops:
  1.9 1.8 %prep.1 = (bf16[144,512]{1,0:T(8,128)(2,1)}, bf16[144,512]{1,0:T(8,128)(2,1)}, s32[1]{0:T(128)}) custom-call(bf16[1,64,1024]{2,1,0:T(8,128)(2,1)} %k_in.1, bf16[1,64,1024]{2,1,0:T(8,128)(2,1)} %v_in.1, s32[1,1]{1,0:T(1,128)S(6)} %copy.19.length_in, f32[1,1]{1,0:T(1,128)S(6)} %copy.20.reward_in), custom_call_target="tpu_custom_call" | custom-call | bytes 500000 | tf_op jit(solution)/shard_map/prep/pallas_call | solution.py:154
  3.7 3.3 %collective-permute-start = (bf16[144,512]{1,0:T(8,128)(2,1)}, bf16[144,512]{1,0:T(8,128)(2,1)S(1)}, u32[]{:S(2)}, u32[]{:S(2)}) collective-permute-start(bf16[144,512]{1,0:T(8,128)(2,1)} %get-tuple-element.55), channel_id=1, source_target_pairs={{0,1},{1,0},{2,3},{3,2},{4,5},{5,4},{6,7},{7,6},{8,9},{9,8},{10,11... | collective-permute-start | bytes 442376 | tf_op jit(solution)/shard_map/ppermute | solution.py:28
  7.0 0.0 copy-start.4
  7.0 0.0 copy-start
  7.0 0.0 copy-start.3
  7.1 3.2 %pack.1 = bf16[128,5120]{1,0:T(8,128)(2,1)} custom-call(s32[1]{0:T(128)} %get-tuple-element.56.side_ref, bf16[1,1,128,4096]{3,2,1,0:T(8,128)(2,1)} %refs_8_.1, bf16[1,1,128,4096]{3,2,1,0:T(8,128)(2,1)} %refs_9_.1, bf16[1,1,128,1024]{3,2,1,0:T(8,128)(2,1)} %refs_10_.1, bf16[1,1,128,1024]{3,2,1,0:T(8,128)(2,1)} %refs_11_.1), custom_call_target="tpu_custom_call" | custom-call | bytes 100000 | tf_op jit(solution)/shard_map/pack/pallas_call | solution.py:182
  10.3 0.1 collective-permute-start.2
  10.4 0.0 copy-done.4
  10.4 0.0 collective-permute-done
  10.5 1.3 %collective-permute-start.5 = (bf16[272,512]{1,0:T(8,128)(2,1)S(1)}, bf16[272,512]{1,0:T(8,128)(2,1)S(1)}, u32[]{:S(2)}, u32[]{:S(2)}) collective-permute-start(bf16[272,512]{1,0:T(8,128)(2,1)S(1)} %constant_dynamic-update-slice_fusion.refs_0_), channel_id=1, source_target_pairs={{0,8},{4,12},{8,0},{12,4},{1,9},{5,13},{9,1},{13,5},{2,10},{6,14},... | collective-permute-start | bytes 835592 | tf_op jit(solution)/shard_map/ppermute | solution.py:28
  11.8 1.6 %collective-permute-start.1 = (bf16[272,512]{1,0:T(8,128)(2,1)S(1)}, bf16[272,512]{1,0:T(8,128)(2,1)S(1)}, u32[]{:S(2)}, u32[]{:S(2)}) collective-permute-start(bf16[272,512]{1,0:T(8,128)(2,1)S(1)} %constant_dynamic-update-slice_fusion.refs_0_), channel_id=1, source_target_pairs={{0,2},{2,0},{1,3},{3,1},{4,6},{6,4},{5,7},{7,5},{8,10},{10,8},{9,1... | collective-permute-start | bytes 835592 | tf_op jit(solution)/shard_map/ppermute | solution.py:28
  13.4 0.4 collective-permute-start.8
  13.8 2.3 %collective-permute-start.7 = (bf16[272,512]{1,0:T(8,128)(2,1)S(1)}, bf16[272,512]{1,0:T(8,128)(2,1)S(1)}, u32[]{:S(2)}, u32[]{:S(2)}) collective-permute-start(bf16[272,512]{1,0:T(8,128)(2,1)S(1)} %constant_dynamic-update-slice_fusion.refs_0_), channel_id=1, source_target_pairs={{0,12},{4,0},{8,4},{12,8},{1,13},{5,1},{9,5},{13,9},{2,14},{6,2},{... | collective-permute-start | bytes 835592 | tf_op jit(solution)/shard_map/ppermute | solution.py:28
  16.1 3.8 %collective-permute-done.5.refs_6_ = bf16[272,512]{1,0:T(8,128)(2,1)S(1)} collective-permute-done((bf16[272,512]{1,0:T(8,128)(2,1)S(1)}, bf16[272,512]{1,0:T(8,128)(2,1)S(1)}, u32[]{:S(2)}, u32[]{:S(2)}) %collective-permute-start.5) | collective-permute-done | bytes 278560 | tf_op jit(solution)/shard_map/ppermute | solution.py:28
  19.9 0.0 collective-permute-start.6
  19.9 0.0 collective-permute-done.1.refs_1_
  19.9 0.0 collective-permute-done.2.refs_12_.refs_13_.refs_14_.refs_15_
  19.9 2.6 %collective-permute-start.4 = (bf16[272,512]{1,0:T(8,128)(2,1)S(1)}, bf16[272,512]{1,0:T(8,128)(2,1)S(1)}, u32[]{:S(2)}, u32[]{:S(2)}) collective-permute-start(bf16[272,512]{1,0:T(8,128)(2,1)S(1)} %collective-permute-done.1.refs_1_), channel_id=1, source_target_pairs={{0,12},{4,0},{8,4},{12,8},{1,13},{5,1},{9,5},{13,9},{2,14},{6,2},{... | collective-permute-start | bytes 835592 | tf_op jit(solution)/shard_map/ppermute | solution.py:28
  22.5 0.0 collective-permute-start.3
  22.5 4.1 %collective-permute-done.8.refs_4_ = bf16[272,512]{1,0:T(8,128)(2,1)S(1)} collective-permute-done((bf16[272,512]{1,0:T(8,128)(2,1)S(1)}, bf16[272,512]{1,0:T(8,128)(2,1)S(1)}, u32[]{:S(2)}, u32[]{:S(2)}) %collective-permute-start.8) | collective-permute-done | bytes 278560 | tf_op jit(solution)/shard_map/ppermute | solution.py:28
  26.6 0.0 collective-permute-done.7.refs_2_
  26.7 1.1 %collective-permute-start.10 = (f32[8,128]{1,0:T(8,128)S(1)}, f32[8,128]{1,0:T(8,128)S(1)}, u32[]{:S(2)}, u32[]{:S(2)}) collective-permute-start(f32[8,128]{1,0:T(8,128)S(1)} %broadcast_in_dim.8), channel_id=1, source_target_pairs={{0,16},{16,0},{32,48},{48,32},{64,80},{80,64},{96,112},{112,96},{1... | collective-permute-start | bytes 12296 | tf_op jit(solution)/shard_map/ppermute | solution.py:34
  27.8 1.0 %collective-permute-start.11 = (f32[8,128]{1,0:T(8,128)S(1)}, f32[8,128]{1,0:T(8,128)S(1)}, u32[]{:S(2)}, u32[]{:S(2)}) collective-permute-start(f32[8,128]{1,0:T(8,128)S(1)} %broadcast_in_dim.8), channel_id=1, source_target_pairs={{0,80},{16,64},{32,112},{48,96},{64,16},{80,0},{96,48},{112,32},{1... | collective-permute-start | bytes 12296 | tf_op jit(solution)/shard_map/ppermute | solution.py:34
  28.8 1.6 %collective-permute-done.10 = f32[8,128]{1,0:T(8,128)S(1)} collective-permute-done((f32[8,128]{1,0:T(8,128)S(1)}, f32[8,128]{1,0:T(8,128)S(1)}, u32[]{:S(2)}, u32[]{:S(2)}) %collective-permute-start.10) | collective-permute-done | bytes 4128 | tf_op jit(solution)/shard_map/ppermute | solution.py:34
  30.4 0.0 collective-permute-start.9
  30.4 1.6 %collective-permute-done.11 = f32[8,128]{1,0:T(8,128)S(1)} collective-permute-done((f32[8,128]{1,0:T(8,128)S(1)}, f32[8,128]{1,0:T(8,128)S(1)}, u32[]{:S(2)}, u32[]{:S(2)}) %collective-permute-start.11) | collective-permute-done | bytes 4128 | tf_op jit(solution)/shard_map/ppermute | solution.py:34
  32.0 0.8 collective-permute-done.9
  32.9 0.0 collective-permute-done.6.refs_7_
  32.9 0.0 collective-permute-done.4.refs_3_
  32.9 0.0 collective-permute-done.3.refs_5_
  32.9 1.3 %collective-permute-start.12 = (f32[8,128]{1,0:T(8,128)S(1)}, f32[8,128]{1,0:T(8,128)S(1)}, u32[]{:S(2)}, u32[]{:S(2)}) collective-permute-start(f32[8,128]{1,0:T(8,128)S(1)} %add_add_fusion), channel_id=1, source_target_pairs={{0,2},{2,0},{1,3},{3,1},{4,6},{6,4},{5,7},{7,5},{8,10},{10,8},{9,1... | collective-permute-start | bytes 12296 | tf_op jit(solution)/shard_map/ppermute | solution.py:28
  34.2 0.0 copy-done
  34.2 0.0 copy-done.1
  34.2 0.0 copy-done.2
  34.2 0.0 copy-done.3
  34.2 21.3 %attention.1 = (bf16[128,2048]{1,0:T(8,128)(2,1)S(1)}, bf16[128,3072]{1,0:T(8,128)(2,1)S(1)}, bf16[128,5120]{1,0:T(8,128)(2,1)S(1)}, f32[256,512]{1,0:T(8,128)S(...) custom-call(s32[1]{0:T(128)} %get-tuple-element.56.side_ref, ...), custom_call_target="tpu_custom_call" | custom-call | flops 14000000000 | bytes 12000000 | tf_op jit(solution)/shard_map/attention/pallas_call | solution.py:248
  55.6 0.0 collective-permute-done.12
  55.6 3.6 %collective-permute-start.16 = (bf16[128,5120]{1,0:T(8,128)(2,1)S(1)}, bf16[128,5120]{1,0:T(8,128)(2,1)S(1)}, u32[]{:S(2)}, u32[]{:S(2)}) collective-permute-start(bf16[128,5120]{1,0:T(8,128)(2,1)S(1)} %get-tuple-element.76), channel_id=1, source_target_pairs={{0,1},{1,0},{2,3},{3,2},{4,5},{5,4},{6,7},{7,6},{8,9},{9,8},{10,11... | collective-permute-start | bytes 3932168 | tf_op jit(solution)/shard_map/ppermute | solution.py:28
  59.2 0.0 collective-permute-start.13
  59.2 1.1 %collective-permute-start.14 = (bf16[256,512]{1,0:T(8,128)(2,1)S(1)}, bf16[256,512]{1,0:T(8,128)(2,1)S(1)}, u32[]{:S(2)}, u32[]{:S(2)}) collective-permute-start(bf16[256,512]{1,0:T(8,128)(2,1)S(1)} %get-tuple-element.74), channel_id=1, source_target_pairs={{0,4},{4,8},{8,12},{12,0},{1,5},{5,9},{9,13},{13,1},{2,6},{6,10},{... | collective-permute-start | bytes 786440 | tf_op jit(solution)/shard_map/ppermute | solution.py:28
  60.2 1.6 %collective-permute-start.15 = (bf16[256,512]{1,0:T(8,128)(2,1)S(1)}, bf16[256,512]{1,0:T(8,128)(2,1)S(1)}, u32[]{:S(2)}, u32[]{:S(2)}) collective-permute-start(bf16[256,512]{1,0:T(8,128)(2,1)S(1)} %get-tuple-element.75), channel_id=1, source_target_pairs={{0,12},{4,0},{8,4},{12,8},{1,13},{5,1},{9,5},{13,9},{2,14},{6,2},{... | collective-permute-start | bytes 786440 | tf_op jit(solution)/shard_map/ppermute | solution.py:28
  61.8 2.5 %collective-permute-start.17 = (f32[8,128]{1,0:T(8,128)S(1)}, f32[8,128]{1,0:T(8,128)S(1)}, u32[]{:S(2)}, u32[]{:S(2)}) collective-permute-start(f32[8,128]{1,0:T(8,128)S(1)} %add.70), channel_id=1, source_target_pairs={{0,192},{16,208},{32,224},{48,240},{64,128},{80,144},{96,160},{112... | collective-permute-start | bytes 12296 | tf_op jit(solution)/shard_map/ppermute | solution.py:34
  64.3 1.5 %collective-permute-done.17 = f32[8,128]{1,0:T(8,128)S(1)} collective-permute-done((f32[8,128]{1,0:T(8,128)S(1)}, f32[8,128]{1,0:T(8,128)S(1)}, u32[]{:S(2)}, u32[]{:S(2)}) %collective-permute-start.17) | collective-permute-done | bytes 4128 | tf_op jit(solution)/shard_map/ppermute | solution.py:34
  65.8 1.2 %collective-permute-done.13 = bf16[256,512]{1,0:T(8,128)(2,1)S(1)} collective-permute-done((bf16[256,512]{1,0:T(8,128)(2,1)S(1)}, bf16[256,512]{1,0:T(8,128)(2,1)S(1)}, u32[]{:S(2)}, u32[]{:S(2)}) %collective-permute-start.13) | collective-permute-done | bytes 262176 | tf_op jit(solution)/shard_map/ppermute | solution.py:28
  67.0 1.1 %collective-permute-done.14 = bf16[256,512]{1,0:T(8,128)(2,1)S(1)} collective-permute-done((bf16[256,512]{1,0:T(8,128)(2,1)S(1)}, bf16[256,512]{1,0:T(8,128)(2,1)S(1)}, u32[]{:S(2)}, u32[]{:S(2)}) %collective-permute-start.14) | collective-permute-done | bytes 262176 | tf_op jit(solution)/shard_map/ppermute | solution.py:28
  68.1 0.0 collective-permute-done.15
  68.1 0.0 collective-permute-done.16.refs_1_
  68.1 0.1 add_convert_fusion
  68.2 1.4 %collective-permute-start.19 = (bf16[256,512]{1,0:T(8,128)(2,1)S(1)}, bf16[256,512]{1,0:T(8,128)(2,1)S(1)}, u32[]{:S(2)}, u32[]{:S(2)}) collective-permute-start(bf16[256,512]{1,0:T(8,128)(2,1)S(1)} %add_convert_fusion), channel_id=1, source_target_pairs={{0,2},{2,0},{1,3},{3,1},{4,6},{6,4},{5,7},{7,5},{8,10},{10,8},{9,1... | collective-permute-start | bytes 786440 | tf_op jit(solution)/shard_map/ppermute | solution.py:28
  69.6 0.1 add_convert_fusion.1
  69.7 1.3 %collective-permute-start.18 = (bf16[256,512]{1,0:T(8,128)(2,1)S(1)}, bf16[256,512]{1,0:T(8,128)(2,1)S(1)}, u32[]{:S(2)}, u32[]{:S(2)}) collective-permute-start(bf16[256,512]{1,0:T(8,128)(2,1)S(1)} %add_convert_fusion.1), channel_id=1, source_target_pairs={{0,8},{4,12},{8,0},{12,4},{1,9},{5,13},{9,1},{13,5},{2,10},{6,14},... | collective-permute-start | bytes 786440 | tf_op jit(solution)/shard_map/ppermute | solution.py:28
  70.9 1.7 %collective-permute-start.20 = (bf16[256,512]{1,0:T(8,128)(2,1)S(1)}, bf16[256,512]{1,0:T(8,128)(2,1)S(1)}, u32[]{:S(2)}, u32[]{:S(2)}) collective-permute-start(bf16[256,512]{1,0:T(8,128)(2,1)S(1)} %get-tuple-element.84), channel_id=1, source_target_pairs={{0,4},{4,8},{8,12},{12,0},{1,5},{5,9},{9,13},{13,1},{2,6},{6,10},{... | collective-permute-start | bytes 786440 | tf_op jit(solution)/shard_map/ppermute | solution.py:28
  72.7 0.9 %collective-permute-start.21 = (bf16[256,512]{1,0:T(8,128)(2,1)S(1)}, bf16[256,512]{1,0:T(8,128)(2,1)S(1)}, u32[]{:S(2)}, u32[]{:S(2)}) collective-permute-start(bf16[256,512]{1,0:T(8,128)(2,1)S(1)} %get-tuple-element.85), channel_id=1, source_target_pairs={{0,12},{4,0},{8,4},{12,8},{1,13},{5,1},{9,5},{13,9},{2,14},{6,2},{... | collective-permute-start | bytes 786440 | tf_op jit(solution)/shard_map/ppermute | solution.py:28
  73.6 4.5 %collective-permute-start.22 = (f32[8,128]{1,0:T(8,128)S(1)}, f32[8,128]{1,0:T(8,128)S(1)}, u32[]{:S(2)}, u32[]{:S(2)}) collective-permute-start(f32[8,128]{1,0:T(8,128)S(1)} %add.71), channel_id=1, source_target_pairs={{0,48},{16,32},{32,16},{48,0},{64,112},{80,96},{96,80},{112,64},{1... | collective-permute-start | bytes 12296 | tf_op jit(solution)/shard_map/ppermute | solution.py:34
  78.2 1.8 %place.1 = bf16[1,1,128,4096]{3,2,1,0:T(8,128)(2,1)} custom-call(s32[1]{0:T(128)} %get-tuple-element.56.side_ref, bf16[128,2048]{1,0:T(8,128)(2,1)S(1)} %get-tuple-element.86.refs_0_, bf16[128,5120]{1,0:T(8,128)(2,1)S(1)} %collective-permute-done.16.refs_1_), custom_call_target="tpu_custom_call" | custom-call | bytes 2000000 | tf_op jit(solution)/shard_map/place/pallas_call | solution.py:330
  80.0 0.0 collective-permute-done.22
  80.0 0.0 collective-permute-done.19
  80.1 0.0 collective-permute-done.18
  80.1 5.0 %collective-permute-done.20 = bf16[256,512]{1,0:T(8,128)(2,1)S(1)} collective-permute-done((bf16[256,512]{1,0:T(8,128)(2,1)S(1)}, bf16[256,512]{1,0:T(8,128)(2,1)S(1)}, u32[]{:S(2)}, u32[]{:S(2)}) %collective-permute-start.20) | collective-permute-done | bytes 262176 | tf_op jit(solution)/shard_map/ppermute | solution.py:28
  85.1 0.0 collective-permute-done.21
  85.1 0.2 fusion.8
  85.3 0.6 collective-permute-start.23
  85.9 1.0 %collective-permute-done.23.refs_3_ = bf16[128,512]{1,0:T(8,128)(2,1)S(1)} collective-permute-done((bf16[128,512]{1,0:T(8,128)(2,1)S(1)}, bf16[128,512]{1,0:T(8,128)(2,1)S(1)}, u32[]{:S(2)}, u32[]{:S(2)}) %collective-permute-start.23) | collective-permute-done | bytes 131104 | tf_op jit(solution)/shard_map/ppermute | solution.py:28
  86.9 2.6 %finish.1 = (bf16[1,1,128,4096]{3,2,1,0:T(8,128)(2,1)}, bf16[1,1,128,1024]{3,2,1,0:T(8,128)(2,1)}, bf16[1,1,128,1024]{3,2,1,0:T(8,128)(2,1)}, bf16[1,64,1024]{2,1,0:T(8,128)(2,1)}, bf16[1,64,1024]{2,1,0:T(8,128)(2,1)}) custom-call(s32[1]{0:T(128)} %get-tuple-element.56.side_ref, bf16[128,3072]{1,0:T(8,128)(2,1)S(1)} %get-tuple-element.90.refs_0_, ...), custom_call_target="tpu_custom_call" | custom-call | bytes 2000000 | tf_op jit(solution)/shard_map/finish/pallas_call | solution.py:330
  (16 shorter events, 0.1 us)
Async XLA Ops:
  3.7 6.7 %collective-permute-start = (bf16[144,512]{1,0:T(8,128)(2,1)}, bf16[144,512]{1,0:T(8,128)(2,1)S(1)}, u32[]{:S(2)}, u32[]{:S(2)}) collective-permute-start(bf16[144,512]{1,0:T(8,128)(2,1)} %get-tuple-element.55), channel_id=1, source_target_pairs={{0,1},{1,0},{2,3},{3,2},{4,5},{5,4},{6,7},{7,6},{8,9},{9,8},{10,11... | collective-permute-start | bytes 442376 | tf_op jit(solution)/shard_map/ppermute | solution.py:28
  7.0 3.4 %copy-start.4 = (bf16[144,512]{1,0:T(8,128)(2,1)S(1)}, bf16[144,512]{1,0:T(8,128)(2,1)}, u32[]{:S(2)}) copy-start(bf16[144,512]{1,0:T(8,128)(2,1)} %get-tuple-element.54) | copy-start | bytes 442372
  7.0 27.2 %copy-start = (bf16[1,1,128,4096]{3,2,1,0:T(8,128)(2,1)S(1)}, bf16[1,1,128,4096]{3,2,1,0:T(8,128)(2,1)}, u32[]{:S(2)}) copy-start(bf16[1,1,128,4096]{3,2,1,0:T(8,128)(2,1)} %refs_8_.1) | copy-start | bytes 3145732
  7.0 27.2 %copy-start.1 = (bf16[1,1,128,4096]{3,2,1,0:T(8,128)(2,1)S(1)}, bf16[1,1,128,4096]{3,2,1,0:T(8,128)(2,1)}, u32[]{:S(2)}) copy-start(bf16[1,1,128,4096]{3,2,1,0:T(8,128)(2,1)} %refs_9_.1) | copy-start | bytes 3145732
  7.0 27.2 %copy-start.2 = (bf16[1,1,128,1024]{3,2,1,0:T(8,128)(2,1)S(1)}, bf16[1,1,128,1024]{3,2,1,0:T(8,128)(2,1)}, u32[]{:S(2)}) copy-start(bf16[1,1,128,1024]{3,2,1,0:T(8,128)(2,1)} %refs_10_.1) | copy-start | bytes 786436
  7.0 27.2 %copy-start.3 = (bf16[1,1,128,1024]{3,2,1,0:T(8,128)(2,1)S(1)}, bf16[1,1,128,1024]{3,2,1,0:T(8,128)(2,1)}, u32[]{:S(2)}) copy-start(bf16[1,1,128,1024]{3,2,1,0:T(8,128)(2,1)} %refs_11_.1) | copy-start | bytes 786436
  10.3 9.6 %collective-permute-start.2 = (bf16[128,5120]{1,0:T(8,128)(2,1)}, bf16[128,5120]{1,0:T(8,128)(2,1)S(1)}, u32[]{:S(2)}, u32[]{:S(2)}) collective-permute-start(bf16[128,5120]{1,0:T(8,128)(2,1)} %pack.1), channel_id=1, source_target_pairs={{0,1},{1,0},{2,3},{3,2},{4,5},{5,4},{6,7},{7,6},{8,9},{9,8},{10,11... | collective-permute-start | bytes 3932168 | tf_op jit(solution)/shard_map/ppermute | solution.py:28
  10.5 9.4 %collective-permute-start.5 = (bf16[272,512]{1,0:T(8,128)(2,1)S(1)}, bf16[272,512]{1,0:T(8,128)(2,1)S(1)}, u32[]{:S(2)}, u32[]{:S(2)}) collective-permute-start(bf16[272,512]{1,0:T(8,128)(2,1)S(1)} %constant_dynamic-update-slice_fusion.refs_0_), channel_id=1, source_target_pairs={{0,8},{4,12},{8,0},{12,4},{1,9},{5,13},{9,1},{13,5},{2,10},{6,14},... | collective-permute-start | bytes 835592 | tf_op jit(solution)/shard_map/ppermute | solution.py:28
  11.8 8.1 %collective-permute-start.1 = (bf16[272,512]{1,0:T(8,128)(2,1)S(1)}, bf16[272,512]{1,0:T(8,128)(2,1)S(1)}, u32[]{:S(2)}, u32[]{:S(2)}) collective-permute-start(bf16[272,512]{1,0:T(8,128)(2,1)S(1)} %constant_dynamic-update-slice_fusion.refs_0_), channel_id=1, source_target_pairs={{0,2},{2,0},{1,3},{3,1},{4,6},{6,4},{5,7},{7,5},{8,10},{10,8},{9,1... | collective-permute-start | bytes 835592 | tf_op jit(solution)/shard_map/ppermute | solution.py:28
  13.4 13.2 %collective-permute-start.8 = (bf16[272,512]{1,0:T(8,128)(2,1)S(1)}, bf16[272,512]{1,0:T(8,128)(2,1)S(1)}, u32[]{:S(2)}, u32[]{:S(2)}) collective-permute-start(bf16[272,512]{1,0:T(8,128)(2,1)S(1)} %constant_dynamic-update-slice_fusion.refs_0_), channel_id=1, source_target_pairs={{0,4},{4,8},{8,12},{12,0},{1,5},{5,9},{9,13},{13,1},{2,6},{6,10},{... | collective-permute-start | bytes 835592 | tf_op jit(solution)/shard_map/ppermute | solution.py:28
  13.8 12.8 %collective-permute-start.7 = (bf16[272,512]{1,0:T(8,128)(2,1)S(1)}, bf16[272,512]{1,0:T(8,128)(2,1)S(1)}, u32[]{:S(2)}, u32[]{:S(2)}) collective-permute-start(bf16[272,512]{1,0:T(8,128)(2,1)S(1)} %constant_dynamic-update-slice_fusion.refs_0_), channel_id=1, source_target_pairs={{0,12},{4,0},{8,4},{12,8},{1,13},{5,1},{9,5},{13,9},{2,14},{6,2},{... | collective-permute-start | bytes 835592 | tf_op jit(solution)/shard_map/ppermute | solution.py:28
  19.9 13.0 %collective-permute-start.6 = (bf16[272,512]{1,0:T(8,128)(2,1)S(1)}, bf16[272,512]{1,0:T(8,128)(2,1)S(1)}, u32[]{:S(2)}, u32[]{:S(2)}) collective-permute-start(bf16[272,512]{1,0:T(8,128)(2,1)S(1)} %collective-permute-done.5.refs_6_), channel_id=1, source_target_pairs={{0,2},{2,0},{1,3},{3,1},{4,6},{6,4},{5,7},{7,5},{8,10},{10,8},{9,1... | collective-permute-start | bytes 835592 | tf_op jit(solution)/shard_map/ppermute | solution.py:28
  19.9 13.0 %collective-permute-start.4 = (bf16[272,512]{1,0:T(8,128)(2,1)S(1)}, bf16[272,512]{1,0:T(8,128)(2,1)S(1)}, u32[]{:S(2)}, u32[]{:S(2)}) collective-permute-start(bf16[272,512]{1,0:T(8,128)(2,1)S(1)} %collective-permute-done.1.refs_1_), channel_id=1, source_target_pairs={{0,12},{4,0},{8,4},{12,8},{1,13},{5,1},{9,5},{13,9},{2,14},{6,2},{... | collective-permute-start | bytes 835592 | tf_op jit(solution)/shard_map/ppermute | solution.py:28
  22.5 10.3 %collective-permute-start.3 = (bf16[272,512]{1,0:T(8,128)(2,1)S(1)}, bf16[272,512]{1,0:T(8,128)(2,1)S(1)}, u32[]{:S(2)}, u32[]{:S(2)}) collective-permute-start(bf16[272,512]{1,0:T(8,128)(2,1)S(1)} %collective-permute-done.1.refs_1_), channel_id=1, source_target_pairs={{0,4},{4,8},{8,12},{12,0},{1,5},{5,9},{9,13},{13,1},{2,6},{6,10},{... | collective-permute-start | bytes 835592 | tf_op jit(solution)/shard_map/ppermute | solution.py:28
  26.7 3.7 %collective-permute-start.10 = (f32[8,128]{1,0:T(8,128)S(1)}, f32[8,128]{1,0:T(8,128)S(1)}, u32[]{:S(2)}, u32[]{:S(2)}) collective-permute-start(f32[8,128]{1,0:T(8,128)S(1)} %broadcast_in_dim.8), channel_id=1, source_target_pairs={{0,16},{16,0},{32,48},{48,32},{64,80},{80,64},{96,112},{112,96},{1... | collective-permute-start | bytes 12296 | tf_op jit(solution)/shard_map/ppermute | solution.py:34
  27.8 4.3 %collective-permute-start.11 = (f32[8,128]{1,0:T(8,128)S(1)}, f32[8,128]{1,0:T(8,128)S(1)}, u32[]{:S(2)}, u32[]{:S(2)}) collective-permute-start(f32[8,128]{1,0:T(8,128)S(1)} %broadcast_in_dim.8), channel_id=1, source_target_pairs={{0,80},{16,64},{32,112},{48,96},{64,16},{80,0},{96,48},{112,32},{1... | collective-permute-start | bytes 12296 | tf_op jit(solution)/shard_map/ppermute | solution.py:34
  30.4 2.5 %collective-permute-start.9 = (f32[8,128]{1,0:T(8,128)S(1)}, f32[8,128]{1,0:T(8,128)S(1)}, u32[]{:S(2)}, u32[]{:S(2)}) collective-permute-start(f32[8,128]{1,0:T(8,128)S(1)} %broadcast_in_dim.8), channel_id=1, source_target_pairs={{0,64},{16,80},{32,96},{48,112},{64,0},{80,16},{96,32},{112,48},{1... | collective-permute-start | bytes 12296 | tf_op jit(solution)/shard_map/ppermute | solution.py:34
  32.9 22.7 %collective-permute-start.12 = (f32[8,128]{1,0:T(8,128)S(1)}, f32[8,128]{1,0:T(8,128)S(1)}, u32[]{:S(2)}, u32[]{:S(2)}) collective-permute-start(f32[8,128]{1,0:T(8,128)S(1)} %add_add_fusion), channel_id=1, source_target_pairs={{0,2},{2,0},{1,3},{3,1},{4,6},{6,4},{5,7},{7,5},{8,10},{10,8},{9,1... | collective-permute-start | bytes 12296 | tf_op jit(solution)/shard_map/ppermute | solution.py:28
  55.6 12.5 %collective-permute-start.16 = (bf16[128,5120]{1,0:T(8,128)(2,1)S(1)}, bf16[128,5120]{1,0:T(8,128)(2,1)S(1)}, u32[]{:S(2)}, u32[]{:S(2)}) collective-permute-start(bf16[128,5120]{1,0:T(8,128)(2,1)S(1)} %get-tuple-element.76), channel_id=1, source_target_pairs={{0,1},{1,0},{2,3},{3,2},{4,5},{5,4},{6,7},{7,6},{8,9},{9,8},{10,11... | collective-permute-start | bytes 3932168 | tf_op jit(solution)/shard_map/ppermute | solution.py:28
  59.2 7.9 %collective-permute-start.13 = (bf16[256,512]{1,0:T(8,128)(2,1)S(1)}, bf16[256,512]{1,0:T(8,128)(2,1)S(1)}, u32[]{:S(2)}, u32[]{:S(2)}) collective-permute-start(bf16[256,512]{1,0:T(8,128)(2,1)S(1)} %get-tuple-element.73), channel_id=1, source_target_pairs={{0,2},{2,0},{1,3},{3,1},{4,6},{6,4},{5,7},{7,5},{8,10},{10,8},{9,1... | collective-permute-start | bytes 786440 | tf_op jit(solution)/shard_map/ppermute | solution.py:28
  59.2 8.9 %collective-permute-start.14 = (bf16[256,512]{1,0:T(8,128)(2,1)S(1)}, bf16[256,512]{1,0:T(8,128)(2,1)S(1)}, u32[]{:S(2)}, u32[]{:S(2)}) collective-permute-start(bf16[256,512]{1,0:T(8,128)(2,1)S(1)} %get-tuple-element.74), channel_id=1, source_target_pairs={{0,4},{4,8},{8,12},{12,0},{1,5},{5,9},{9,13},{13,1},{2,6},{6,10},{... | collective-permute-start | bytes 786440 | tf_op jit(solution)/shard_map/ppermute | solution.py:28
  60.2 7.9 %collective-permute-start.15 = (bf16[256,512]{1,0:T(8,128)(2,1)S(1)}, bf16[256,512]{1,0:T(8,128)(2,1)S(1)}, u32[]{:S(2)}, u32[]{:S(2)}) collective-permute-start(bf16[256,512]{1,0:T(8,128)(2,1)S(1)} %get-tuple-element.75), channel_id=1, source_target_pairs={{0,12},{4,0},{8,4},{12,8},{1,13},{5,1},{9,5},{13,9},{2,14},{6,2},{... | collective-permute-start | bytes 786440 | tf_op jit(solution)/shard_map/ppermute | solution.py:28
  61.8 4.0 %collective-permute-start.17 = (f32[8,128]{1,0:T(8,128)S(1)}, f32[8,128]{1,0:T(8,128)S(1)}, u32[]{:S(2)}, u32[]{:S(2)}) collective-permute-start(f32[8,128]{1,0:T(8,128)S(1)} %add.70), channel_id=1, source_target_pairs={{0,192},{16,208},{32,224},{48,240},{64,128},{80,144},{96,160},{112... | collective-permute-start | bytes 12296 | tf_op jit(solution)/shard_map/ppermute | solution.py:34
  68.2 11.8 %collective-permute-start.19 = (bf16[256,512]{1,0:T(8,128)(2,1)S(1)}, bf16[256,512]{1,0:T(8,128)(2,1)S(1)}, u32[]{:S(2)}, u32[]{:S(2)}) collective-permute-start(bf16[256,512]{1,0:T(8,128)(2,1)S(1)} %add_convert_fusion), channel_id=1, source_target_pairs={{0,2},{2,0},{1,3},{3,1},{4,6},{6,4},{5,7},{7,5},{8,10},{10,8},{9,1... | collective-permute-start | bytes 786440 | tf_op jit(solution)/shard_map/ppermute | solution.py:28
  69.7 10.4 %collective-permute-start.18 = (bf16[256,512]{1,0:T(8,128)(2,1)S(1)}, bf16[256,512]{1,0:T(8,128)(2,1)S(1)}, u32[]{:S(2)}, u32[]{:S(2)}) collective-permute-start(bf16[256,512]{1,0:T(8,128)(2,1)S(1)} %add_convert_fusion.1), channel_id=1, source_target_pairs={{0,8},{4,12},{8,0},{12,4},{1,9},{5,13},{9,1},{13,5},{2,10},{6,14},... | collective-permute-start | bytes 786440 | tf_op jit(solution)/shard_map/ppermute | solution.py:28
  70.9 14.2 %collective-permute-start.20 = (bf16[256,512]{1,0:T(8,128)(2,1)S(1)}, bf16[256,512]{1,0:T(8,128)(2,1)S(1)}, u32[]{:S(2)}, u32[]{:S(2)}) collective-permute-start(bf16[256,512]{1,0:T(8,128)(2,1)S(1)} %get-tuple-element.84), channel_id=1, source_target_pairs={{0,4},{4,8},{8,12},{12,0},{1,5},{5,9},{9,13},{13,1},{2,6},{6,10},{... | collective-permute-start | bytes 786440 | tf_op jit(solution)/shard_map/ppermute | solution.py:28
  72.7 12.4 %collective-permute-start.21 = (bf16[256,512]{1,0:T(8,128)(2,1)S(1)}, bf16[256,512]{1,0:T(8,128)(2,1)S(1)}, u32[]{:S(2)}, u32[]{:S(2)}) collective-permute-start(bf16[256,512]{1,0:T(8,128)(2,1)S(1)} %get-tuple-element.85), channel_id=1, source_target_pairs={{0,12},{4,0},{8,4},{12,8},{1,13},{5,1},{9,5},{13,9},{2,14},{6,2},{... | collective-permute-start | bytes 786440 | tf_op jit(solution)/shard_map/ppermute | solution.py:28
  73.6 6.4 %collective-permute-start.22 = (f32[8,128]{1,0:T(8,128)S(1)}, f32[8,128]{1,0:T(8,128)S(1)}, u32[]{:S(2)}, u32[]{:S(2)}) collective-permute-start(f32[8,128]{1,0:T(8,128)S(1)} %add.71), channel_id=1, source_target_pairs={{0,48},{16,32},{32,16},{48,0},{64,112},{80,96},{96,80},{112,64},{1... | collective-permute-start | bytes 12296 | tf_op jit(solution)/shard_map/ppermute | solution.py:34
  85.3 1.6 %collective-permute-start.23 = (bf16[128,512]{1,0:T(8,128)(2,1)S(1)}, bf16[128,512]{1,0:T(8,128)(2,1)S(1)}, u32[]{:S(2)}, u32[]{:S(2)}) collective-permute-start(bf16[128,512]{1,0:T(8,128)(2,1)S(1)} %pad_maximum_fusion), channel_id=1, source_target_pairs={{0,1},{1,0},{2,3},{3,2},{4,5},{5,4},{6,7},{7,6},{8,9},{9,8},{10,11... | collective-permute-start | bytes 393224 | tf_op jit(solution)/shard_map/ppermute | solution.py:28
